TPU v7x, 512 devices: a whole 4x8x8 slice. The times are simulated.
512 devices in a mesh: leaf: 128 (over z, y, core), rhs: 4 (over x).
Axes of the slice: x: 4, y: 8, z: 8, core: 2. Of those that a mesh axis runs over, the one named last changes fastest.
Arguments:
- leaf_shift: float32 [256, 262144], P('rhs', 'leaf'), may hold values from -6 to 6
- sep_shift: float32 [256, 4096], P('rhs', 'leaf'), may hold values from -6 to 6
- leaf_noise: float32 [256, 262144], P('rhs', 'leaf'), may hold values from -6 to 6
- sep_noise: float32 [256, 4096], P('rhs', 'leaf'), may hold values from -6 to 6
- leaf_inverse: float32 [2048, 128, 128], P('leaf'), may hold values from -1 to 2, as said below
- leaf_panel: float32 [2048, 64, 128], P('leaf'), may hold values from -0.0625 to 0.0625
- panel_blocks: int32 [2048, 8], P('leaf'), may hold values from 0 to 239, as said below
- sep_inverse: float32 [1024, 1920], P('leaf', 'rhs'), may hold values from -1 to 2, as said below
- sep_coupling: float32 [1024, 4352], P('leaf', 'rhs'), may hold values from -0.125 to 0.125
Outputs:
- leaf_sample: float32 [256, 262144], P('rhs', 'leaf')
- sep_sample: float32 [256, 4096], P('rhs', 'leaf')
Inputs may be any that keep to these rules, and one draw needn't show every extreme that they name: `leaf_inverse`: each [128, 128] block is lower triangular with a positive diagonal. `sep_inverse`: in the column block of depth k (columns O_k to O_k + S_k - 1), row p has zeros beyond column O_k + (p mod S_k) and a positive entry there: each separator's inverse is lower triangular. `panel_blocks`: the 8 numbers of a row are different.
All inputs are finite; a program needn't handle non-finite values.
Results may differ from a plain program's by a relative error of at most 0.00015.
Values sent between devices are 32-bit elements; how exact they have to be, the bound alone decides.
No kernel may reach another device: no remote copies, remote signals or barrier semaphores. Data moves between devices by JAX's collectives and lax.ppermute only.
A program may use at most 64 MiB of HBM per device.

v0:
```python
import jax
import jax.numpy as jnp
from jax import lax
from jax.sharding import PartitionSpec as P

SEP_DEV = 8
LEVELS = 4
NB = 8


exact_mode = lax.Precision.HIGHEST


def level_offsets(root_size):
    starts = [0]
    for height in range(LEVELS):
        starts.append(starts[-1] + (root_size >> height))
    return starts


def subcube_total(partial_value, height):
    leaf_count = lax.axis_size("leaf")
    dev_index = lax.axis_index("leaf")
    cube_size = leaf_count >> height
    sep_size = partial_value.shape[1]
    sep_start = dev_index // cube_size * sep_size
    buffer = jnp.zeros((partial_value.shape[0], SEP_DEV * leaf_count), jnp.float32)
    buffer = lax.dynamic_update_slice_in_dim(buffer, partial_value, sep_start, 1)
    summed = lax.psum(buffer, "leaf")
    full_sum = lax.dynamic_slice_in_dim(summed, sep_start, sep_size, 1)
    own_rows = lax.dynamic_slice_in_dim(full_sum, dev_index % cube_size * SEP_DEV, SEP_DEV, 1)
    return (own_rows, full_sum)


def body(
    leaf_shift,
    sep_shift,
    leaf_noise,
    sep_noise,
    leaf_inverse,
    leaf_panel,
    panel_blocks,
    sep_inverse,
    sep_coupling,
):
    inverse_rows, coupling_rows = (
        lax.all_gather(sep_inverse, "rhs", axis=1, tiled=True),
        lax.all_gather(sep_coupling, "rhs", axis=1, tiled=True),
    )
    leaf_count = lax.axis_size("leaf")
    dev_index = lax.axis_index("leaf")
    root_size = SEP_DEV * leaf_count
    starts = level_offsets(root_size)
    ancestry = starts[LEVELS]
    segment_at = [0]
    for height in range(1, LEVELS):
        segment_at.append(segment_at[-1] + starts[height])
    samples = leaf_shift.shape[0]
    node_count = leaf_inverse.shape[0]
    tile_size = leaf_inverse.shape[1]
    block_count = ancestry // SEP_DEV
    selector = (
        panel_blocks[:, :, None] == jnp.arange(block_count, dtype=jnp.int32)[None, None, :]
    ).astype(jnp.float32)
    shifted = leaf_shift.reshape(samples, node_count, tile_size)
    leaf_forward = jnp.einsum("rnt,nct->rnc", shifted, leaf_inverse, precision=exact_mode)
    pieces = jnp.einsum("rnc,nkc->rnk", leaf_forward, leaf_panel, precision=exact_mode)
    pieces = pieces.reshape(samples, node_count, NB, SEP_DEV)
    update = jnp.einsum("rnbi,nba->rai", pieces, selector, precision=exact_mode).reshape(
        samples, ancestry
    )
    sep_own = sep_shift.reshape(samples, LEVELS, SEP_DEV)
    noise_own = sep_noise.reshape(samples, LEVELS, SEP_DEV)
    forward_sep = [None] * LEVELS
    for height in reversed(range(LEVELS)):
        cube_size = leaf_count >> height
        sep_size = root_size >> height
        local_at = dev_index % cube_size * SEP_DEV
        placed = lax.dynamic_update_slice_in_dim(
            jnp.zeros((samples, sep_size), jnp.float32), sep_own[:, height, :], local_at, 1
        )
        partial_value = placed - update[:, starts[height] : starts[height] + sep_size]
        own_rows, full_rest = subcube_total(partial_value, height)
        inverse_block = inverse_rows[:, starts[height] : starts[height] + sep_size]
        solved = jnp.dot(full_rest, inverse_block.T, precision=exact_mode)
        forward_sep[height] = solved
        if height > 0:
            couple_block = coupling_rows[
                :, segment_at[height - 1] : segment_at[height - 1] + starts[height]
            ]
            update = update.at[:, : starts[height]].add(
                jnp.dot(solved, couple_block, precision=exact_mode)
            )
    gathered = jnp.zeros((samples, ancestry), jnp.float32)
    sep_result = [None] * LEVELS
    for height in range(LEVELS):
        sep_size = root_size >> height
        lifted = forward_sep[height] + noise_own[:, height, :]
        if height > 0:
            couple_block = coupling_rows[
                :, segment_at[height - 1] : segment_at[height - 1] + starts[height]
            ]
            lifted = lifted - jnp.dot(
                gathered[:, : starts[height]], couple_block.T, precision=exact_mode
            )
        inverse_block = inverse_rows[:, starts[height] : starts[height] + sep_size]
        partial_value = jnp.dot(lifted, inverse_block, precision=exact_mode)
        own_rows, full_sum = subcube_total(partial_value, height)
        sep_result[height] = own_rows
        gathered = lax.dynamic_update_slice_in_dim(gathered, full_sum, starts[height], 1)
    blocks_view = gathered.reshape(samples, block_count, SEP_DEV)
    picked = jnp.einsum("rai,nba->rnbi", blocks_view, selector, precision=exact_mode).reshape(
        samples, node_count, NB * SEP_DEV
    )
    leaf_lifted = leaf_forward + leaf_noise.reshape(samples, node_count, tile_size)
    leaf_lifted = leaf_lifted - jnp.einsum("rnk,nkc->rnc", picked, leaf_panel, precision=exact_mode)
    leaf_out = jnp.einsum("rnt,ntc->rnc", leaf_lifted, leaf_inverse, precision=exact_mode).reshape(
        samples, node_count * tile_size
    )
    sep_out = jnp.stack(sep_result, axis=1).reshape(samples, LEVELS * SEP_DEV)
    return (leaf_out, sep_out)


def solution(mesh):
    placed = (
        P("rhs", "leaf"),
        P("rhs", "leaf"),
        P("rhs", "leaf"),
        P("rhs", "leaf"),
        P("leaf", None, None),
        P("leaf", None, None),
        P("leaf", None),
        P("leaf", "rhs"),
        P("leaf", "rhs"),
    )
    return jax.shard_map(
        body,
        mesh=mesh,
        in_specs=placed,
        out_specs=(P("rhs", "leaf"), P("rhs", "leaf")),
        check_vma=False,
    )
```

profile of v0, /device:TPU:1, one launch (start us, length us, event | category | flops | bytes accessed | tf_op | source)
XLA Modules:
  0.0 1559.3 jit_solution(408747007953209379)
XLA Ops:
  7.3 0.8 copy-done.15
  8.4 3.2 convolution_bitcast_fusion.3
  11.6 1.0 convolution_bitcast_fusion.5
  12.6 1.0 copy.43
  13.7 1.6 convolution_bitcast_fusion.2
  16.4 0.7 copy-done.6
  17.2 1.0 slice.157
  18.2 10.3 all-gather
  28.6 9.1 all-gather.1
  38.3 0.6 dynamic_update_slice.47
  38.9 0.6 compare_reduce_fusion
  39.6 171.9 %all-reduce.10.cloned.1.call-done = f32[64,1024]{1,0:T(8,128)} async-done(((f32[64,1024]{1,0:T(8,128)}), f32[64,1024]{1,0:T(8,128)}) %all-reduce.10.cloned.1.call-update) | async-done | bytes 262160 | tf_op jit(solution)/shard_map/psum | solution.py:29
  211.5 0.9 fusion.29
  212.4 1.2 fusion.1
  213.7 0.7 copy-done.7
  214.6 0.6 dynamic_update_slice.49
  215.2 0.6 compare_reduce_fusion.1
  215.8 186.1 %all-reduce.12.cloned.1.call-done = f32[64,1024]{1,0:T(8,128)} async-done(((f32[64,1024]{1,0:T(8,128)}), f32[64,1024]{1,0:T(8,128)}) %all-reduce.12.cloned.1.call-update) | async-done | bytes 262160 | tf_op jit(solution)/shard_map/psum | solution.py:29
  401.9 1.0 fusion.21
  402.9 1.2 fusion
  404.1 0.7 copy-done.8
  405.6 0.6 compare_reduce_fusion.2
  406.3 186.0 %all-reduce.14.cloned.1.call-done = f32[64,1024]{1,0:T(8,128)} async-done(((f32[64,1024]{1,0:T(8,128)}), f32[64,1024]{1,0:T(8,128)}) %all-reduce.14.cloned.1.call-update) | async-done | bytes 262160 | tf_op jit(solution)/shard_map/psum | solution.py:29
  592.3 1.1 fusion.14
  593.4 1.8 fusion.4
  595.3 187.3 %all-reduce.16.cloned.1.call-done = f32[64,1024]{1,0:T(8,128)} async-done(((f32[64,1024]{1,0:T(8,128)}), f32[64,1024]{1,0:T(8,128)}) %all-reduce.16.cloned.1.call-update) | async-done | bytes 262160 | tf_op jit(solution)/shard_map/psum | solution.py:29
  782.5 1.2 convolution_add_fusion.3
  783.8 1.2 fusion.31
  785.0 187.8 %all-reduce.18.cloned.1.call-done = f32[64,1024]{1,0:T(8,128)} async-done(((f32[64,1024]{1,0:T(8,128)}), f32[64,1024]{1,0:T(8,128)}) %all-reduce.18.cloned.1.call-update) | async-done | bytes 262160 | tf_op jit(solution)/shard_map/psum | solution.py:29
  972.8 1.2 convolution_subtract_fusion
  974.4 0.7 copy-done.9
  975.3 187.8 %all-reduce.20.cloned.1.call-done = f32[64,1024]{1,0:T(8,128)} async-done(((f32[64,1024]{1,0:T(8,128)}), f32[64,1024]{1,0:T(8,128)}) %all-reduce.20.cloned.1.call-update) | async-done | bytes 262160 | tf_op jit(solution)/shard_map/psum | solution.py:29
  1163.1 0.9 dynamic-slice_dynamic-update-slice_fusion
  1164.7 0.7 copy-done.10
  1165.9 187.6 %all-reduce.22.cloned.1.call-done = f32[64,1024]{1,0:T(8,128)} async-done(((f32[64,1024]{1,0:T(8,128)}), f32[64,1024]{1,0:T(8,128)}) %all-reduce.22.cloned.1.call-update) | async-done | bytes 262160 | tf_op jit(solution)/shard_map/psum | solution.py:29
  1353.5 0.8 dynamic-slice_dynamic-update-slice_fusion.1
  1355.1 0.7 copy-done.5
  1355.8 0.9 constant_dynamic-slice_fusion.1
  1356.8 0.9 constant_dynamic-slice_fusion
  1357.8 186.1 %all-reduce.24.cloned.1.call-done = f32[64,1024]{1,0:T(8,128)} async-done(((f32[64,1024]{1,0:T(8,128)}), f32[64,1024]{1,0:T(8,128)}) %all-reduce.24.cloned.1.call-update) | async-done | bytes 262160 | tf_op jit(solution)/shard_map/psum | solution.py:29
  1543.9 0.9 constant_dynamic-slice_fusion.3
  1544.9 0.8 dynamic-slice_dynamic-update-slice_fusion.2
  1546.0 1.2 copy.54
  1547.2 1.7 convolution_bitcast_fusion.1
  1548.9 1.0 fusion.2
  1549.9 1.1 convolution_bitcast_fusion
  1551.0 0.8 copy.86
  1551.8 0.6 maximum_bitcast_fusion
  (84 shorter events, 6.2 us)
Async XLA Ops:
  7.2 1.2 copy-start
  7.2 204.3 %all-reduce.10.cloned.1.call-start = ((), (), s32[]{:S(2)}) async-start(), calls=%async_computation | async-start | bytes 524288 | tf_op jit(solution)/shard_map/psum | solution.py:29
  7.2 0.8 copy-start.15
  8.4 3.2 copy-start.2
  12.6 1.0 copy-start.16
  16.4 0.7 copy-start.6
  17.1 384.8 %all-reduce.12.cloned.1.call-start = ((), (), s32[]{:S(2)}) async-start(), calls=%async_computation.1 | async-start | bytes 524288 | tf_op jit(solution)/shard_map/psum | solution.py:29
  17.1 1.0 copy-start.14
  17.1 11.5 copy-start.12
  18.2 19.8 %copy-start.1 = (f32[64,1792]{0,1:T(8,128)S(1)}, f32[64,1792]{0,1:T(8,128)}, u32[]{:S(2)}) copy-start(f32[64,1792]{0,1:T(8,128)} %slice.157) | copy-start | bytes 1376260
  213.7 0.7 copy-start.7
  214.4 377.9 %all-reduce.14.cloned.1.call-start = ((), (), s32[]{:S(2)}) async-start(), calls=%async_computation.2 | async-start | bytes 524288 | tf_op jit(solution)/shard_map/psum | solution.py:29
  404.1 0.7 copy-start.8
  404.8 377.7 %all-reduce.16.cloned.1.call-start = ((), (), s32[]{:S(2)}) async-start(), calls=%async_computation.3 | async-start | bytes 524288 | tf_op jit(solution)/shard_map/psum | solution.py:29
  595.2 187.4 %copy-start.13 = (f32[64,32]{0,1:T(8,128)S(1)}, f32[64,32]{0,1:T(8,128)}, u32[]{:S(2)}) copy-start(f32[64,32]{0,1:T(8,128)} %param.18) | copy-start | bytes 24580
  595.2 377.6 %all-reduce.18.cloned.1.call-start = ((), (), s32[]{:S(2)}) async-start(), calls=%async_computation.4 | async-start | bytes 524288 | tf_op jit(solution)/shard_map/psum | solution.py:29
  785.0 378.1 %all-reduce.20.cloned.1.call-start = ((), (), s32[]{:S(2)}) async-start(), calls=%async_computation.5 | async-start | bytes 524288 | tf_op jit(solution)/shard_map/psum | solution.py:29
  974.1 1.1 copy-start.4
  974.4 0.7 copy-start.9
  975.2 378.3 %all-reduce.22.cloned.1.call-start = ((), (), s32[]{:S(2)}) async-start(), calls=%async_computation.6 | async-start | bytes 524288 | tf_op jit(solution)/shard_map/psum | solution.py:29
  1164.7 0.7 copy-start.10
  1165.4 378.4 %all-reduce.24.cloned.1.call-start = ((), (), s32[]{:S(2)}) async-start(), calls=%async_computation.7 | async-start | bytes 524288 | tf_op jit(solution)/shard_map/psum | solution.py:29
  1355.1 0.7 copy-start.5
  1547.1 1.7 copy-start.3
  1547.1 1.7 copy-start.11
Sparse Core Ops, SparseCore 0:
  17.2 194.2 all-reduce.9
  215.3 186.5 all-reduce.11
  405.7 186.5 all-reduce.13
  595.9 186.5 all-reduce.15
  786.2 186.5 all-reduce.17
  976.5 186.5 all-reduce.19
  1166.9 186.5 all-reduce.21
  1357.3 186.5 all-reduce.23
where the time goes:
time: 1560 us
  waiting for transfers between devices  1480 us (95%)
  matrix products  22.1 us (1%)
  blocking collectives  19.4 us (1%)
  local copies, waits for them, and re-layouts  19.3 us (1%)
    psum x8, waiting for transfers between devices, subcube_total(): summed = lax.psum(buffer, 'leaf')  1480 us
  transfers between devices with their start and end apart: 8, of which 8 were waited for; matrix products, arithmetic and copies ran while one was open for 0% of the time, Pallas kernels for 0%

commit v1 on v0

v1 whole, which is shorter than its diff:
```python
import jax
import jax.numpy as jnp
from jax import lax
from jax.sharding import Mesh, PartitionSpec as P

SEP_DEV = 8
LEVELS = 4
NB = 8
S0 = 1024
ANC = 1920
PLANE = 16
STARTS = (0, 1024, 1536, 1792, 1920)
SEG = (0, 0, 1024, 2560)

exact = lax.Precision.HIGHEST


def ein(spec, a, b):
    return jnp.einsum(spec, a, b, precision=exact)


def body(
    leaf_shift,
    sep_shift,
    leaf_noise,
    sep_noise,
    leaf_inverse,
    leaf_panel,
    panel_blocks,
    sep_inverse,
    sep_coupling,
):
    yc = ("y", "core")
    zz = ("zh", "zq")
    samples = leaf_shift.shape[0]
    nodes, tile = leaf_inverse.shape[0], leaf_inverse.shape[1]
    group = samples // PLANE
    zq = lax.axis_index("zq")
    zh = lax.axis_index("zh")
    z = zh * 4 + zq
    dev = z * PLANE + lax.axis_index("y") * 2 + lax.axis_index("core")

    own = jnp.concatenate([sep_inverse, sep_coupling], axis=1)
    quad = lax.all_gather(own, ("zq", "rhs"), axis=0, tiled=False).reshape(4, 4, 8, 1568)
    quad = jnp.transpose(quad, (0, 2, 1, 3))
    inv = quad[..., :480].reshape(4, 8, 1920)
    cou = quad[..., 480:].reshape(4, 8, 4352)
    l1 = jnp.concatenate([inv[..., 1024:1536], cou[..., :1024]], axis=2)
    l2 = jnp.concatenate([inv[..., 1536:1792], cou[..., 1024:2560]], axis=2)
    l2 = lax.dynamic_slice_in_dim(l2, zq // 2 * 2, 2, 0)
    l3 = jnp.concatenate([inv[..., 1792:], cou[..., 2560:]], axis=2)
    l3 = lax.dynamic_slice_in_dim(l3, zq, 1, 0)
    l0 = lax.dynamic_slice_in_dim(inv[..., :1024], zq, 1, 0)
    flat = lambda m: jnp.transpose(m, (1, 0, 2)).reshape(8, -1)
    packed = jnp.concatenate([flat(l1), flat(l2), flat(l3), flat(l0)], axis=1)
    path = lax.all_gather(packed, yc, axis=0, tiled=True)
    f1 = path[:, :6144].reshape(512, 1536)
    f2 = path[:, 6144:9728].reshape(256, 1792)
    f3 = path[:, 9728:11648]
    f0 = path[:, 11648:]

    selector = (
        panel_blocks[:, :, None] == jnp.arange(ANC // 8, dtype=jnp.int32)[None, None, :]
    ).astype(jnp.float32)
    shifted = leaf_shift.reshape(samples, nodes, tile)
    leaf_forward = ein("rnt,nct->rnc", shifted, leaf_inverse)
    pieces = ein("rnc,nkc->rnk", leaf_forward, leaf_panel).reshape(samples, nodes, NB, SEP_DEV)
    update = ein("rnbi,nba->rai", pieces, selector).reshape(samples, ANC)
    part = -update
    sep_own = sep_shift.reshape(samples, LEVELS, SEP_DEV)
    for k in range(LEVELS):
        at = STARTS[k] + dev % (128 >> k) * SEP_DEV
        cur = lax.dynamic_slice_in_dim(part, at, SEP_DEV, 1)
        part = lax.dynamic_update_slice_in_dim(part, cur + sep_own[:, k, :], at, 1)
    pay = jnp.concatenate([part, sep_noise, jnp.zeros((samples, 96), jnp.float32)], axis=1)
    pay = lax.all_to_all(pay.reshape(PLANE, group, 2048), yc, 0, 0)
    v = jnp.sum(pay[..., :ANC], axis=0)
    noise = pay[..., ANC : ANC + 32].reshape(PLANE, group, LEVELS, SEP_DEV)
    noise = jnp.transpose(noise, (2, 1, 0, 3)).reshape(LEVELS, group, 128)

    g3 = ein("rc,gc->rg", v[:, 1792:], f3[:, :128])
    w = v[:, :1792] - ein("rg,gc->rc", g3, f3[:, 128:])
    g2 = ein("rc,gc->rg", w[:, 1536:], f2[:, :256])
    w = w[:, :1536] - ein("rg,gc->rc", g2, f2[:, 256:])
    g1 = ein("rc,gc->rg", w[:, 1024:], f1[:, :512])
    w = w[:, :1024] - ein("rg,gc->rc", g1, f1[:, 512:])
    mask1 = (jnp.arange(4) == zq).astype(jnp.float32)
    mask2 = (jnp.arange(2) == zq % 2).astype(jnp.float32)
    g1 = g1 + (noise[1][:, :, None] * mask1).reshape(group, 512)
    g2 = g2 + (noise[2][:, :, None] * mask2).reshape(group, 256)
    send = jnp.concatenate([w, g1, g2], axis=1)
    got = lax.all_to_all(jnp.broadcast_to(send, (8,) + send.shape), zz, 0, 0)
    r0 = jnp.sum(got[..., :1024], axis=0)
    in_quad = (jnp.arange(8) // 4 == zh).astype(jnp.float32)[:, None, None]
    in_pair = (jnp.arange(8) // 2 == z // 2).astype(jnp.float32)[:, None, None]
    g1 = jnp.sum(got[..., 1024:1536] * in_quad, axis=0)
    g2 = jnp.sum(got[..., 1536:] * in_pair, axis=0)

    y0 = ein("rc,gc->rg", r0, f0) + noise[0]
    x0p = ein("rg,gc->rc", y0, f0)
    x0 = jnp.sum(lax.all_to_all(jnp.broadcast_to(x0p, (8,) + x0p.shape), zz, 0, 0), axis=0)
    y1 = g1 - ein("rc,gc->rg", x0, f1[:, 512:])
    x1 = ein("rg,gc->rc", y1, f1[:, :512])
    x = jnp.concatenate([x0, x1], axis=1)
    y2 = g2 - ein("rc,gc->rg", x, f2[:, 256:])
    x2 = ein("rg,gc->rc", y2, f2[:, :256])
    x = jnp.concatenate([x, x2], axis=1)
    y3 = g3 + noise[3] - ein("rc,gc->rg", x, f3[:, 128:])
    x3 = ein("rg,gc->rc", y3, f3[:, :128])
    x = jnp.concatenate([x, x3], axis=1)
    gathered = lax.all_gather(x, yc, axis=0, tiled=True)

    sep_out = jnp.concatenate(
        [
            lax.dynamic_slice_in_dim(gathered, STARTS[k] + dev % (128 >> k) * SEP_DEV, SEP_DEV, 1)
            for k in range(LEVELS)
        ],
        axis=1,
    )
    blocks_view = gathered.reshape(samples, ANC // 8, SEP_DEV)
    picked = ein("rai,nba->rnbi", blocks_view, selector).reshape(samples, nodes, NB * SEP_DEV)
    lifted = leaf_forward + leaf_noise.reshape(samples, nodes, tile)
    lifted = lifted - ein("rnk,nkc->rnc", picked, leaf_panel)
    leaf_out = ein("rnt,ntc->rnc", lifted, leaf_inverse).reshape(samples, nodes * tile)
    return leaf_out, sep_out


def solution(mesh):
    inner = Mesh(mesh.devices.reshape(2, 4, 8, 2, 4), ("zh", "zq", "y", "core", "rhs"))
    leaf = ("zh", "zq", "y", "core")
    data = P("rhs", leaf)
    rows = P(leaf, "rhs")
    return jax.shard_map(
        body,
        mesh=inner,
        in_specs=(data, data, data, data, P(leaf), P(leaf), P(leaf), rows, rows),
        out_specs=(data, data),
        check_vma=False,
    )
```

time: 1560 us -> 233 us (0.15)
  waiting for transfers between devices: 1480 us -> 51.8 us
  blocking collectives: 19.4 us -> 63.4 us
  starting transfers between devices: 0.51 us -> 25.4 us
  local copies, waits for them, and re-layouts: 19.3 us -> 35.4 us
    psum x8 -> x0, waiting for transfers between devices: 1480 us -> none  [subcube_total(): summed = lax.psum(buffer, 'leaf')]
    all_gather x2, blocking collectives: 19.4 us -> 63.4 us  [the longest x1 43.6 us: body(): lax.all_gather(own, ('zq', 'rhs'), axis=0, tiled=False)]
    all_to_all x0 -> x3, waiting for transfers between devices: none -> 36.5 us  [the longest x1 21.9 us: body(): pay = lax.all_to_all(pay.reshape(PLANE, group, 2048), yc, 0, 0)]
    all_to_all x0 -> x3, starting transfers between devices: none -> 25.4 us  [the longest x1 14.9 us: body(): pay = lax.all_to_all(pay.reshape(PLANE, group, 2048), yc, 0, 0)]
    reshape x2 -> x9, local copies, waits for them, and re-layouts: 2 us -> 20.2 us  [the longest x2 11.4 us: body(): blocks_view = gathered.reshape(samples, ANC // 8, SEP_DEV)]
  transfers between devices with their start and end apart: 8 -> 4, of which waited for: 8 -> 4; matrix products, arithmetic and copies ran while one was open for 0% -> 8% of each run, Pallas kernels for 0% -> 0%
where the time goes in v1:
time: 233 us; the launch traced here: 231 us
  blocking collectives  63.4 us (27%)
  waiting for transfers between devices  51.8 us (22%)
  local copies, waits for them, and re-layouts  35.4 us (15%)
  matrix products  29.9 us (13%)
  starting transfers between devices  25.4 us (11%)
  between operations  14.6 us (6%)
  other arithmetic  10.9 us (5%)
    all_gather x1, blocking collectives, body(): lax.all_gather(own, ('zq', 'rhs'), axis=0, tiled=False)  43.6 us
    dot_general x20, matrix products, ein(): return jnp.einsum(spec, a, b, precision=exact)  29.9 us
    all_to_all x1, waiting for transfers between devices, body(): pay = lax.all_to_all(pay.reshape(PLANE, group, 2048), yc, 0, 0)  21.9 us
    all_gather x1, blocking collectives, body(): gathered = lax.all_gather(x, yc, axis=0, tiled=True)  19.7 us
    all_gather x1, waiting for transfers between devices, body(): path = lax.all_gather(packed, yc, axis=0, tiled=True)  15.3 us
    all_to_all x1, starting transfers between devices, body(): pay = lax.all_to_all(pay.reshape(PLANE, group, 2048), yc, 0, 0)  14.9 us
    reshape x2, local copies, waits for them, and re-layouts, body(): blocks_view = gathered.reshape(samples, ANC // 8, SEP_DEV)  11.4 us
    all_to_all x1, waiting for transfers between devices, body(): got = lax.all_to_all(jnp.broadcast_to(send, (8,) + send.shape), zz, 0, 0)  9.7 us
  transfers between devices with their start and end apart: 4, of which 4 were waited for; matrix products, arithmetic and copies ran while one was open for 8% of the time, Pallas kernels for 0%

profile of v1, /device:TPU:1, one launch (start us, length us, event | category | flops | bytes accessed | tf_op | source)
XLA Modules:
  0.0 231.3 jit_solution(10123868117476852024)
XLA Ops:
  7.2 0.9 pad_maximum_fusion.2
  8.2 43.6 %all-gather = f32[128,1568]{1,0:T(8,128)S(1)} all-gather(f32[8,1568]{1,0:T(8,128)S(1)} %pad_maximum_fusion.2), channel_id=2, replica_groups=mesh['zh'=2,'zq'=4,'y'=8,'core'=2,'rhs'=4] {'zq','rhs'}, dimensions={0}, use_global_device_ids=true | all-gather | bytes 852992 | tf_op jit(solution)/shard_map/all_gather | solution.py:44
  53.3 0.8 pad_maximum_fusion
  54.3 3.2 %convolution_bitcast_fusion.3 = f32[64,16,128]{2,0,1:T(8,128)S(1)} fusion(f32[16,128,128]{2,1,0:T(8,128)S(1)} %copy-done, f32[64,2048]{1,0:T(8,128)} %param.9), kind=kOutput, calls=%fused_computation.14 | convolution fusion | flops 201326592 | bytes 2097152 | tf_op jit(solution)/shard_map/rnt,nct->rnc/dot_general | solution.py:19
  57.5 0.9 convolution_bitcast_fusion.5
  59.2 1.3 copy.110
  60.6 1.3 constant_dynamic-update-slice_fusion.3
  61.9 1.3 constant_dynamic-update-slice_fusion.2
  63.1 1.3 constant_dynamic-update-slice_fusion.1
  64.4 1.3 constant_dynamic-update-slice_fusion
  65.7 1.5 maximum_maximum_fusion
  67.6 0.9 reshape.115
  68.5 14.9 %all-to-all-start = ((f32[16,4,2048]{2,1,0:T(4,128)}), f32[16,4,2048]{2,1,0:T(4,128)S(1)}, u32[]{:S(2)}, u32[]{:S(2)}) async-start(f32[16,4,2048]{2,1,0:T(4,128)} %reshape.115), calls=%async_computation | async-start | bytes 1048576 | tf_op jit(solution)/shard_map/all_to_all | solution.py:76
  83.7 21.9 %all-to-all-done = f32[16,4,2048]{2,1,0:T(4,128)S(1)} async-done(((f32[16,4,2048]{2,1,0:T(4,128)}), f32[16,4,2048]{2,1,0:T(4,128)S(1)}, u32[]{:S(2)}, u32[]{:S(2)}) %all-to-all-start) | async-done | bytes 524320 | tf_op jit(solution)/shard_map/all_to_all | solution.py:76
  106.5 15.3 %all-gather.4.cloned.1.call-done = f32[128,12672]{1,0:T(8,128)} async-done(((f32[8,12672]{1,0:T(8,128)}), f32[128,12672]{1,0:T(8,128)}) %all-gather.4.cloned.1.call-update) | async-done | bytes 6488080 | tf_op jit(solution)/shard_map/all_gather | solution.py:56
  121.8 2.9 %slice.181 = f32[128,3584]{1,0:T(8,128)} slice(f32[128,12672]{1,0:T(8,128)} %all-gather.4.cloned.1.call-done), slice={[0:128], [6144:9728]} | slice | bytes 3670016 | tf_op jit(solution)/shard_map/slice | solution.py:58
  124.7 1.6 reshape.121
  126.3 1.0 fusion.48
  127.3 1.7 convolution_subtract_fusion.1
  129.4 0.8 convolution_subtract_fusion
  130.2 3.9 %slice.186 = f32[128,6144]{1,0:T(8,128)} slice(f32[128,12672]{1,0:T(8,128)} %all-gather.4.cloned.1.call-done), slice={[0:128], [0:6144]} | slice | bytes 6291456 | tf_op jit(solution)/shard_map/slice | solution.py:57
  134.1 4.5 %reshape.122 = f32[512,1536]{1,0:T(8,128)} reshape(f32[128,6144]{1,0:T(8,128)} %slice.186) | data formatting | bytes 6291456 | tf_op jit(solution)/shard_map/reshape | solution.py:57
  138.6 2.2 multiply_add_fusion
  140.8 2.7 %fusion.10 = f32[4,1024]{1,0:T(4,128)S(1)} fusion(f32[4,512]{1,0:T(4,128)S(1)} %get-tuple-element.23, f32[512,1536]{1,0:T(8,128)} %reshape.122, f32[4,1536]{1,0:T(4,128)S(1)} %convolution_subtract_fusion), kind=kOutput, calls=%fused_computation.18 | convolution fusion | flops 25169920 | bytes 2138112 | tf_op jit(solution)/shard_map/rg,gc->rc/dot_general | solution.py:19
  143.5 0.7 broadcast_in_dim.7
  144.2 7.1 %all-to-all-start.1 = ((f32[8,4,1792]{2,1,0:T(4,128)}), f32[8,4,1792]{2,1,0:T(4,128)}, u32[]{:S(2)}, u32[]{:S(2)}) async-start(f32[8,4,1792]{2,1,0:T(4,128)} %broadcast_in_dim.7), calls=%async_computation.1 | async-start | bytes 458752 | tf_op jit(solution)/shard_map/all_to_all | solution.py:92
  152.2 9.7 %all-to-all-done.1 = f32[8,4,1792]{2,1,0:T(4,128)} async-done(((f32[8,4,1792]{2,1,0:T(4,128)}), f32[8,4,1792]{2,1,0:T(4,128)}, u32[]{:S(2)}, u32[]{:S(2)}) %all-to-all-start.1) | async-done | bytes 229408 | tf_op jit(solution)/shard_map/all_to_all | solution.py:92
  161.9 0.9 slice_reduce_fusion.1
  162.9 1.5 convolution_add_fusion
  164.3 1.5 fusion.31
  166.5 3.4 %all-to-all-start.2 = ((f32[8,4,1024]{2,1,0:T(4,128)}), f32[8,4,1024]{2,1,0:T(4,128)S(1)}, u32[]{:S(2)}, u32[]{:S(2)}) async-start(f32[8,4,1024]{2,1,0:T(4,128)} %broadcast_in_dim.8), calls=%async_computation.2 | async-start | bytes 262144 | tf_op jit(solution)/shard_map/all_to_all | solution.py:101
  169.9 0.8 slice.196
  170.7 0.8 slice.195
  171.5 0.7 fusion.52
  172.2 0.7 fusion.43
  172.9 4.9 %all-to-all-done.2 = f32[8,4,1024]{2,1,0:T(4,128)S(1)} async-done(((f32[8,4,1024]{2,1,0:T(4,128)}), f32[8,4,1024]{2,1,0:T(4,128)S(1)}, u32[]{:S(2)}, u32[]{:S(2)}) %all-to-all-start.2) | async-done | bytes 131104 | tf_op jit(solution)/shard_map/all_to_all | solution.py:101
  177.8 3.4 %fusion.13 = f32[4,512]{1,0:T(4,128)S(1)} fusion(f32[4,512]{1,0:T(4,128)} %fusion.43, f32[4,1024]{1,0:T(4,128)S(1)} %reduce_sum.47, f32[512,1536]{1,0:T(8,128)} %reshape.122), kind=kOutput, calls=%fused_computation.19 | convolution fusion | flops 25167872 | bytes 2129920 | tf_op jit(solution)/shard_map/rc,gc->rg/dot_general | solution.py:19
  181.2 1.8 fusion.19
  183.0 1.3 fusion.16
  184.6 2.0 convolution_subtract_fusion.2
  186.6 1.0 fusion.46
  187.6 19.7 %all-gather.1 = f32[16,4,1920]{2,1,0:T(4,128)S(1)} all-gather(f32[1,4,1920]{2,1,0:T(4,128)S(1)} %maximum_bitcast_fusion), channel_id=1, replica_groups=mesh['zh'=2,'zq'=4,'y'=8,'core'=2,'rhs'=4] {'y','core'}, dimensions={0}, use_global_device_ids=true | all-gather | bytes 522240 | tf_op jit(solution)/shard_map/all_gather | solution.py:111
  207.5 6.2 %reshape.124 = f32[64,240,8]{2,1,0:T(8,128)} reshape(f32[16,4,1920]{2,1,0:T(4,128)S(1)} %all-gather.1) | data formatting | bytes 983040 | tf_op jit(solution)/shard_map/reshape | solution.py:120
  214.0 0.7 copy.128
  214.7 5.2 %copy.124 = f32[64,240,8]{1,0,2:T(8,128)S(1)} copy(f32[64,240,8]{2,1,0:T(8,128)} %reshape.124) | data formatting | bytes 983040 | tf_op jit(solution)/shard_map/reshape | solution.py:120
  220.5 2.1 fusion.9
  222.5 1.1 convolution_bitcast_fusion
  223.6 0.8 copy.161
  (80 shorter events, 7.0 us)
Async XLA Ops:
  7.2 47.1 %copy-start = (f32[16,128,128]{2,1,0:T(8,128)S(1)}, f32[16,128,128]{2,1,0:T(8,128)}, u32[]{:S(2)}) copy-start(f32[16,128,128]{2,1,0:T(8,128)} %param.13) | copy-start | bytes 3145732
  7.2 114.6 %all-gather.4.cloned.1.call-start = ((), (), s32[]{:S(2)}) async-start(), calls=%async_computation.3 | async-start | bytes 6893568 | tf_op jit(solution)/shard_map/all_gather | solution.py:56
  52.4 1.7 copy-start.11
  52.7 4.7 %copy-start.1 = (f32[16,64,128]{2,1,0:T(8,128)S(1)}, f32[16,64,128]{2,1,0:T(8,128)}, u32[]{:S(2)}) copy-start(f32[16,64,128]{2,1,0:T(8,128)} %param.14) | copy-start | bytes 1572868
  54.3 6.3 %copy-start.3 = (s32[16,8]{1,0:T(8,128)}, s32[16,8]{1,0:T(8,128)S(1)}, u32[]{:S(2)}) copy-start(s32[16,8]{1,0:T(8,128)S(1)} %copy.107) | copy-start | bytes 1540
  54.3 6.3 %copy-start.9 = (f32[64,32]{0,1:T(8,128)S(1)}, f32[64,32]{0,1:T(8,128)}, u32[]{:S(2)}) copy-start(f32[64,32]{0,1:T(8,128)} %param.10) | copy-start | bytes 24580
  57.4 8.3 %copy-start.7 = (f32[64,32]{0,1:T(8,128)S(1)}, f32[64,32]{0,1:T(8,128)}, u32[]{:S(2)}) copy-start(f32[64,32]{0,1:T(8,128)} %param.12) | copy-start | bytes 24580
  68.5 37.1 %all-to-all-start = ((f32[16,4,2048]{2,1,0:T(4,128)}), f32[16,4,2048]{2,1,0:T(4,128)S(1)}, u32[]{:S(2)}, u32[]{:S(2)}) async-start(f32[16,4,2048]{2,1,0:T(4,128)} %reshape.115), calls=%async_computation | async-start | bytes 1048576 | tf_op jit(solution)/shard_map/all_to_all | solution.py:76
  127.3 2.0 copy-start.5
  144.2 17.7 %all-to-all-start.1 = ((f32[8,4,1792]{2,1,0:T(4,128)}), f32[8,4,1792]{2,1,0:T(4,128)}, u32[]{:S(2)}, u32[]{:S(2)}) async-start(f32[8,4,1792]{2,1,0:T(4,128)} %broadcast_in_dim.7), calls=%async_computation.1 | async-start | bytes 458752 | tf_op jit(solution)/shard_map/all_to_all | solution.py:92
  166.5 11.2 %all-to-all-start.2 = ((f32[8,4,1024]{2,1,0:T(4,128)}), f32[8,4,1024]{2,1,0:T(4,128)S(1)}, u32[]{:S(2)}, u32[]{:S(2)}) async-start(f32[8,4,1024]{2,1,0:T(4,128)} %broadcast_in_dim.8), calls=%async_computation.2 | async-start | bytes 262144 | tf_op jit(solution)/shard_map/all_to_all | solution.py:101
  177.8 5.3 %copy-start.8 = (f32[4,256]{1,0:T(4,128)S(1)}, f32[4,256]{1,0:T(4,128)}, u32[]{:S(2)}) copy-start(f32[4,256]{1,0:T(4,128)} %fusion.52) | copy-start | bytes 12292
  177.8 6.8 %copy-start.6 = (f32[4,128]{1,0:T(4,128)S(1)}, f32[4,128]{1,0:T(4,128)}, u32[]{:S(2)}) copy-start(f32[4,128]{1,0:T(4,128)} %copy-done.5) | copy-start | bytes 6148
  177.8 6.8 %copy-start.10 = (f32[4,128]{1,0:T(4,128)S(1)}, f32[4,128]{1,0:T(4,128)}, u32[]{:S(2)}) copy-start(f32[4,128]{1,0:T(4,128)} %squeeze.23) | copy-start | bytes 6148
  214.7 5.2 %copy-start.4 = (s32[16,8]{1,0:T(8,128)S(1)}, s32[16,8]{1,0:T(8,128)}, u32[]{:S(2)}) copy-start(s32[16,8]{1,0:T(8,128)} %copy-done.3) | copy-start | bytes 1540
  214.7 5.8 %copy-start.2 = (f32[16,64,128]{2,1,0:T(8,128)S(1)}, f32[16,64,128]{2,1,0:T(8,128)}, u32[]{:S(2)}) copy-start(f32[16,64,128]{2,1,0:T(8,128)} %param.14) | copy-start | bytes 1572868
Sparse Core Ops, SparseCore 0:
  54.2 67.4 all-gather.3

commit v2 on v1

v2 whole, which is shorter than its diff:
```python
import jax
import jax.numpy as jnp
from jax import lax
from jax.experimental import pallas as pl
from jax.experimental.pallas import tpu as pltpu
from jax.sharding import Mesh, PartitionSpec as P

SEP_DEV = 8
LEVELS = 4
NB = 8
ANC = 1920
PLANE = 16
GROUP = 4
SAMPLES = 64
NODES = 16
TILE = 128
STARTS = (0, 1024, 1536, 1792, 1920)
L2_AT = 6144
L3_AT = 9728
L0_AT = 11648
PACK = 12672

exact = lax.Precision.HIGHEST
VMEM_LIMIT = 48 * 1024 * 1024


def nn(a, b):
    return lax.dot_general(a, b, (((1,), (0,)), ((), ())), precision=exact, preferred_element_type=jnp.float32)


def nt(a, b):
    return lax.dot_general(a, b, (((1,), (1,)), ((), ())), precision=exact, preferred_element_type=jnp.float32)


def tn(a, b):
    return lax.dot_general(a, b, (((0,), (0,)), ((), ())), precision=exact, preferred_element_type=jnp.float32)


def vspec(n):
    return [pl.BlockSpec(memory_space=pltpu.VMEM)] * n


def call(kernel, outs, ins, smem=0, scratch=(), flops=0, nbytes=0):
    many = isinstance(outs, (list, tuple))
    return pl.pallas_call(
        kernel,
        out_shape=outs,
        in_specs=[pl.BlockSpec(memory_space=pltpu.SMEM)] * smem + vspec(len(ins) - smem),
        out_specs=tuple(vspec(len(outs))) if many else vspec(1)[0],
        scratch_shapes=list(scratch),
        compiler_params=pltpu.CompilerParams(vmem_limit_bytes=VMEM_LIMIT),
        cost_estimate=pl.CostEstimate(flops=flops, bytes_accessed=nbytes, transcendentals=0),
    )(*ins)


def f32(*shape):
    return jax.ShapeDtypeStruct(shape, jnp.float32)


def leaf_forward_kernel(blocks, at, shift, sep_t, sep_noise, inverse, panel, lf_out, pay_out, acc):
    acc[...] = jnp.zeros_like(acc)

    def step(n, carry):
        cols = pl.ds(pl.multiple_of(n * TILE, TILE), TILE)
        lf = nt(shift[:, cols], inverse[n])
        lf_out[:, cols] = lf
        pieces = nt(panel[n], lf)
        for b in range(NB):
            rows = pl.ds(pl.multiple_of(blocks[n, b] * SEP_DEV, SEP_DEV), SEP_DEV)
            acc[rows, :] = acc[rows, :] - pieces[b * SEP_DEV : (b + 1) * SEP_DEV, :]
        return carry

    lax.fori_loop(0, NODES, step, 0)
    for k in range(LEVELS):
        rows = pl.ds(pl.multiple_of(at[k], SEP_DEV), SEP_DEV)
        acc[rows, :] = acc[rows, :] + sep_t[k * SEP_DEV : (k + 1) * SEP_DEV, :]
    for c in range(ANC // TILE):
        pay_out[:, c * TILE : (c + 1) * TILE] = acc[c * TILE : (c + 1) * TILE, :].T
    pay_out[:, ANC:] = sep_noise[...]


def leaf_prepare_kernel(lf, noise, inverse, panel, base_out, w_out):
    def step(n, carry):
        cols = pl.ds(pl.multiple_of(n * TILE, TILE), TILE)
        base_out[:, cols] = nn(lf[:, cols] + noise[:, cols], inverse[n])
        w_out[n] = nn(panel[n], inverse[n])
        return carry

    lax.fori_loop(0, NODES, step, 0)


def forward_kernel(place, v, noise, path, send_out, g3_out):
    w = v[...]
    g3 = nt(w[:, 1792:], path[:, L3_AT : L3_AT + 128])
    w = w[:, :1792] - nn(g3, path[:, L3_AT + 128 : L0_AT])
    g3_out[...] = g3 + noise[3]
    zq = place[0]
    two = []
    r2 = w[:, 1536:]
    w = w[:, :1536]
    for p in range(2):
        at = L2_AT + p * 1792
        g = nt(r2, path[:, at : at + 256])
        w = w - nn(g, path[:, at + 256 : at + 1792])
        two.append(g + jnp.where(zq % 2 == p, noise[2], 0.0))
    r1 = w[:, 1024:]
    w = w[:, :1024]
    one = []
    for q in range(4):
        at = q * 1536
        g = nt(r1, path[:, at : at + 512])
        w = w - nn(g, path[:, at + 512 : at + 1536])
        one.append(g + jnp.where(zq == q, noise[1], 0.0))
    for d in range(8):
        send_out[d, :, :1024] = w
        for q in range(4):
            send_out[d, :, 1024 + q * 128 : 1152 + q * 128] = one[q]
        for p in range(2):
            send_out[d, :, 1536 + p * 128 : 1664 + p * 128] = two[p]


def top_kernel(got, noise, path, send_out):
    r0 = got[0, :, :1024]
    for d in range(1, 8):
        r0 = r0 + got[d, :, :1024]
    y0 = nt(r0, path[...]) + noise[0]
    x0 = nn(y0, path[...])
    for d in range(8):
        send_out[d] = x0


def backward_kernel(place, got, got0, g3, path, x_out):
    x0 = got0[0]
    for d in range(1, 8):
        x0 = x0 + got0[d]
    x_out[:, :1024] = x0
    z = place[0] + 4 * place[1]
    g1 = jnp.zeros((GROUP, 512), jnp.float32)
    g2 = jnp.zeros((GROUP, 256), jnp.float32)
    for d in range(8):
        g1 = g1 + jnp.where(z // 4 == d // 4, got[d, :, 1024:1536], 0.0)
        g2 = g2 + jnp.where(z // 2 == d // 2, got[d, :, 1536:], 0.0)
    x1 = jnp.zeros((GROUP, 512), jnp.float32)
    for q in range(4):
        at = q * 1536
        y = g1[:, q * 128 : (q + 1) * 128] - nt(x0, path[:, at + 512 : at + 1536])
        x1 = x1 + nn(y, path[:, at : at + 512])
    x_out[:, 1024:1536] = x1
    x2 = jnp.zeros((GROUP, 256), jnp.float32)
    for p in range(2):
        at = L2_AT + p * 1792
        y = g2[:, p * 128 : (p + 1) * 128] - nt(x_out[:, :1536], path[:, at + 256 : at + 1792])
        x2 = x2 + nn(y, path[:, at : at + 256])
    x_out[:, 1536:1792] = x2
    y = g3[...] - nt(x_out[:, :1792], path[:, L3_AT + 128 : L0_AT])
    x_out[:, 1792:] = nn(y, path[:, L3_AT : L3_AT + 128])


def leaf_backward_kernel(blocks, at, x, base, w, leaf_out, sep_out, rows_s, cols_s):
    for g in range(PLANE):
        rows_s[g * GROUP : (g + 1) * GROUP, :] = x[g]
    for c in range(ANC // TILE):
        cols_s[c * TILE : (c + 1) * TILE, :] = rows_s[:, c * TILE : (c + 1) * TILE].T
    for k in range(LEVELS):
        rows = pl.ds(pl.multiple_of(at[k], SEP_DEV), SEP_DEV)
        sep_out[k * SEP_DEV : (k + 1) * SEP_DEV, :] = cols_s[rows, :]

    def step(n, carry):
        cols = pl.ds(pl.multiple_of(n * TILE, TILE), TILE)
        picked = jnp.concatenate(
            [cols_s[pl.ds(pl.multiple_of(blocks[n, b] * SEP_DEV, SEP_DEV), SEP_DEV), :] for b in range(NB)],
            axis=0,
        )
        leaf_out[:, cols] = base[:, cols] - tn(picked, w[n])
        return carry

    lax.fori_loop(0, NODES, step, 0)


def body(
    leaf_shift,
    sep_shift,
    leaf_noise,
    sep_noise,
    leaf_inverse,
    leaf_panel,
    panel_blocks,
    sep_inverse,
    sep_coupling,
):
    yc = ("y", "core")
    zz = ("zh", "zq")
    zq = lax.axis_index("zq")
    zh = lax.axis_index("zh")
    dev = (zh * 4 + zq) * PLANE + lax.axis_index("y") * 2 + lax.axis_index("core")
    place = jnp.stack([zq, zh]).astype(jnp.int32)
    at = jnp.stack([STARTS[k] + dev % (128 >> k) * SEP_DEV for k in range(LEVELS)]).astype(jnp.int32)

    own = jnp.concatenate([sep_inverse, sep_coupling], axis=1)
    quad = lax.all_to_all(jnp.broadcast_to(own, (16,) + own.shape), ("zq", "rhs"), 0, 0)
    quad = jnp.transpose(quad.reshape(4, 4, 8, 1568), (0, 2, 1, 3))
    inv = quad[..., :480].reshape(4, 8, 1920)
    cou = quad[..., 480:].reshape(4, 8, 4352)
    l1 = jnp.concatenate([inv[..., 1024:1536], cou[..., :1024]], axis=2)
    l2 = jnp.concatenate([inv[..., 1536:1792], cou[..., 1024:2560]], axis=2)
    l2 = lax.dynamic_slice_in_dim(l2, zq // 2 * 2, 2, 0)
    l3 = jnp.concatenate([inv[..., 1792:], cou[..., 2560:]], axis=2)
    l3 = lax.dynamic_slice_in_dim(l3, zq, 1, 0)
    l0 = lax.dynamic_slice_in_dim(inv[..., :1024], zq, 1, 0)
    flat = lambda m: jnp.transpose(m, (1, 0, 2)).reshape(8, -1)
    packed = jnp.concatenate([flat(l1), flat(l2), flat(l3), flat(l0)], axis=1)
    path = lax.all_gather(packed, yc, axis=0, tiled=True)

    leaf_forward, pay = call(
        leaf_forward_kernel,
        [f32(SAMPLES, NODES * TILE), f32(SAMPLES, 2048)],
        [
            panel_blocks,
            at,
            leaf_shift,
            sep_shift.T,
            jnp.pad(sep_noise, ((0, 0), (0, 96))),
            leaf_inverse,
            leaf_panel,
        ],
        smem=2,
        scratch=[pltpu.VMEM((ANC, SAMPLES), jnp.float32)],
        flops=50_000_000,
        nbytes=3_000_000,
    )
    pay = lax.all_to_all(pay.reshape(PLANE, GROUP, 2048), yc, 0, 0)
    base, w = call(
        leaf_prepare_kernel,
        [f32(SAMPLES, NODES * TILE), f32(NODES, 64, TILE)],
        [leaf_forward, leaf_noise, leaf_inverse, leaf_panel],
        flops=70_000_000,
        nbytes=4_000_000,
    )
    v = jnp.sum(pay[..., :ANC], axis=0)
    noise = pay[..., ANC : ANC + 32].reshape(PLANE, GROUP, LEVELS, SEP_DEV)
    noise = jnp.transpose(noise, (2, 1, 0, 3)).reshape(LEVELS, GROUP, 128)

    send, g3 = call(
        forward_kernel,
        [f32(8, GROUP, 1792), f32(GROUP, 128)],
        [place, v, noise, path],
        smem=1,
        flops=12_000_000,
        nbytes=6_500_000,
    )
    got = lax.all_to_all(send, zz, 0, 0)
    top_send = call(
        top_kernel, f32(8, GROUP, 1024), [got, noise, path[:, L0_AT:]], flops=2_000_000, nbytes=600_000
    )
    got0 = lax.all_to_all(top_send, zz, 0, 0)
    x = call(
        backward_kernel,
        f32(GROUP, ANC),
        [place, got, got0, g3, path],
        smem=1,
        flops=12_000_000,
        nbytes=6_500_000,
    )
    gathered = lax.all_gather(x, yc, axis=0, tiled=False)

    leaf_out, sep_t = call(
        leaf_backward_kernel,
        [f32(SAMPLES, NODES * TILE), f32(LEVELS * SEP_DEV, SAMPLES)],
        [panel_blocks, at, gathered, base, w],
        smem=2,
        scratch=[pltpu.VMEM((SAMPLES, ANC), jnp.float32), pltpu.VMEM((ANC, SAMPLES), jnp.float32)],
        flops=20_000_000,
        nbytes=2_000_000,
    )
    return leaf_out, sep_t.T


def solution(mesh):
    inner = Mesh(mesh.devices.reshape(2, 4, 8, 2, 4), ("zh", "zq", "y", "core", "rhs"))
    leaf = ("zh", "zq", "y", "core")
    data = P("rhs", leaf)
    rows = P(leaf, "rhs")
    return jax.shard_map(
        body,
        mesh=inner,
        in_specs=(data, data, data, data, P(leaf), P(leaf), P(leaf), rows, rows),
        out_specs=(data, data),
        check_vma=False,
    )
```

time: 233 us -> 188 us (0.81)
  blocking collectives: 63.4 us -> 19.7 us
  Pallas kernels: 0 us -> 37.8 us
  matrix products: 29.9 us -> 0 us
  local copies, waits for them, and re-layouts: 35.4 us -> 9.15 us
  waiting for transfers between devices: 51.8 us -> 73.6 us
  other arithmetic: 10.9 us -> 2.03 us
  starting transfers between devices: 25.4 us -> 31 us
    all_gather x2 -> x1, blocking collectives: 63.4 us -> 19.7 us  [body(): gathered = lax.all_gather(x, yc, axis=0, tiled=False)]
    pallas_call x0 -> x6, Pallas kernels: none -> 37.8 us  [call(): pl.pallas_call(kernel, out_shape=outs, in_specs=[pl.BlockSpec(memory_spac...]
    dot_general x20 -> x0, matrix products: 29.9 us -> none  [ein(): return jnp.einsum(spec, a, b, precision=exact)]
    reshape x7 -> x2, local copies, waits for them, and re-layouts: 19.5 us -> 1.06 us  [the longest x1 0.94 us: body(): pay = lax.all_to_all(pay.reshape(PLANE, GROUP, 2048), yc, 0, 0)]
    all_to_all x3 -> x4, waiting for transfers between devices: 36.5 us -> 53.2 us  [the longest x1 22.2 us: body(): pay = lax.all_to_all(pay.reshape(PLANE, GROUP, 2048), yc, 0, 0)]
    slice x10 -> x2, local copies, waits for them, and re-layouts: 8.67 us -> 1.09 us  [the longest x1 1.08 us: body(): path[:, L0_AT:]]
    all_to_all x3 -> x4, starting transfers between devices: 25.4 us -> 31 us  [the longest x1 10.4 us: body(): lax.all_to_all(jnp.broadcast_to(own, (16,) + own.shape), ('zq', 'rhs'), 0...]
    all_gather x1, waiting for transfers between devices: 15.3 us -> 20.4 us  [body(): path = lax.all_gather(packed, yc, axis=0, tiled=True)]
  transfers between devices with their start and end apart: 4 -> 5, of which waited for: 4 -> 5; matrix products, arithmetic and copies ran while one was open for 8% -> 2% of each run, Pallas kernels for 0% -> 7%
where the time goes in v2:
time: 188 us
  waiting for transfers between devices  73.6 us (39%)
  Pallas kernels  37.8 us (20%)
  starting transfers between devices  31 us (16%)
  blocking collectives  19.7 us (10%)
  between operations  14.3 us (8%)
  local copies, waits for them, and re-layouts  9.15 us (5%)
  other arithmetic  2.03 us (1%)
    pallas_call x6, Pallas kernels, call(): pl.pallas_call(kernel, out_shape=outs, in_specs=[pl.BlockSpec(memory_spac...  37.8 us
    all_to_all x1, waiting for transfers between devices, body(): pay = lax.all_to_all(pay.reshape(PLANE, GROUP, 2048), yc, 0, 0)  22.2 us
    all_gather x1, waiting for transfers between devices, body(): path = lax.all_gather(packed, yc, axis=0, tiled=True)  20.4 us
    all_gather x1, blocking collectives, body(): gathered = lax.all_gather(x, yc, axis=0, tiled=False)  19.7 us
    all_to_all x1, waiting for transfers between devices, body(): lax.all_to_all(jnp.broadcast_to(own, (16,) + own.shape), ('zq', 'rhs'), 0...  19.1 us
    all_to_all x1, starting transfers between devices, body(): lax.all_to_all(jnp.broadcast_to(own, (16,) + own.shape), ('zq', 'rhs'), 0...  10.4 us
    all_to_all x1, starting transfers between devices, body(): pay = lax.all_to_all(pay.reshape(PLANE, GROUP, 2048), yc, 0, 0)  10.1 us
    all_to_all x1, waiting for transfers between devices, body(): got = lax.all_to_all(send, zz, 0, 0)  9.43 us
  transfers between devices with their start and end apart: 5, of which 5 were waited for; matrix products, arithmetic and copies ran while one was open for 2% of the time, Pallas kernels for 7%

profile of v2, /device:TPU:1, one launch (start us, length us, event | category | flops | bytes accessed | tf_op | source)
XLA Modules:
  0.0 187.5 jit_solution(7739599868072026775)
XLA Ops:
  7.2 0.0 copy-start.2
  7.2 0.0 copy-start.8
  7.2 0.0 copy-start
  7.2 0.0 copy-start.1
  7.2 1.0 pad_maximum_fusion.2
  8.2 1.0 broadcast_in_dim.3
  9.2 10.4 %all-to-all-start.1 = ((f32[16,8,1568]{2,1,0:T(8,128)}), f32[16,8,1568]{2,1,0:T(8,128)S(1)}, u32[]{:S(2)}, u32[]{:S(2)}) async-start(f32[16,8,1568]{2,1,0:T(8,128)} %broadcast_in_dim.3), calls=%async_computation.1 | async-start | bytes 1703936 | tf_op jit(solution)/shard_map/all_to_all | solution.py:200
  19.5 0.0 all-gather.4.cloned.1.call-start
  19.6 19.1 %all-to-all-done.1 = f32[16,8,1568]{2,1,0:T(8,128)S(1)} async-done(((f32[16,8,1568]{2,1,0:T(8,128)}), f32[16,8,1568]{2,1,0:T(8,128)S(1)}, u32[]{:S(2)}, u32[]{:S(2)}) %all-to-all-start.1) | async-done | bytes 802848 | tf_op jit(solution)/shard_map/all_to_all | solution.py:200
  38.7 0.2 copy.30
  38.9 0.2 reshape.32
  39.1 0.7 slice.58
  39.8 0.2 slice.52
  40.0 0.2 copy.31
  40.2 0.4 reshape.33
  40.6 0.8 dynamic-slice_bitcast_fusion
  41.5 0.8 pad_maximum_fusion
  42.2 0.0 all-gather.4.cloned.1.call-update
  42.3 0.8 copy.32.blocks
  43.1 0.8 copy.26
  43.9 0.1 pad_add_fusion.at
  44.0 0.0 copy-done.2
  44.0 0.0 copy-done.8
  44.0 0.0 copy-done
  44.0 9.4 %shard_map.104 = (f32[64,2048]{1,0:T(8,128)S(1)}, f32[64,2048]{1,0:T(8,128)S(1)}) custom-call(s32[16,8]{1,0:T(8,128)S(1)} %copy.32.blocks, s32[4]{0:T(128)S(1)} %pad_add_fusion.at, f32[64,2048]{1,0:T(8,128)S(1)} %copy-done.2, f32[32,64]{1,0:T(8,128)S(1)} %bitcast.28, f32[64,128]{1,0:T(8,128)S(1)} %pad.4.sep_noise, f32[16,128,128]{2,1,0:T(8,128)S(1)} %copy-done, ...), custom_call_target="tpu_custom_call" | custom-call | flops 50000000 | bytes 3000000 | tf_op jit(solution)/shard_map/pallas_call | solution.py:45
  53.4 0.9 reshape.28
  54.4 10.1 %all-to-all-start = ((f32[16,4,2048]{2,1,0:T(4,128)}), f32[16,4,2048]{2,1,0:T(4,128)S(1)}, u32[]{:S(2)}, u32[]{:S(2)}) async-start(f32[16,4,2048]{2,1,0:T(4,128)} %reshape.28), calls=%async_computation | async-start | bytes 1048576 | tf_op jit(solution)/shard_map/all_to_all | solution.py:231
  64.5 0.1 pad_add_fusion.1.place
  64.6 22.2 %all-to-all-done = f32[16,4,2048]{2,1,0:T(4,128)S(1)} async-done(((f32[16,4,2048]{2,1,0:T(4,128)}), f32[16,4,2048]{2,1,0:T(4,128)S(1)}, u32[]{:S(2)}, u32[]{:S(2)}) %all-to-all-start) | async-done | bytes 524320 | tf_op jit(solution)/shard_map/all_to_all | solution.py:231
  86.8 0.1 copy.33
  86.8 0.1 copy.29
  86.9 0.1 reshape.30.noise
  87.1 0.1 slice_reduce_fusion.v
  87.1 20.4 %all-gather.4.cloned.1.call-done.path = f32[128,12672]{1,0:T(8,128)} async-done(((f32[8,12672]{1,0:T(8,128)}), f32[128,12672]{1,0:T(8,128)}) %all-gather.4.cloned.1.call-update) | async-done | bytes 6488080 | tf_op jit(solution)/shard_map/all_gather | solution.py:212
  107.5 7.6 %shard_map.105 = (f32[8,4,1792]{2,1,0:T(4,128)}, f32[4,128]{1,0:T(4,128)S(1)}) custom-call(s32[2]{0:T(128)S(1)} %pad_add_fusion.1.place, f32[4,1920]{1,0:T(4,128)S(1)} %slice_reduce_fusion.v, f32[4,4,128]{2,1,0:T(4,128)S(1)} %reshape.30.noise, f32[128,12672]{1,0:T(8,128)} %all-gather.4.cloned.1.call-done.path), custom_call_target="tpu_custom_call" | custom-call | flops 12000000 | bytes 6500000 | tf_op jit(solution)/shard_map/pallas_call | solution.py:45
  115.1 7.1 %all-to-all-start.2 = ((f32[8,4,1792]{2,1,0:T(4,128)}), f32[8,4,1792]{2,1,0:T(4,128)S(1)}, u32[]{:S(2)}, u32[]{:S(2)}) async-start(f32[8,4,1792]{2,1,0:T(4,128)} %get-tuple-element.11), calls=%async_computation.2 | async-start | bytes 458752 | tf_op jit(solution)/shard_map/all_to_all | solution.py:251
  122.2 1.1 slice.59.path
  123.3 9.4 %all-to-all-done.2.got = f32[8,4,1792]{2,1,0:T(4,128)S(1)} async-done(((f32[8,4,1792]{2,1,0:T(4,128)}), f32[8,4,1792]{2,1,0:T(4,128)S(1)}, u32[]{:S(2)}, u32[]{:S(2)}) %all-to-all-start.2) | async-done | bytes 229408 | tf_op jit(solution)/shard_map/all_to_all | solution.py:251
  132.7 1.9 %shard_map.106 = f32[8,4,1024]{2,1,0:T(4,128)} custom-call(f32[8,4,1792]{2,1,0:T(4,128)S(1)} %all-to-all-done.2.got, f32[4,4,128]{2,1,0:T(4,128)S(1)} %reshape.30.noise, f32[128,1024]{1,0:T(8,128)S(1)} %slice.59.path), custom_call_target="tpu_custom_call" | custom-call | flops 2000000 | bytes 600000 | tf_op jit(solution)/shard_map/pallas_call | solution.py:45
  134.6 3.4 %all-to-all-start.3 = ((f32[8,4,1024]{2,1,0:T(4,128)}), f32[8,4,1024]{2,1,0:T(4,128)S(1)}, u32[]{:S(2)}, u32[]{:S(2)}) async-start(f32[8,4,1024]{2,1,0:T(4,128)} %shard_map.106), calls=%async_computation.3 | async-start | bytes 262144 | tf_op jit(solution)/shard_map/all_to_all | solution.py:255
  138.0 3.7 %shard_map.108 = (f32[64,2048]{1,0:T(8,128)S(1)}, f32[16,64,128]{2,1,0:T(8,128)S(1)}) custom-call(f32[64,2048]{1,0:T(8,128)S(1)} %get-tuple-element.13.lf, f32[64,2048]{1,0:T(8,128)S(1)} %copy-done.3, f32[16,128,128]{2,1,0:T(8,128)S(1)} %copy-done, f32[16,64,128]{2,1,0:T(8,128)S(1)} %copy-done.1), custom_call_target="tpu_custom_call" | custom-call | flops 70000000 | bytes 4000000 | tf_op jit(solution)/shard_map/pallas_call | solution.py:45
  141.7 0.8 copy-done.4
  142.5 0.8 copy-done.6
  143.4 2.5 %all-to-all-done.3.got0 = f32[8,4,1024]{2,1,0:T(4,128)S(1)} async-done(((f32[8,4,1024]{2,1,0:T(4,128)}), f32[8,4,1024]{2,1,0:T(4,128)S(1)}, u32[]{:S(2)}, u32[]{:S(2)}) %all-to-all-start.3) | async-done | bytes 131104 | tf_op jit(solution)/shard_map/all_to_all | solution.py:255
  145.9 9.6 %shard_map.107 = f32[4,1920]{1,0:T(4,128)S(1)} custom-call(s32[2]{0:T(128)S(1)} %pad_add_fusion.1.place, f32[8,4,1792]{2,1,0:T(4,128)S(1)} %all-to-all-done.2.got, f32[8,4,1024]{2,1,0:T(4,128)S(1)} %all-to-all-done.3.got0, f32[4,128]{1,0:T(4,128)S(1)} %get-tuple-element.12.g3, f32[128,12672]{1,0:T(8,128)} %all-gather.4.cloned.1.call-done.path), custom_call_target="tpu_custom_call" | custom-call | flops 12000000 | bytes 6500000 | tf_op jit(solution)/shard_map/pallas_call | solution.py:45
  155.4 19.7 %all-gather.1.x = f32[16,4,1920]{2,1,0:T(4,128)S(1)} all-gather(f32[1,4,1920]{2,1,0:T(4,128)S(1)} %bitcast.27), channel_id=2, replica_groups=mesh['zh'=2,'zq'=4,'y'=8,'core'=2,'rhs'=4] {'y','core'}, dimensions={0}, use_global_device_ids=true | all-gather | bytes 522240 | tf_op jit(solution)/shard_map/all_gather | solution.py:264
  175.2 0.0 copy-done.7
  175.2 5.5 %shard_map.109 = (f32[64,2048]{1,0:T(8,128)}, f32[32,64]{1,0:T(8,128)}) custom-call(s32[16,8]{1,0:T(8,128)S(1)} %copy.32.blocks, s32[4]{0:T(128)S(1)} %pad_add_fusion.at, f32[16,4,1920]{2,1,0:T(4,128)S(1)} %all-gather.1.x, f32[64,2048]{1,0:T(8,128)S(1)} %copy-done.5, f32[16,64,128]{2,1,0:T(8,128)S(1)} %copy-done.7), custom_call_target="tpu_custom_call" | custom-call | flops 20000000 | bytes 2000000 | tf_op jit(solution)/shard_map/pallas_call | solution.py:45
  (20 shorter events, 0.1 us)
Async XLA Ops:
  7.2 36.8 %copy-start.2 = (f32[64,2048]{1,0:T(8,128)S(1)}, f32[64,2048]{1,0:T(8,128)}, u32[]{:S(2)}) copy-start(f32[64,2048]{1,0:T(8,128)} %shift.1) | copy-start | bytes 1572868
  7.2 36.8 %copy-start.8 = (f32[64,32]{0,1:T(8,128)S(1)}, f32[64,32]{0,1:T(8,128)}, u32[]{:S(2)}) copy-start(f32[64,32]{0,1:T(8,128)} %param.10) | copy-start | bytes 24580
  7.2 36.8 %copy-start = (f32[16,128,128]{2,1,0:T(8,128)S(1)}, f32[16,128,128]{2,1,0:T(8,128)}, u32[]{:S(2)}) copy-start(f32[16,128,128]{2,1,0:T(8,128)} %inverse.3) | copy-start | bytes 3145732
  7.2 36.8 %copy-start.1 = (f32[16,64,128]{2,1,0:T(8,128)S(1)}, f32[16,64,128]{2,1,0:T(8,128)}, u32[]{:S(2)}) copy-start(f32[16,64,128]{2,1,0:T(8,128)} %panel.3) | copy-start | bytes 1572868
  9.2 29.5 %all-to-all-start.1 = ((f32[16,8,1568]{2,1,0:T(8,128)}), f32[16,8,1568]{2,1,0:T(8,128)S(1)}, u32[]{:S(2)}, u32[]{:S(2)}) async-start(f32[16,8,1568]{2,1,0:T(8,128)} %broadcast_in_dim.3), calls=%async_computation.1 | async-start | bytes 1703936 | tf_op jit(solution)/shard_map/all_to_all | solution.py:200
  19.5 88.0 %all-gather.4.cloned.1.call-start = ((), (), s32[]{:S(2)}) async-start(), calls=%async_computation.4 | async-start | bytes 6893568 | tf_op jit(solution)/shard_map/all_gather | solution.py:212
  53.4 84.6 %copy-start.3 = (f32[64,2048]{1,0:T(8,128)S(1)}, f32[64,2048]{1,0:T(8,128)}, u32[]{:S(2)}) copy-start(f32[64,2048]{1,0:T(8,128)} %noise.1) | copy-start | bytes 1572868
  54.4 32.4 %all-to-all-start = ((f32[16,4,2048]{2,1,0:T(4,128)}), f32[16,4,2048]{2,1,0:T(4,128)S(1)}, u32[]{:S(2)}, u32[]{:S(2)}) async-start(f32[16,4,2048]{2,1,0:T(4,128)} %reshape.28), calls=%async_computation | async-start | bytes 1048576 | tf_op jit(solution)/shard_map/all_to_all | solution.py:231
  115.1 17.6 %all-to-all-start.2 = ((f32[8,4,1792]{2,1,0:T(4,128)}), f32[8,4,1792]{2,1,0:T(4,128)S(1)}, u32[]{:S(2)}, u32[]{:S(2)}) async-start(f32[8,4,1792]{2,1,0:T(4,128)} %get-tuple-element.11), calls=%async_computation.2 | async-start | bytes 458752 | tf_op jit(solution)/shard_map/all_to_all | solution.py:251
  134.6 11.2 %all-to-all-start.3 = ((f32[8,4,1024]{2,1,0:T(4,128)}), f32[8,4,1024]{2,1,0:T(4,128)S(1)}, u32[]{:S(2)}, u32[]{:S(2)}) async-start(f32[8,4,1024]{2,1,0:T(4,128)} %shard_map.106), calls=%async_computation.3 | async-start | bytes 262144 | tf_op jit(solution)/shard_map/all_to_all | solution.py:255
  141.7 0.8 copy-start.4
  142.5 0.8 copy-start.6
  145.9 29.3 %copy-start.5 = (f32[64,2048]{1,0:T(8,128)S(1)}, f32[64,2048]{1,0:T(8,128)}, u32[]{:S(2)}) copy-start(f32[64,2048]{1,0:T(8,128)} %copy-done.4) | copy-start | bytes 1572868
  145.9 29.3 %copy-start.7 = (f32[16,64,128]{2,1,0:T(8,128)S(1)}, f32[16,64,128]{2,1,0:T(8,128)}, u32[]{:S(2)}) copy-start(f32[16,64,128]{2,1,0:T(8,128)} %copy-done.6) | copy-start | bytes 1572868
Sparse Core Ops, SparseCore 0:
  42.4 65.0 all-gather.3

commit v3 on v2

--- a/solution.py
+++ b/solution.py
@@ -19,9 +19,10 @@
 L3_AT = 9728
 L0_AT = 11648
 PACK = 12672
+RANGES = {"l1": (0, L2_AT), "l2": (L2_AT, L3_AT), "l3": (L3_AT, L0_AT)}
 
 exact = lax.Precision.HIGHEST
-VMEM_LIMIT = 48 * 1024 * 1024
+MIB = 1024 * 1024
 
 
 def nn(a, b):
@@ -40,15 +41,17 @@
     return [pl.BlockSpec(memory_space=pltpu.VMEM)] * n
 
 
-def call(kernel, outs, ins, smem=0, scratch=(), flops=0, nbytes=0):
+def call(kernel, outs, ins, smem=0, hbm=0, scratch=(), flops=0, nbytes=0, vmem=12):
     many = isinstance(outs, (list, tuple))
     return pl.pallas_call(
         kernel,
         out_shape=outs,
-        in_specs=[pl.BlockSpec(memory_space=pltpu.SMEM)] * smem + vspec(len(ins) - smem),
+        in_specs=[pl.BlockSpec(memory_space=pltpu.SMEM)] * smem
+        + vspec(len(ins) - smem - hbm)
+        + [pl.BlockSpec(memory_space=pl.ANY)] * hbm,
         out_specs=tuple(vspec(len(outs))) if many else vspec(1)[0],
         scratch_shapes=list(scratch),
-        compiler_params=pltpu.CompilerParams(vmem_limit_bytes=VMEM_LIMIT),
+        compiler_params=pltpu.CompilerParams(vmem_limit_bytes=vmem * MIB),
         cost_estimate=pl.CostEstimate(flops=flops, bytes_accessed=nbytes, transcendentals=0),
     )(*ins)
 
@@ -89,12 +92,24 @@
     lax.fori_loop(0, NODES, step, 0)
 
 
-def forward_kernel(place, v, noise, path, send_out, g3_out):
+def fetch(source, path, sems, order):
+    copies = {}
+    for name in order:
+        lo, hi = RANGES[name]
+        copies[name] = pltpu.make_async_copy(source.at[:, lo:hi], path.at[:, lo:hi], sems.at[order.index(name)])
+        copies[name].start()
+    return copies
+
+
+def forward_kernel(place, v, noise, source, send_out, g3_out, path, sems):
+    copies = fetch(source, path, sems, ("l3", "l2", "l1"))
     w = v[...]
+    copies["l3"].wait()
     g3 = nt(w[:, 1792:], path[:, L3_AT : L3_AT + 128])
     w = w[:, :1792] - nn(g3, path[:, L3_AT + 128 : L0_AT])
     g3_out[...] = g3 + noise[3]
     zq = place[0]
+    copies["l2"].wait()
     two = []
     r2 = w[:, 1536:]
     w = w[:, :1536]
@@ -105,6 +120,7 @@
         two.append(g + jnp.where(zq % 2 == p, noise[2], 0.0))
     r1 = w[:, 1024:]
     w = w[:, :1024]
+    copies["l1"].wait()
     one = []
     for q in range(4):
         at = q * 1536
@@ -119,17 +135,21 @@
             send_out[d, :, 1536 + p * 128 : 1664 + p * 128] = two[p]
 
 
-def top_kernel(got, noise, path, send_out):
+def top_kernel(got, noise, source, send_out, path, sem):
+    copy = pltpu.make_async_copy(source.at[:, L0_AT:], path, sem)
+    copy.start()
     r0 = got[0, :, :1024]
     for d in range(1, 8):
         r0 = r0 + got[d, :, :1024]
+    copy.wait()
     y0 = nt(r0, path[...]) + noise[0]
     x0 = nn(y0, path[...])
     for d in range(8):
         send_out[d] = x0
 
 
-def backward_kernel(place, got, got0, g3, path, x_out):
+def backward_kernel(place, got, got0, g3, source, x_out, path, sems):
+    copies = fetch(source, path, sems, ("l1", "l2", "l3"))
     x0 = got0[0]
     for d in range(1, 8):
         x0 = x0 + got0[d]
@@ -140,18 +160,21 @@
     for d in range(8):
         g1 = g1 + jnp.where(z // 4 == d // 4, got[d, :, 1024:1536], 0.0)
         g2 = g2 + jnp.where(z // 2 == d // 2, got[d, :, 1536:], 0.0)
+    copies["l1"].wait()
     x1 = jnp.zeros((GROUP, 512), jnp.float32)
     for q in range(4):
         at = q * 1536
         y = g1[:, q * 128 : (q + 1) * 128] - nt(x0, path[:, at + 512 : at + 1536])
         x1 = x1 + nn(y, path[:, at : at + 512])
     x_out[:, 1024:1536] = x1
+    copies["l2"].wait()
     x2 = jnp.zeros((GROUP, 256), jnp.float32)
     for p in range(2):
         at = L2_AT + p * 1792
         y = g2[:, p * 128 : (p + 1) * 128] - nt(x_out[:, :1536], path[:, at + 256 : at + 1792])
         x2 = x2 + nn(y, path[:, at : at + 256])
     x_out[:, 1536:1792] = x2
+    copies["l3"].wait()
     y = g3[...] - nt(x_out[:, :1792], path[:, L3_AT + 128 : L0_AT])
     x_out[:, 1792:] = nn(y, path[:, L3_AT : L3_AT + 128])
 
@@ -198,6 +221,29 @@
 
     own = jnp.concatenate([sep_inverse, sep_coupling], axis=1)
     quad = lax.all_to_all(jnp.broadcast_to(own, (16,) + own.shape), ("zq", "rhs"), 0, 0)
+    first = lax.axis_index("core") == 0
+    noise_slot = jnp.concatenate(
+        [jnp.where(first, sep_noise, 0.0), jnp.where(first, 0.0, sep_noise), jnp.zeros((SAMPLES, 64), jnp.float32)],
+        axis=1,
+    )
+    leaf_forward, pay = call(
+        leaf_forward_kernel,
+        [f32(SAMPLES, NODES * TILE), f32(SAMPLES, 2048)],
+        [
+            panel_blocks,
+            at,
+            leaf_shift,
+            sep_shift.T,
+            noise_slot,
+            leaf_inverse,
+            leaf_panel,
+        ],
+        smem=2,
+        scratch=[pltpu.VMEM((ANC, SAMPLES), jnp.float32)],
+        flops=50_000_000,
+        nbytes=3_000_000,
+    )
+    quad, pay = lax.optimization_barrier((quad, pay))
     quad = jnp.transpose(quad.reshape(4, 4, 8, 1568), (0, 2, 1, 3))
     inv = quad[..., :480].reshape(4, 8, 1920)
     cou = quad[..., 480:].reshape(4, 8, 4352)
@@ -211,24 +257,12 @@
     packed = jnp.concatenate([flat(l1), flat(l2), flat(l3), flat(l0)], axis=1)
     path = lax.all_gather(packed, yc, axis=0, tiled=True)
 
-    leaf_forward, pay = call(
-        leaf_forward_kernel,
-        [f32(SAMPLES, NODES * TILE), f32(SAMPLES, 2048)],
-        [
-            panel_blocks,
-            at,
-            leaf_shift,
-            sep_shift.T,
-            jnp.pad(sep_noise, ((0, 0), (0, 96))),
-            leaf_inverse,
-            leaf_panel,
-        ],
-        smem=2,
-        scratch=[pltpu.VMEM((ANC, SAMPLES), jnp.float32)],
-        flops=50_000_000,
-        nbytes=3_000_000,
-    )
-    pay = lax.all_to_all(pay.reshape(PLANE, GROUP, 2048), yc, 0, 0)
+    core = lax.axis_index("core")
+    pay = pay.reshape(8, 2, GROUP, 2048)
+    kept = lax.dynamic_index_in_dim(pay, core, 1, False)
+    sent = lax.dynamic_index_in_dim(pay, 1 - core, 1, False)
+    pay = kept + lax.ppermute(sent, "core", [(0, 1), (1, 0)])
+    pay = lax.all_to_all(pay, "y", 0, 0)
     base, w = call(
         leaf_prepare_kernel,
         [f32(SAMPLES, NODES * TILE), f32(NODES, 64, TILE)],
@@ -237,20 +271,31 @@
         nbytes=4_000_000,
     )
     v = jnp.sum(pay[..., :ANC], axis=0)
-    noise = pay[..., ANC : ANC + 32].reshape(PLANE, GROUP, LEVELS, SEP_DEV)
-    noise = jnp.transpose(noise, (2, 1, 0, 3)).reshape(LEVELS, GROUP, 128)
-
+    noise = pay[..., ANC : ANC + 64].reshape(8, GROUP, 2, LEVELS, SEP_DEV)
+    noise = jnp.transpose(noise, (3, 1, 0, 2, 4)).reshape(LEVELS, GROUP, 128)
+
+    v, base, w = lax.optimization_barrier((v, base, w))
     send, g3 = call(
         forward_kernel,
         [f32(8, GROUP, 1792), f32(GROUP, 128)],
         [place, v, noise, path],
         smem=1,
+        hbm=1,
+        scratch=[pltpu.VMEM((128, L0_AT), jnp.float32), pltpu.SemaphoreType.DMA((3,))],
+        vmem=56,
         flops=12_000_000,
         nbytes=6_500_000,
     )
     got = lax.all_to_all(send, zz, 0, 0)
     top_send = call(
-        top_kernel, f32(8, GROUP, 1024), [got, noise, path[:, L0_AT:]], flops=2_000_000, nbytes=600_000
+        top_kernel,
+        f32(8, GROUP, 1024),
+        [got, noise, path],
+        hbm=1,
+        scratch=[pltpu.VMEM((128, 1024), jnp.float32), pltpu.SemaphoreType.DMA],
+        vmem=56,
+        flops=2_000_000,
+        nbytes=600_000,
     )
     got0 = lax.all_to_all(top_send, zz, 0, 0)
     x = call(
@@ -258,6 +303,9 @@
         f32(GROUP, ANC),
         [place, got, got0, g3, path],
         smem=1,
+        hbm=1,
+        scratch=[pltpu.VMEM((128, L0_AT), jnp.float32), pltpu.SemaphoreType.DMA((3,))],
+        vmem=56,
         flops=12_000_000,
         nbytes=6_500_000,
     )

time: 188 us -> 196 us (1.043)
  waiting for transfers between devices: 73.6 us -> 40 us
  blocking collectives: 19.7 us -> 50 us
  local copies, waits for them, and re-layouts: 9.15 us -> 23.1 us
  starting transfers between devices: 31 us -> 22.2 us
  other arithmetic: 2.03 us -> 4.87 us
  Pallas kernels: 37.8 us -> 40.5 us
    all_to_all x0 -> x2, blocking collectives: none -> 30.1 us  [the longest x1 18.2 us: body(): got = lax.all_to_all(send, zz, 0, 0)]
    all_to_all x3 -> x1, waiting for transfers between devices: 34.1 us -> 8.21 us  [body(): pay = lax.all_to_all(pay, 'y', 0, 0)]
    all_to_all x1, waiting for transfers between devices: 19.1 us -> 3.77 us  [body(): lax.all_to_all(jnp.broadcast_to(own, (16,) + own.shape), ('zq', 'rhs'), 0...]
    all_to_all x3 -> x1, starting transfers between devices: 20.6 us -> 6.82 us  [body(): pay = lax.all_to_all(pay, 'y', 0, 0)]
    all_gather x1, waiting for transfers between devices: 20.4 us -> 26.9 us  [body(): path = lax.all_gather(packed, yc, axis=0, tiled=True)]
    ppermute x0 -> x1, starting transfers between devices: none -> 4.93 us  [body(): pay = kept + lax.ppermute(sent, 'core', [(0, 1), (1, 0)])]
    unnamed x21 -> x20, local copies, waits for them, and re-layouts: 3.28 us -> 6.41 us
    pallas_call x6, Pallas kernels: 37.8 us -> 40.5 us  [call(): pl.pallas_call(kernel, out_shape=outs, in_specs=[pl.BlockSpec(memory_spac...]
  transfers between devices with their start and end apart: 5 -> 4, of which waited for: 5 -> 4; matrix products, arithmetic and copies ran while one was open for 2% -> 4% of each run, Pallas kernels for 7% -> 7%
where the time goes in v3:
time: 196 us; the launch traced here: 195 us
  blocking collectives  50 us (26%)
  Pallas kernels  40.5 us (21%)
  waiting for transfers between devices  40 us (20%)
  local copies, waits for them, and re-layouts  23.1 us (12%)
  starting transfers between devices  22.2 us (11%)
  between operations  14.3 us (7%)
  other arithmetic  4.87 us (2%)
    pallas_call x6, Pallas kernels, call(): pl.pallas_call(kernel, out_shape=outs, in_specs=[pl.BlockSpec(memory_spac...  40.5 us
    all_gather x1, waiting for transfers between devices, body(): path = lax.all_gather(packed, yc, axis=0, tiled=True)  26.9 us
    all_gather x1, blocking collectives, body(): gathered = lax.all_gather(x, yc, axis=0, tiled=False)  19.9 us
    all_to_all x1, blocking collectives, body(): got = lax.all_to_all(send, zz, 0, 0)  18.2 us
    all_to_all x1, blocking collectives, body(): got0 = lax.all_to_all(top_send, zz, 0, 0)  11.9 us
    all_to_all x1, starting transfers between devices, body(): lax.all_to_all(jnp.broadcast_to(own, (16,) + own.shape), ('zq', 'rhs'), 0...  10.4 us
    all_to_all x1, waiting for transfers between devices, body(): pay = lax.all_to_all(pay, 'y', 0, 0)  8.21 us
    all_to_all x1, starting transfers between devices, body(): pay = lax.all_to_all(pay, 'y', 0, 0)  6.82 us
  transfers between devices with their start and end apart: 4, of which 4 were waited for; matrix products, arithmetic and copies ran while one was open for 4% of the time, Pallas kernels for 7%

profile of v3, /device:TPU:1, one launch (start us, length us, event | category | flops | bytes accessed | tf_op | source)
XLA Modules:
  0.0 194.9 jit_solution(3564394923611794456)
XLA Ops:
  7.2 0.8 pad_maximum_fusion.2
  8.0 1.0 broadcast_in_dim.12
  9.0 10.4 %all-to-all-start = ((f32[16,8,1568]{2,1,0:T(8,128)}), f32[16,8,1568]{2,1,0:T(8,128)}, u32[]{:S(2)}, u32[]{:S(2)}) async-start(f32[16,8,1568]{2,1,0:T(8,128)} %broadcast_in_dim.12), calls=%async_computation | async-start | bytes 1703936 | tf_op jit(solution)/shard_map/all_to_all | solution.py:223
  19.6 0.8 copy.38.blocks
  20.3 0.8 copy.31
  21.2 0.1 pad_add_fusion.at
  21.3 0.1 maximum_maximum_fusion.sep_noise
  21.4 1.2 copy-done
  22.6 1.0 copy-done.2
  23.7 1.0 copy-done.4
  24.7 0.7 copy-done.8
  25.4 9.4 %shard_map.104 = (f32[64,2048]{1,0:T(8,128)S(1)}, f32[64,2048]{1,0:T(8,128)S(1)}) custom-call(s32[16,8]{1,0:T(8,128)S(1)} %copy.38.blocks, s32[4]{0:T(128)S(1)} %pad_add_fusion.at, f32[64,2048]{1,0:T(8,128)S(1)} %copy-done.4, f32[32,64]{1,0:T(8,128)S(1)} %bitcast.29, f32[64,128]{1,0:T(8,128)S(1)} %maximum_maximum_fusion.sep_noise, ...), custom_call_target="tpu_custom_call" | custom-call | flops 50000000 | bytes 3000000 | tf_op jit(solution)/shard_map/pallas_call | solution.py:46
  34.9 3.8 %all-to-all-done = f32[16,8,1568]{2,1,0:T(8,128)} async-done(((f32[16,8,1568]{2,1,0:T(8,128)}), f32[16,8,1568]{2,1,0:T(8,128)}, u32[]{:S(2)}, u32[]{:S(2)}) %all-to-all-start) | async-done | bytes 802848 | tf_op jit(solution)/shard_map/all_to_all | solution.py:223
  38.7 1.0 slice.46
  39.6 0.2 copy.36
  39.8 0.9 reshape.32
  40.8 0.9 slice.54
  41.7 0.7 slice.52
  42.4 1.3 slice.48
  43.7 0.8 slice.50
  44.5 1.0 copy.37
  45.4 2.3 %reshape.33 = f32[4,8,4352]{2,1,0:T(8,128)} reshape(f32[4,8,4,1088]{3,2,1,0:T(4,128)} %copy.37) | data formatting | bytes 1114112 | tf_op jit(solution)/shard_map/reshape | solution.py:249
  47.7 1.0 slice.53
  48.6 0.9 slice.51
  49.6 0.9 slice.49
  50.5 0.8 slice.47
  51.4 0.8 pad_maximum_fusion
  52.2 0.9 reshape.28
  53.2 1.0 dynamic-slice_bitcast_fusion
  54.2 4.9 %collective-permute-start = (f32[8,4,2048]{2,1,0:T(4,128)S(1)}, f32[8,4,2048]{2,1,0:T(4,128)S(1)}, u32[]{:S(2)}, u32[]{:S(2)}) collective-permute-start(f32[8,4,2048]{2,1,0:T(4,128)S(1)} %dynamic-slice_bitcast_fusion), channel_id=1, source_target_pairs={{0,4},{4,0},{1,5},{5,1},{2,6},{6,2},{3,7},{7,3},{8,12},{12,8},{9,1... | collective-permute-start | bytes 786440 | tf_op jit(solution)/shard_map/ppermute | solution.py:264
  59.1 1.1 collective-permute-done
  60.2 1.7 bitcast_add_fusion
  62.0 6.8 %all-to-all-start.1 = ((f32[8,4,2048]{2,1,0:T(4,128)}), f32[8,4,2048]{2,1,0:T(4,128)S(1)}, u32[]{:S(2)}, u32[]{:S(2)}) async-start(f32[8,4,2048]{2,1,0:T(4,128)} %bitcast_add_fusion), calls=%async_computation.1 | async-start | bytes 524288 | tf_op jit(solution)/shard_map/all_to_all | solution.py:265
  68.8 3.7 %shard_map.105 = (f32[64,2048]{1,0:T(8,128)S(1)}, f32[16,64,128]{2,1,0:T(8,128)S(1)}) custom-call(f32[64,2048]{1,0:T(8,128)S(1)} %get-tuple-element.17.lf, f32[64,2048]{1,0:T(8,128)S(1)} %copy-done.5, f32[16,128,128]{2,1,0:T(8,128)S(1)} %copy-done.1, f32[16,64,128]{2,1,0:T(8,128)S(1)} %copy-done.3), custom_call_target="tpu_custom_call" | custom-call | flops 70000000 | bytes 4000000 | tf_op jit(solution)/shard_map/pallas_call | solution.py:46
  72.6 0.8 copy-done.6
  73.4 0.7 pad_add_fusion.1.place
  74.0 8.2 %all-to-all-done.1 = f32[8,4,2048]{2,1,0:T(4,128)S(1)} async-done(((f32[8,4,2048]{2,1,0:T(4,128)}), f32[8,4,2048]{2,1,0:T(4,128)S(1)}, u32[]{:S(2)}, u32[]{:S(2)}) %all-to-all-start.1) | async-done | bytes 262176 | tf_op jit(solution)/shard_map/all_to_all | solution.py:265
  82.2 0.6 slice_reduce_fusion.v
  82.9 0.1 reshape.29
  83.1 0.8 reshape.30.noise
  83.9 26.9 %all-gather.4.cloned.1.call-done.source = f32[128,12672]{1,0:T(8,128)} async-done(((f32[8,12672]{1,0:T(8,128)}), f32[128,12672]{1,0:T(8,128)}) %all-gather.4.cloned.1.call-update) | async-done | bytes 6488080 | tf_op jit(solution)/shard_map/all_gather | solution.py:258
  110.8 7.1 %shard_map.106 = (f32[8,4,1792]{2,1,0:T(4,128)}, f32[4,128]{1,0:T(4,128)}) custom-call(s32[2]{0:T(128)} %pad_add_fusion.1.place, f32[4,1920]{1,0:T(4,128)} %slice_reduce_fusion.v, f32[4,4,128]{2,1,0:T(4,128)} %reshape.30.noise, f32[128,12672]{1,0:T(8,128)} %all-gather.4.cloned.1.call-done.source), custom_call_target="tpu_custom_call" | custom-call | flops 12000000 | bytes 6500000 | tf_op jit(solution)/shard_map/pallas_call | solution.py:46
  117.9 18.2 %all_to_all.20.got = f32[8,4,1792]{2,1,0:T(4,128)} all-to-all(f32[8,4,1792]{2,1,0:T(4,128)} %get-tuple-element.22), channel_id=1, replica_groups=mesh['zh'=2,'zq'=4,'y'=8,'core'=2,'rhs'=4] {'zh','zq'}, dimensions={0} | all-to-all | bytes 458752 | tf_op jit(solution)/shard_map/all_to_all | solution.py:289
  136.1 3.9 %shard_map.107 = f32[8,4,1024]{2,1,0:T(4,128)} custom-call(f32[8,4,1792]{2,1,0:T(4,128)} %all_to_all.20.got, f32[4,4,128]{2,1,0:T(4,128)} %reshape.30.noise, f32[128,12672]{1,0:T(8,128)} %all-gather.4.cloned.1.call-done.source), custom_call_target="tpu_custom_call" | custom-call | flops 2000000 | bytes 600000 | tf_op jit(solution)/shard_map/pallas_call | solution.py:46
  140.0 11.9 %all_to_all.21.got0 = f32[8,4,1024]{2,1,0:T(4,128)} all-to-all(f32[8,4,1024]{2,1,0:T(4,128)} %shard_map.107), channel_id=1, replica_groups=mesh['zh'=2,'zq'=4,'y'=8,'core'=2,'rhs'=4] {'zh','zq'}, dimensions={0} | all-to-all | bytes 262144 | tf_op jit(solution)/shard_map/all_to_all | solution.py:300
  151.9 10.7 %shard_map.108 = f32[4,1920]{1,0:T(4,128)} custom-call(s32[2]{0:T(128)} %pad_add_fusion.1.place, f32[8,4,1792]{2,1,0:T(4,128)} %all_to_all.20.got, f32[8,4,1024]{2,1,0:T(4,128)} %all_to_all.21.got0, f32[4,128]{1,0:T(4,128)} %get-tuple-element.23.g3, f32[128,12672]{1,0:T(8,128)} %all-gather.4.cloned.1.call-done.source), custom_call_target="tpu_custom_call" | custom-call | flops 12000000 | bytes 6500000 | tf_op jit(solution)/shard_map/pallas_call | solution.py:46
  162.7 19.9 %all-gather.1.x = f32[16,4,1920]{2,1,0:T(4,128)S(1)} all-gather(f32[1,4,1920]{2,1,0:T(4,128)} %bitcast.33), channel_id=2, replica_groups=mesh['zh'=2,'zq'=4,'y'=8,'core'=2,'rhs'=4] {'y','core'}, dimensions={0}, use_global_device_ids=true | all-gather | bytes 522240 | tf_op jit(solution)/shard_map/all_gather | solution.py:312
  182.5 5.5 %shard_map.109 = (f32[64,2048]{1,0:T(8,128)}, f32[32,64]{1,0:T(8,128)}) custom-call(s32[16,8]{1,0:T(8,128)S(1)} %copy.38.blocks, s32[4]{0:T(128)S(1)} %pad_add_fusion.at, f32[16,4,1920]{2,1,0:T(4,128)S(1)} %all-gather.1.x, f32[64,2048]{1,0:T(8,128)S(1)} %get-tuple-element.24.base, f32[16,64,128]{2,1,0:T(8,128)S(1)} %copy-done.7), custom_call_target="tpu_custom_call" | custom-call | flops 20000000 | bytes 2000000 | tf_op jit(solution)/shard_map/pallas_call | solution.py:46
  (25 shorter events, 0.3 us)
Async XLA Ops:
  9.0 29.6 %all-to-all-start = ((f32[16,8,1568]{2,1,0:T(8,128)}), f32[16,8,1568]{2,1,0:T(8,128)}, u32[]{:S(2)}, u32[]{:S(2)}) async-start(f32[16,8,1568]{2,1,0:T(8,128)} %broadcast_in_dim.12), calls=%async_computation | async-start | bytes 1703936 | tf_op jit(solution)/shard_map/all_to_all | solution.py:223
  19.5 91.3 %all-gather.4.cloned.1.call-start = ((), (), s32[]{:S(2)}) async-start(), calls=%async_computation.4 | async-start | bytes 6893568 | tf_op jit(solution)/shard_map/all_gather | solution.py:258
  21.4 1.2 copy-start
  22.6 1.0 copy-start.2
  23.7 1.0 copy-start.4
  24.7 0.7 copy-start.8
  34.9 33.9 %copy-start.1 = (f32[16,128,128]{2,1,0:T(8,128)S(1)}, f32[16,128,128]{2,1,0:T(8,128)}, u32[]{:S(2)}) copy-start(f32[16,128,128]{2,1,0:T(8,128)} %inverse.3) | copy-start | bytes 3145732
  34.9 33.9 %copy-start.3 = (f32[16,64,128]{2,1,0:T(8,128)S(1)}, f32[16,64,128]{2,1,0:T(8,128)}, u32[]{:S(2)}) copy-start(f32[16,64,128]{2,1,0:T(8,128)} %panel.3) | copy-start | bytes 1572868
  34.9 33.9 %copy-start.5 = (f32[64,2048]{1,0:T(8,128)S(1)}, f32[64,2048]{1,0:T(8,128)}, u32[]{:S(2)}) copy-start(f32[64,2048]{1,0:T(8,128)} %noise.1) | copy-start | bytes 1572868
  54.2 6.1 %collective-permute-start = (f32[8,4,2048]{2,1,0:T(4,128)S(1)}, f32[8,4,2048]{2,1,0:T(4,128)S(1)}, u32[]{:S(2)}, u32[]{:S(2)}) collective-permute-start(f32[8,4,2048]{2,1,0:T(4,128)S(1)} %dynamic-slice_bitcast_fusion), channel_id=1, source_target_pairs={{0,4},{4,0},{1,5},{5,1},{2,6},{6,2},{3,7},{7,3},{8,12},{12,8},{9,1... | collective-permute-start | bytes 786440 | tf_op jit(solution)/shard_map/ppermute | solution.py:264
  62.0 20.2 %all-to-all-start.1 = ((f32[8,4,2048]{2,1,0:T(4,128)}), f32[8,4,2048]{2,1,0:T(4,128)S(1)}, u32[]{:S(2)}, u32[]{:S(2)}) async-start(f32[8,4,2048]{2,1,0:T(4,128)} %bitcast_add_fusion), calls=%async_computation.1 | async-start | bytes 524288 | tf_op jit(solution)/shard_map/all_to_all | solution.py:265
  72.6 0.8 copy-start.6
  136.1 46.5 %copy-start.7 = (f32[16,64,128]{2,1,0:T(8,128)S(1)}, f32[16,64,128]{2,1,0:T(8,128)}, u32[]{:S(2)}) copy-start(f32[16,64,128]{2,1,0:T(8,128)} %copy-done.6) | copy-start | bytes 1572868
Sparse Core Ops, SparseCore 0:
  52.4 58.3 all-gather.3

commit v4 on v3

--- a/solution.py
+++ b/solution.py
@@ -58,6 +58,35 @@
 
 def f32(*shape):
     return jax.ShapeDtypeStruct(shape, jnp.float32)
+
+
+def copies_kernel(inverse, coupling, out):
+    for d in range(16):
+        out[d, :, :480] = inverse[...]
+        out[d, :, 480:] = coupling[...]
+
+
+def pack_kernel(place, quad, out):
+    def rows_of(plane):
+        parts = [quad[plane * 4 + x] for x in range(4)]
+        inv = jnp.concatenate([p[:, :480] for p in parts], axis=1)
+        cou = jnp.concatenate([p[:, 480:] for p in parts], axis=1)
+        return inv, cou
+
+    for q in range(4):
+        inv, cou = rows_of(q)
+        out[:, q * 1536 : q * 1536 + 512] = inv[:, 1024:1536]
+        out[:, q * 1536 + 512 : (q + 1) * 1536] = cou[:, :1024]
+    pair = place[0] // 2 * 2
+    for p in range(2):
+        inv, cou = rows_of(pair + p)
+        at = L2_AT + p * 1792
+        out[:, at : at + 256] = inv[:, 1536:1792]
+        out[:, at + 256 : at + 1792] = cou[:, 1024:2560]
+    inv, cou = rows_of(place[0])
+    out[:, L3_AT : L3_AT + 128] = inv[:, 1792:]
+    out[:, L3_AT + 128 : L0_AT] = cou[:, 2560:]
+    out[:, L0_AT:] = inv[:, :1024]
 
 
 def leaf_forward_kernel(blocks, at, shift, sep_t, sep_noise, inverse, panel, lf_out, pay_out, acc):
@@ -219,8 +248,8 @@
     place = jnp.stack([zq, zh]).astype(jnp.int32)
     at = jnp.stack([STARTS[k] + dev % (128 >> k) * SEP_DEV for k in range(LEVELS)]).astype(jnp.int32)
 
-    own = jnp.concatenate([sep_inverse, sep_coupling], axis=1)
-    quad = lax.all_to_all(jnp.broadcast_to(own, (16,) + own.shape), ("zq", "rhs"), 0, 0)
+    copies = call(copies_kernel, f32(16, 8, 1568), [sep_inverse, sep_coupling], nbytes=900_000)
+    quad = lax.all_to_all(copies, ("zq", "rhs"), 0, 0)
     first = lax.axis_index("core") == 0
     noise_slot = jnp.concatenate(
         [jnp.where(first, sep_noise, 0.0), jnp.where(first, 0.0, sep_noise), jnp.zeros((SAMPLES, 64), jnp.float32)],
@@ -244,17 +273,7 @@
         nbytes=3_000_000,
     )
     quad, pay = lax.optimization_barrier((quad, pay))
-    quad = jnp.transpose(quad.reshape(4, 4, 8, 1568), (0, 2, 1, 3))
-    inv = quad[..., :480].reshape(4, 8, 1920)
-    cou = quad[..., 480:].reshape(4, 8, 4352)
-    l1 = jnp.concatenate([inv[..., 1024:1536], cou[..., :1024]], axis=2)
-    l2 = jnp.concatenate([inv[..., 1536:1792], cou[..., 1024:2560]], axis=2)
-    l2 = lax.dynamic_slice_in_dim(l2, zq // 2 * 2, 2, 0)
-    l3 = jnp.concatenate([inv[..., 1792:], cou[..., 2560:]], axis=2)
-    l3 = lax.dynamic_slice_in_dim(l3, zq, 1, 0)
-    l0 = lax.dynamic_slice_in_dim(inv[..., :1024], zq, 1, 0)
-    flat = lambda m: jnp.transpose(m, (1, 0, 2)).reshape(8, -1)
-    packed = jnp.concatenate([flat(l1), flat(l2), flat(l3), flat(l0)], axis=1)
+    packed = call(pack_kernel, f32(8, PACK), [place, quad], smem=1, nbytes=1_500_000)
     path = lax.all_gather(packed, yc, axis=0, tiled=True)
 
     core = lax.axis_index("core")
@@ -282,7 +301,7 @@
         smem=1,
         hbm=1,
         scratch=[pltpu.VMEM((128, L0_AT), jnp.float32), pltpu.SemaphoreType.DMA((3,))],
-        vmem=56,
+        vmem=48,
         flops=12_000_000,
         nbytes=6_500_000,
     )
@@ -293,7 +312,7 @@
         [got, noise, path],
         hbm=1,
         scratch=[pltpu.VMEM((128, 1024), jnp.float32), pltpu.SemaphoreType.DMA],
-        vmem=56,
+        vmem=48,
         flops=2_000_000,
         nbytes=600_000,
     )
@@ -305,7 +324,7 @@
         smem=1,
         hbm=1,
         scratch=[pltpu.VMEM((128, L0_AT), jnp.float32), pltpu.SemaphoreType.DMA((3,))],
-        vmem=56,
+        vmem=48,
         flops=12_000_000,
         nbytes=6_500_000,
     )

time: 196 us -> 179 us (0.913)
  local copies, waits for them, and re-layouts: 23.1 us -> 10.5 us
  other arithmetic: 4.87 us -> 1.98 us
    slice x11 -> x0, local copies, waits for them, and re-layouts: 9.47 us -> none  [the longest x2 2.27 us: body(): cou = quad[..., 480:].reshape(4, 8, 4352)]
    reshape x2 -> x0, local copies, waits for them, and re-layouts: 3.2 us -> none  [the longest x1 2.26 us: body(): cou = quad[..., 480:].reshape(4, 8, 4352)]
    unnamed x20 -> x26, local copies, waits for them, and re-layouts: 6.41 us -> 8.8 us
    pallas_call x6 -> x8, Pallas kernels: 40.5 us -> 39.5 us  [call(): pl.pallas_call(kernel, out_shape=outs, in_specs=[pl.BlockSpec(memory_spac...]
  transfers between devices with their start and end apart: 4 -> 4, of which waited for: 4 -> 4; matrix products, arithmetic and copies ran while one was open for 4% -> 3% of each run, Pallas kernels for 7% -> 7%
where the time goes in v4:
time: 179 us; the launch traced here: 178 us
  blocking collectives  48.2 us (27%)
  waiting for transfers between devices  41.1 us (23%)
  Pallas kernels  39.5 us (22%)
  starting transfers between devices  22.2 us (12%)
  between operations  14.2 us (8%)
  local copies, waits for them, and re-layouts  10.5 us (6%)
  other arithmetic  1.98 us (1%)
    pallas_call x8, Pallas kernels, call(): pl.pallas_call(kernel, out_shape=outs, in_specs=[pl.BlockSpec(memory_spac...  39.5 us
    all_gather x1, waiting for transfers between devices, body(): path = lax.all_gather(packed, yc, axis=0, tiled=True)  28.6 us
    all_gather x1, blocking collectives, body(): gathered = lax.all_gather(x, yc, axis=0, tiled=False)  19.5 us
    all_to_all x1, blocking collectives, body(): got = lax.all_to_all(send, zz, 0, 0)  18.4 us
    all_to_all x1, starting transfers between devices, body(): quad = lax.all_to_all(copies, ('zq', 'rhs'), 0, 0)  10.4 us
    all_to_all x1, blocking collectives, body(): got0 = lax.all_to_all(top_send, zz, 0, 0)  10.3 us
    unnamed x26, local copies, waits for them, and re-layouts  8.8 us
    all_to_all x1, waiting for transfers between devices, body(): pay = lax.all_to_all(pay, 'y', 0, 0)  8.34 us
  transfers between devices with their start and end apart: 4, of which 4 were waited for; matrix products, arithmetic and copies ran while one was open for 3% of the time, Pallas kernels for 7%

profile of v4, /device:TPU:1, one launch (start us, length us, event | category | flops | bytes accessed | tf_op | source)
XLA Modules:
  0.0 177.7 jit_solution(188838025488881520)
XLA Ops:
  7.2 0.0 copy-start.1
  7.2 0.0 copy-start.3
  7.2 0.0 copy-start.9
  7.2 0.9 copy-done.9
  8.1 0.0 copy-start.10
  8.1 0.7 copy-done.10
  8.8 0.0 copy-start.5
  8.8 1.1 shard_map.104
  9.9 10.4 %all-to-all-start = ((f32[16,8,1568]{2,1,0:T(8,128)}), f32[16,8,1568]{2,1,0:T(8,128)S(1)}, u32[]{:S(2)}, u32[]{:S(2)}) async-start(f32[16,8,1568]{2,1,0:T(8,128)} %shard_map.104), calls=%async_computation | async-start | bytes 1703936 | tf_op jit(solution)/shard_map/all_to_all | solution.py:252
  20.3 0.0 all-gather.4.cloned.1.call-start
  20.4 0.8 copy.22
  21.2 0.8 copy.27.blocks
  22.0 0.1 pad.2.clone
  22.1 0.1 pad_add_fusion.at
  22.1 0.1 maximum_maximum_fusion.sep_noise
  22.2 1.2 copy-done
  23.5 1.0 copy-done.2
  24.5 1.0 copy-done.4
  25.5 0.7 copy-done.11
  26.3 9.4 %shard_map.105 = (f32[64,2048]{1,0:T(8,128)S(1)}, f32[64,2048]{1,0:T(8,128)S(1)}) custom-call(s32[16,8]{1,0:T(8,128)S(1)} %copy.27.blocks, s32[4]{0:T(128)S(1)} %pad_add_fusion.at, f32[64,2048]{1,0:T(8,128)S(1)} %copy-done.4, f32[32,64]{1,0:T(8,128)S(1)} %bitcast.17, f32[64,128]{1,0:T(8,128)S(1)} %maximum_maximum_fusion.sep_noise, ...), custom_call_target="tpu_custom_call" | custom-call | flops 50000000 | bytes 3000000 | tf_op jit(solution)/shard_map/pallas_call | solution.py:46
  35.7 0.8 copy-done.8
  36.5 0.1 pad_add_fusion.1.place
  36.6 2.9 %all-to-all-done.quad = f32[16,8,1568]{2,1,0:T(8,128)S(1)} async-done(((f32[16,8,1568]{2,1,0:T(8,128)}), f32[16,8,1568]{2,1,0:T(8,128)S(1)}, u32[]{:S(2)}, u32[]{:S(2)}) %all-to-all-start) | async-done | bytes 802848 | tf_op jit(solution)/shard_map/all_to_all | solution.py:252
  39.4 1.5 shard_map.107
  41.0 0.0 all-gather.4.cloned.1.call-update
  41.0 1.2 reshape.13
  42.2 4.9 %collective-permute-start = (f32[8,4,2048]{2,1,0:T(4,128)S(1)}, f32[8,4,2048]{2,1,0:T(4,128)}, u32[]{:S(2)}, u32[]{:S(2)}) collective-permute-start(f32[8,4,2048]{2,1,0:T(4,128)S(1)} %dynamic-slice_bitcast_fusion), channel_id=1, source_target_pairs={{0,4},{4,0},{1,5},{5,1},{2,6},{6,2},{3,7},{7,3},{8,12},{12,8},{9,1... | collective-permute-start | bytes 786440 | tf_op jit(solution)/shard_map/ppermute | solution.py:283
  47.1 1.3 collective-permute-done
  48.4 1.7 bitcast_add_fusion
  50.1 6.8 %all-to-all-start.1 = ((f32[8,4,2048]{2,1,0:T(4,128)}), f32[8,4,2048]{2,1,0:T(4,128)S(1)}, u32[]{:S(2)}, u32[]{:S(2)}) async-start(f32[8,4,2048]{2,1,0:T(4,128)} %bitcast_add_fusion), calls=%async_computation.1 | async-start | bytes 524288 | tf_op jit(solution)/shard_map/all_to_all | solution.py:284
  56.9 0.0 copy-done.1
  57.0 0.0 copy-done.3
  57.0 0.0 copy-done.5
  57.0 3.7 %shard_map.106 = (f32[64,2048]{1,0:T(8,128)S(1)}, f32[16,64,128]{2,1,0:T(8,128)S(1)}) custom-call(f32[64,2048]{1,0:T(8,128)S(1)} %get-tuple-element.17.lf, f32[64,2048]{1,0:T(8,128)S(1)} %copy-done.5, f32[16,128,128]{2,1,0:T(8,128)S(1)} %copy-done.1, f32[16,64,128]{2,1,0:T(8,128)S(1)} %copy-done.3), custom_call_target="tpu_custom_call" | custom-call | flops 70000000 | bytes 4000000 | tf_op jit(solution)/shard_map/pallas_call | solution.py:46
  60.7 0.8 copy-done.6
  61.5 8.3 %all-to-all-done.1 = f32[8,4,2048]{2,1,0:T(4,128)S(1)} async-done(((f32[8,4,2048]{2,1,0:T(4,128)}), f32[8,4,2048]{2,1,0:T(4,128)S(1)}, u32[]{:S(2)}, u32[]{:S(2)}) %all-to-all-start.1) | async-done | bytes 262176 | tf_op jit(solution)/shard_map/all_to_all | solution.py:284
  69.9 0.1 reshape.14
  70.0 0.1 copy.26
  70.1 0.2 reshape.15.noise
  70.3 28.6 %all-gather.4.cloned.1.call-done.source = f32[128,12672]{1,0:T(8,128)} async-done(((f32[8,12672]{1,0:T(8,128)}), f32[128,12672]{1,0:T(8,128)}) %all-gather.4.cloned.1.call-update) | async-done | bytes 6488080 | tf_op jit(solution)/shard_map/all_gather | solution.py:277
  98.9 6.2 %shard_map.108 = (f32[8,4,1792]{2,1,0:T(4,128)S(1)}, f32[4,128]{1,0:T(4,128)S(1)}) custom-call(s32[2]{0:T(128)S(1)} %pad_add_fusion.1.place, f32[4,1920]{1,0:T(4,128)S(1)} %slice_reduce_fusion.v, f32[4,4,128]{2,1,0:T(4,128)S(1)} %reshape.15.noise, f32[128,12672]{1,0:T(8,128)} %all-gather.4.cloned.1.call-done.source), custom_call_target="tpu_custom_call" | custom-call | flops 12000000 | bytes 6500000 | tf_op jit(solution)/shard_map/pallas_call | solution.py:46
  105.1 18.4 %all_to_all.20.got = f32[8,4,1792]{2,1,0:T(4,128)S(1)} all-to-all(f32[8,4,1792]{2,1,0:T(4,128)S(1)} %get-tuple-element.22), channel_id=1, replica_groups=mesh['zh'=2,'zq'=4,'y'=8,'core'=2,'rhs'=4] {'zh','zq'}, dimensions={0} | all-to-all | bytes 458752 | tf_op jit(solution)/shard_map/all_to_all | solution.py:308
  123.5 2.3 %shard_map.109 = f32[8,4,1024]{2,1,0:T(4,128)S(1)} custom-call(f32[8,4,1792]{2,1,0:T(4,128)S(1)} %all_to_all.20.got, f32[4,4,128]{2,1,0:T(4,128)S(1)} %reshape.15.noise, f32[128,12672]{1,0:T(8,128)} %all-gather.4.cloned.1.call-done.source), custom_call_target="tpu_custom_call" | custom-call | flops 2000000 | bytes 600000 | tf_op jit(solution)/shard_map/pallas_call | solution.py:46
  125.8 10.3 %all_to_all.21.got0 = f32[8,4,1024]{2,1,0:T(4,128)S(1)} all-to-all(f32[8,4,1024]{2,1,0:T(4,128)S(1)} %shard_map.109), channel_id=1, replica_groups=mesh['zh'=2,'zq'=4,'y'=8,'core'=2,'rhs'=4] {'zh','zq'}, dimensions={0} | all-to-all | bytes 262144 | tf_op jit(solution)/shard_map/all_to_all | solution.py:319
  136.2 9.6 %shard_map.110 = f32[4,1920]{1,0:T(4,128)S(1)} custom-call(s32[2]{0:T(128)S(1)} %pad_add_fusion.1.place, f32[8,4,1792]{2,1,0:T(4,128)S(1)} %all_to_all.20.got, f32[8,4,1024]{2,1,0:T(4,128)S(1)} %all_to_all.21.got0, f32[4,128]{1,0:T(4,128)S(1)} %get-tuple-element.23.g3, f32[128,12672]{1,0:T(8,128)} %all-gather.4.cloned.1.call-done.source), custom_call_target="tpu_custom_call" | custom-call | flops 12000000 | bytes 6500000 | tf_op jit(solution)/shard_map/pallas_call | solution.py:46
  145.8 19.5 %all-gather.1.x = f32[16,4,1920]{2,1,0:T(4,128)S(1)} all-gather(f32[1,4,1920]{2,1,0:T(4,128)S(1)} %bitcast.16), channel_id=2, replica_groups=mesh['zh'=2,'zq'=4,'y'=8,'core'=2,'rhs'=4] {'y','core'}, dimensions={0}, use_global_device_ids=true | all-gather | bytes 522240 | tf_op jit(solution)/shard_map/all_gather | solution.py:331
  165.3 0.0 copy-done.7
  165.3 5.5 %shard_map.111 = (f32[64,2048]{1,0:T(8,128)}, f32[32,64]{1,0:T(8,128)}) custom-call(s32[16,8]{1,0:T(8,128)S(1)} %copy.27.blocks, s32[4]{0:T(128)S(1)} %pad_add_fusion.at, f32[16,4,1920]{2,1,0:T(4,128)S(1)} %all-gather.1.x, f32[64,2048]{1,0:T(8,128)S(1)} %get-tuple-element.24.base, f32[16,64,128]{2,1,0:T(8,128)S(1)} %copy-done.7), custom_call_target="tpu_custom_call" | custom-call | flops 20000000 | bytes 2000000 | tf_op jit(solution)/shard_map/pallas_call | solution.py:46
  (13 shorter events, 0.1 us)
Async XLA Ops:
  7.2 49.8 %copy-start.1 = (f32[16,128,128]{2,1,0:T(8,128)S(1)}, f32[16,128,128]{2,1,0:T(8,128)}, u32[]{:S(2)}) copy-start(f32[16,128,128]{2,1,0:T(8,128)} %inverse.5) | copy-start | bytes 3145732
  7.2 49.8 %copy-start.3 = (f32[16,64,128]{2,1,0:T(8,128)S(1)}, f32[16,64,128]{2,1,0:T(8,128)}, u32[]{:S(2)}) copy-start(f32[16,64,128]{2,1,0:T(8,128)} %panel.3) | copy-start | bytes 1572868
  7.2 0.9 copy-start.9
  8.1 0.7 copy-start.10
  8.8 48.2 %copy-start.5 = (f32[64,2048]{1,0:T(8,128)S(1)}, f32[64,2048]{1,0:T(8,128)}, u32[]{:S(2)}) copy-start(f32[64,2048]{1,0:T(8,128)} %noise.1) | copy-start | bytes 1572868
  9.9 29.5 %all-to-all-start = ((f32[16,8,1568]{2,1,0:T(8,128)}), f32[16,8,1568]{2,1,0:T(8,128)S(1)}, u32[]{:S(2)}, u32[]{:S(2)}) async-start(f32[16,8,1568]{2,1,0:T(8,128)} %shard_map.104), calls=%async_computation | async-start | bytes 1703936 | tf_op jit(solution)/shard_map/all_to_all | solution.py:252
  20.3 78.6 %all-gather.4.cloned.1.call-start = ((), (), s32[]{:S(2)}) async-start(), calls=%async_computation.4 | async-start | bytes 6893568 | tf_op jit(solution)/shard_map/all_gather | solution.py:277
  22.2 1.2 copy-start
  23.5 1.0 copy-start.2
  24.5 1.0 copy-start.4
  25.5 0.7 copy-start.11
  35.7 0.8 copy-start.8
  42.2 6.2 %collective-permute-start = (f32[8,4,2048]{2,1,0:T(4,128)S(1)}, f32[8,4,2048]{2,1,0:T(4,128)}, u32[]{:S(2)}, u32[]{:S(2)}) collective-permute-start(f32[8,4,2048]{2,1,0:T(4,128)S(1)} %dynamic-slice_bitcast_fusion), channel_id=1, source_target_pairs={{0,4},{4,0},{1,5},{5,1},{2,6},{6,2},{3,7},{7,3},{8,12},{12,8},{9,1... | collective-permute-start | bytes 786440 | tf_op jit(solution)/shard_map/ppermute | solution.py:283
  50.1 19.7 %all-to-all-start.1 = ((f32[8,4,2048]{2,1,0:T(4,128)}), f32[8,4,2048]{2,1,0:T(4,128)S(1)}, u32[]{:S(2)}, u32[]{:S(2)}) async-start(f32[8,4,2048]{2,1,0:T(4,128)} %bitcast_add_fusion), calls=%async_computation.1 | async-start | bytes 524288 | tf_op jit(solution)/shard_map/all_to_all | solution.py:284
  60.7 0.8 copy-start.6
  123.5 41.8 %copy-start.7 = (f32[16,64,128]{2,1,0:T(8,128)S(1)}, f32[16,64,128]{2,1,0:T(8,128)}, u32[]{:S(2)}) copy-start(f32[16,64,128]{2,1,0:T(8,128)} %copy-done.6) | copy-start | bytes 1572868
Sparse Core Ops, SparseCore 0:
  41.1 57.7 all-gather.3

commit v5 on v4

--- a/solution.py
+++ b/solution.py
@@ -25,16 +25,28 @@
 MIB = 1024 * 1024
 
 
+def halves(a):
+    high = a.astype(jnp.bfloat16)
+    return high, (a - high.astype(jnp.float32)).astype(jnp.bfloat16)
+
+
+def split_dot(a, b, dims):
+    ah, al = halves(a)
+    bh, bl = halves(b)
+    dot = lambda p, q: lax.dot_general(p, q, (dims, ((), ())), preferred_element_type=jnp.float32)
+    return dot(ah, bh) + (dot(ah, bl) + dot(al, bh))
+
+
 def nn(a, b):
-    return lax.dot_general(a, b, (((1,), (0,)), ((), ())), precision=exact, preferred_element_type=jnp.float32)
+    return split_dot(a, b, ((1,), (0,)))
 
 
 def nt(a, b):
-    return lax.dot_general(a, b, (((1,), (1,)), ((), ())), precision=exact, preferred_element_type=jnp.float32)
+    return split_dot(a, b, ((1,), (1,)))
 
 
 def tn(a, b):
-    return lax.dot_general(a, b, (((0,), (0,)), ((), ())), precision=exact, preferred_element_type=jnp.float32)
+    return split_dot(a, b, ((0,), (0,)))
 
 
 def vspec(n):
@@ -164,25 +176,49 @@
             send_out[d, :, 1536 + p * 128 : 1664 + p * 128] = two[p]
 
 
-def top_kernel(got, noise, source, send_out, path, sem):
-    copy = pltpu.make_async_copy(source.at[:, L0_AT:], path, sem)
-    copy.start()
+def top_kernel(got, noise, path, send_out):
     r0 = got[0, :, :1024]
     for d in range(1, 8):
         r0 = r0 + got[d, :, :1024]
-    copy.wait()
     y0 = nt(r0, path[...]) + noise[0]
     x0 = nn(y0, path[...])
     for d in range(8):
         send_out[d] = x0
 
 
-def backward_kernel(place, got, got0, g3, source, x_out, path, sems):
+def operator_kernel(source, high_out, low_out, path, found, sems):
     copies = fetch(source, path, sems, ("l1", "l2", "l3"))
-    x0 = got0[0]
-    for d in range(1, 8):
-        x0 = x0 + got0[d]
-    x_out[:, :1024] = x0
+
+    def keep(lo, hi):
+        high, low = halves(found[lo:hi, :])
+        high_out[lo:hi, :] = high
+        low_out[lo:hi, :] = low
+
+    copies["l1"].wait()
+    total = None
+    for q in range(4):
+        at = q * 1536
+        term = tn(path[:, at : at + 512], path[:, at + 512 : at + 1536])
+        total = term if total is None else total + term
+    found[:512, :] = -total
+    keep(0, 512)
+    copies["l2"].wait()
+    total = None
+    for p in range(2):
+        at = L2_AT + p * 1792
+        y = path[:, at + 256 : at + 1280] + nn(path[:, at + 1280 : at + 1792], found[:512, :])
+        term = tn(path[:, at : at + 256], y)
+        total = term if total is None else total + term
+    found[512:768, :] = -total
+    keep(512, 768)
+    copies["l3"].wait()
+    y = path[:, L3_AT + 128 : L3_AT + 1152] + nn(path[:, L3_AT + 1152 : L0_AT], found[:768, :])
+    found[768:, :] = -tn(path[:, L3_AT : L3_AT + 128], y)
+    keep(768, 896)
+
+
+def rest_kernel(place, got, g3, source, x_out, path, sems):
+    copies = fetch(source, path, sems, ("l1", "l2", "l3"))
     z = place[0] + 4 * place[1]
     g1 = jnp.zeros((GROUP, 512), jnp.float32)
     g2 = jnp.zeros((GROUP, 256), jnp.float32)
@@ -192,20 +228,28 @@
     copies["l1"].wait()
     x1 = jnp.zeros((GROUP, 512), jnp.float32)
     for q in range(4):
-        at = q * 1536
-        y = g1[:, q * 128 : (q + 1) * 128] - nt(x0, path[:, at + 512 : at + 1536])
-        x1 = x1 + nn(y, path[:, at : at + 512])
-    x_out[:, 1024:1536] = x1
+        x1 = x1 + nn(g1[:, q * 128 : (q + 1) * 128], path[:, q * 1536 : q * 1536 + 512])
+    x_out[:, :512] = x1
     copies["l2"].wait()
     x2 = jnp.zeros((GROUP, 256), jnp.float32)
     for p in range(2):
         at = L2_AT + p * 1792
-        y = g2[:, p * 128 : (p + 1) * 128] - nt(x_out[:, :1536], path[:, at + 256 : at + 1792])
+        y = g2[:, p * 128 : (p + 1) * 128] - nt(x_out[:, :512], path[:, at + 1280 : at + 1792])
         x2 = x2 + nn(y, path[:, at : at + 256])
-    x_out[:, 1536:1792] = x2
+    x_out[:, 512:768] = x2
     copies["l3"].wait()
-    y = g3[...] - nt(x_out[:, :1792], path[:, L3_AT + 128 : L0_AT])
-    x_out[:, 1792:] = nn(y, path[:, L3_AT : L3_AT + 128])
+    y = g3[...] - nt(x_out[:, :768], path[:, L3_AT + 1152 : L0_AT])
+    x_out[:, 768:] = nn(y, path[:, L3_AT : L3_AT + 128])
+
+
+def backward_kernel(got0, rest, high, low, x_out):
+    x0 = got0[0]
+    for d in range(1, 8):
+        x0 = x0 + got0[d]
+    x_out[:, :1024] = x0
+    xh, xl = halves(x0)
+    dot = lambda p, q: lax.dot_general(p, q[...], (((1,), (1,)), ((), ())), preferred_element_type=jnp.float32)
+    x_out[:, 1024:] = rest[...] + (dot(xh, high) + (dot(xh, low) + dot(xl, high)))
 
 
 def leaf_backward_kernel(blocks, at, x, base, w, leaf_out, sep_out, rows_s, cols_s):
@@ -226,7 +270,11 @@
         leaf_out[:, cols] = base[:, cols] - tn(picked, w[n])
         return carry
 
-    lax.fori_loop(0, NODES, step, 0)
+    lax.fori_loop(0, NODES, step, 0, unroll=4)
+
+
+def path_scratch(*more):
+    return [pltpu.VMEM((128, L0_AT), jnp.float32), *more, pltpu.SemaphoreType.DMA((3,))]
 
 
 def body(
@@ -300,33 +348,47 @@
         [place, v, noise, path],
         smem=1,
         hbm=1,
-        scratch=[pltpu.VMEM((128, L0_AT), jnp.float32), pltpu.SemaphoreType.DMA((3,))],
+        scratch=path_scratch(),
         vmem=48,
         flops=12_000_000,
         nbytes=6_500_000,
     )
+    path, send = lax.optimization_barrier((path, send))
     got = lax.all_to_all(send, zz, 0, 0)
+    high, low = call(
+        operator_kernel,
+        [jax.ShapeDtypeStruct((896, 1024), jnp.bfloat16)] * 2,
+        [path],
+        hbm=1,
+        scratch=path_scratch(pltpu.VMEM((896, 1024), jnp.float32)),
+        vmem=48,
+        flops=3_500_000_000,
+        nbytes=10_000_000,
+    )
+    top_rows = path[:, L0_AT:]
+    got, high, low, top_rows = lax.optimization_barrier((got, high, low, top_rows))
     top_send = call(
-        top_kernel,
-        f32(8, GROUP, 1024),
-        [got, noise, path],
+        top_kernel, f32(8, GROUP, 1024), [got, noise, top_rows], flops=2_000_000, nbytes=600_000, vmem=8
+    )
+    got0 = lax.all_to_all(top_send, zz, 0, 0)
+    rest = call(
+        rest_kernel,
+        f32(GROUP, 896),
+        [place, got, g3, path],
+        smem=1,
         hbm=1,
-        scratch=[pltpu.VMEM((128, 1024), jnp.float32), pltpu.SemaphoreType.DMA],
-        vmem=48,
-        flops=2_000_000,
-        nbytes=600_000,
-    )
-    got0 = lax.all_to_all(top_send, zz, 0, 0)
+        scratch=path_scratch(),
+        vmem=20,
+        flops=300_000_000,
+        nbytes=6_500_000,
+    )
     x = call(
         backward_kernel,
         f32(GROUP, ANC),
-        [place, got, got0, g3, path],
-        smem=1,
-        hbm=1,
-        scratch=[pltpu.VMEM((128, L0_AT), jnp.float32), pltpu.SemaphoreType.DMA((3,))],
-        vmem=48,
-        flops=12_000_000,
-        nbytes=6_500_000,
+        [got0, rest, high, low],
+        flops=20_000_000,
+        nbytes=4_000_000,
+        vmem=16,
     )
     gathered = lax.all_gather(x, yc, axis=0, tiled=False)
 

time: 179 us -> 172 us (0.961)
  blocking collectives: 48.2 us -> 19.3 us
  starting transfers between devices: 22.2 us -> 36.4 us
  waiting for transfers between devices: 41.1 us -> 51.7 us
  Pallas kernels: 39.5 us -> 34.6 us
  local copies, waits for them, and re-layouts: 10.5 us -> 12.6 us
    all_to_all x2 -> x0, blocking collectives: 28.7 us -> none  [the longest x1 18.4 us: body(): got = lax.all_to_all(send, zz, 0, 0)]
    all_to_all x0 -> x2, starting transfers between devices: none -> 14.3 us  [the longest x1 7.62 us: body(): got = lax.all_to_all(send, zz, 0, 0)]
    all_to_all x1, waiting for transfers between devices: 2.87 us -> 10.7 us  [body(): quad = lax.all_to_all(copies, ('zq', 'rhs'), 0, 0)]
    pallas_call x8 -> x10, Pallas kernels: 39.5 us -> 34.6 us  [call(): pl.pallas_call(kernel, out_shape=outs, in_specs=[pl.BlockSpec(memory_spac...]
    all_to_all x0 -> x2, waiting for transfers between devices: none -> 2.26 us  [the longest x1 2.25 us: body(): got0 = lax.all_to_all(top_send, zz, 0, 0)]
    unnamed x26 -> x38, local copies, waits for them, and re-layouts: 8.8 us -> 9.15 us
  transfers between devices with their start and end apart: 4 -> 6, of which waited for: 4 -> 5; matrix products, arithmetic and copies ran while one was open for 3% -> 3% of each run, Pallas kernels for 7% -> 12%
where the time goes in v5:
time: 172 us; the launch traced here: 171 us
  waiting for transfers between devices  51.7 us (30%)
  starting transfers between devices  36.4 us (21%)
  Pallas kernels  34.6 us (20%)
  blocking collectives  19.3 us (11%)
  between operations  14.3 us (8%)
  local copies, waits for them, and re-layouts  12.6 us (7%)
  other arithmetic  1.99 us (1%)
    pallas_call x10, Pallas kernels, call(): pl.pallas_call(kernel, out_shape=outs, in_specs=[pl.BlockSpec(memory_spac...  34.6 us
    all_gather x1, waiting for transfers between devices, body(): path = lax.all_gather(packed, yc, axis=0, tiled=True)  28 us
    all_gather x1, blocking collectives, body(): gathered = lax.all_gather(x, yc, axis=0, tiled=False)  19.3 us
    all_to_all x1, waiting for transfers between devices, body(): quad = lax.all_to_all(copies, ('zq', 'rhs'), 0, 0)  10.7 us
    all_to_all x1, starting transfers between devices, body(): quad = lax.all_to_all(copies, ('zq', 'rhs'), 0, 0)  10.4 us
    all_to_all x1, waiting for transfers between devices, body(): pay = lax.all_to_all(pay, 'y', 0, 0)  9.61 us
    unnamed x38, local copies, waits for them, and re-layouts  9.15 us
    all_to_all x1, starting transfers between devices, body(): got = lax.all_to_all(send, zz, 0, 0)  7.62 us
  transfers between devices with their start and end apart: 6, of which 5 were waited for; matrix products, arithmetic and copies ran while one was open for 3% of the time, Pallas kernels for 12%

profile of v5, /device:TPU:1, one launch (start us, length us, event | category | flops | bytes accessed | tf_op | source)
XLA Modules:
  0.0 171.0 jit_solution(9405723778296662012)
XLA Ops:
  7.2 0.0 copy-start.2
  7.2 0.0 copy-start.1
  7.2 0.9 copy-done.13
  8.1 0.7 copy-done.14
  8.8 1.1 shard_map.104
  10.0 10.4 %all-to-all-start = ((f32[16,8,1568]{2,1,0:T(8,128)}), f32[16,8,1568]{2,1,0:T(8,128)S(1)}, u32[]{:S(2)}, u32[]{:S(2)}) async-start(f32[16,8,1568]{2,1,0:T(8,128)} %shard_map.104), calls=%async_computation | async-start | bytes 1703936 | tf_op jit(solution)/shard_map/all_to_all | solution.py:300
  20.3 0.0 all-gather.4.cloned.1.call-start
  20.5 0.1 copy.27.blocks
  20.5 0.1 copy.22
  20.6 0.1 pad.2.clone
  20.7 0.1 pad_add_fusion.at
  20.8 0.1 maximum_maximum_fusion.sep_noise
  20.9 7.0 %shard_map.105 = (f32[64,2048]{1,0:T(8,128)S(1)}, f32[64,2048]{1,0:T(8,128)S(1)}) custom-call(s32[16,8]{1,0:T(8,128)S(1)} %copy.27.blocks, s32[4]{0:T(128)S(1)} %pad_add_fusion.at, f32[64,2048]{1,0:T(8,128)S(1)} %copy-done.5, f32[32,64]{1,0:T(8,128)S(1)} %bitcast.17, f32[64,128]{1,0:T(8,128)S(1)} %maximum_maximum_fusion.sep_noise, ...), custom_call_target="tpu_custom_call" | custom-call | flops 50000000 | bytes 3000000 | tf_op jit(solution)/shard_map/pallas_call | solution.py:58
  27.9 0.8 copy-done.11
  28.7 0.1 pad_add_fusion.1.place
  28.8 10.7 %all-to-all-done.quad = f32[16,8,1568]{2,1,0:T(8,128)S(1)} async-done(((f32[16,8,1568]{2,1,0:T(8,128)}), f32[16,8,1568]{2,1,0:T(8,128)S(1)}, u32[]{:S(2)}, u32[]{:S(2)}) %all-to-all-start) | async-done | bytes 802848 | tf_op jit(solution)/shard_map/all_to_all | solution.py:300
  39.5 1.5 shard_map.106
  41.0 0.0 all-gather.4.cloned.1.call-update
  41.0 0.9 reshape.13
  42.0 1.0 dynamic-slice_bitcast_fusion
  42.9 4.9 %collective-permute-start = (f32[8,4,2048]{2,1,0:T(4,128)S(1)}, f32[8,4,2048]{2,1,0:T(4,128)S(1)}, u32[]{:S(2)}, u32[]{:S(2)}) collective-permute-start(f32[8,4,2048]{2,1,0:T(4,128)S(1)} %dynamic-slice_bitcast_fusion), channel_id=1, source_target_pairs={{0,4},{4,0},{1,5},{5,1},{2,6},{6,2},{3,7},{7,3},{8,12},{12,8},{9,1... | collective-permute-start | bytes 786440 | tf_op jit(solution)/shard_map/ppermute | solution.py:331
  47.9 1.1 collective-permute-done
  49.0 1.7 %bitcast_add_fusion = f32[8,4,2048]{2,1,0:T(4,128)} fusion(f32[8,4,2048]{2,1,0:T(4,128)S(1)} %collective-permute-done, f32[8,2,4,2048]{3,2,1,0:T(4,128)} %reshape.13, s32[]{:T(128)S(6)} %select_n.47), kind=kLoop, calls=%fused_computation | loop fusion | flops 65536 | bytes 786436 | tf_op jit(solution)/shard_map/add | solution.py:331
  50.7 6.8 %all-to-all-start.1 = ((f32[8,4,2048]{2,1,0:T(4,128)}), f32[8,4,2048]{2,1,0:T(4,128)S(1)}, u32[]{:S(2)}, u32[]{:S(2)}) async-start(f32[8,4,2048]{2,1,0:T(4,128)} %bitcast_add_fusion), calls=%async_computation.1 | async-start | bytes 524288 | tf_op jit(solution)/shard_map/all_to_all | solution.py:332
  57.5 3.0 %shard_map.107 = (f32[64,2048]{1,0:T(8,128)S(1)}, f32[16,64,128]{2,1,0:T(8,128)S(1)}) custom-call(f32[64,2048]{1,0:T(8,128)S(1)} %get-tuple-element.26.lf, f32[64,2048]{1,0:T(8,128)S(1)} %copy-done.6, f32[16,128,128]{2,1,0:T(8,128)S(1)} %copy-done.1, f32[16,64,128]{2,1,0:T(8,128)S(1)} %copy-done.2), custom_call_target="tpu_custom_call" | custom-call | flops 70000000 | bytes 4000000 | tf_op jit(solution)/shard_map/pallas_call | solution.py:58
  60.5 0.9 copy-done.9
  61.4 9.6 %all-to-all-done.1 = f32[8,4,2048]{2,1,0:T(4,128)S(1)} async-done(((f32[8,4,2048]{2,1,0:T(4,128)}), f32[8,4,2048]{2,1,0:T(4,128)S(1)}, u32[]{:S(2)}, u32[]{:S(2)}) %all-to-all-start.1) | async-done | bytes 262176 | tf_op jit(solution)/shard_map/all_to_all | solution.py:332
  71.0 0.1 reshape.14
  71.2 0.1 copy.26
  71.3 0.2 reshape.15.noise
  71.5 28.0 %all-gather.4.cloned.1.call-done.source = f32[128,12672]{1,0:T(8,128)} async-done(((f32[8,12672]{1,0:T(8,128)}), f32[128,12672]{1,0:T(8,128)}) %all-gather.4.cloned.1.call-update) | async-done | bytes 6488080 | tf_op jit(solution)/shard_map/all_gather | solution.py:325
  99.5 5.3 %shard_map.108 = (f32[8,4,1792]{2,1,0:T(4,128)}, f32[4,128]{1,0:T(4,128)S(1)}) custom-call(s32[2]{0:T(128)S(1)} %pad_add_fusion.1.place, f32[4,1920]{1,0:T(4,128)S(1)} %slice_reduce_fusion.v, f32[4,4,128]{2,1,0:T(4,128)S(1)} %reshape.15.noise, f32[128,12672]{1,0:T(8,128)} %all-gather.4.cloned.1.call-done.source), custom_call_target="tpu_custom_call" | custom-call | flops 12000000 | bytes 6500000 | tf_op jit(solution)/shard_map/pallas_call | solution.py:58
  104.8 7.6 %all-to-all-start.2 = ((f32[8,4,1792]{2,1,0:T(4,128)}), f32[8,4,1792]{2,1,0:T(4,128)S(1)}, u32[]{:S(2)}, u32[]{:S(2)}) async-start(f32[8,4,1792]{2,1,0:T(4,128)} %get-tuple-element.31), calls=%async_computation.2 | async-start | bytes 458752 | tf_op jit(solution)/shard_map/all_to_all | solution.py:357
  112.4 1.1 slice.11.path
  113.5 8.5 %shard_map.109 = (bf16[896,1024]{1,0:T(8,128)(2,1)S(1)}, bf16[896,1024]{1,0:T(8,128)(2,1)S(1)}) custom-call(f32[128,12672]{1,0:T(8,128)} %all-gather.4.cloned.1.call-done.source), custom_call_target="tpu_custom_call" | custom-call | flops 3500000000 | bytes 10000000 | tf_op jit(solution)/shard_map/pallas_call | solution.py:58
  122.0 0.0 copy-start.3
  122.0 1.3 copy-done.3
  123.4 0.0 all-to-all-done.2.got
  123.4 1.2 shard_map.110
  124.5 6.6 %all-to-all-start.3 = ((f32[8,4,1024]{2,1,0:T(4,128)}), f32[8,4,1024]{2,1,0:T(4,128)S(1)}, u32[]{:S(2)}, u32[]{:S(2)}) async-start(f32[8,4,1024]{2,1,0:T(4,128)} %shard_map.110), calls=%async_computation.3 | async-start | bytes 262144 | tf_op jit(solution)/shard_map/all_to_all | solution.py:373
  131.2 2.8 %copy-done = f32[128,12672]{1,0:T(8,128)S(1)} copy-done((f32[128,12672]{1,0:T(8,128)S(1)}, f32[128,12672]{1,0:T(8,128)}, u32[]{:S(2)}) %copy-start) | copy-done | bytes 6488088
  134.0 2.7 %shard_map.111.rest = f32[4,896]{1,0:T(4,128)S(1)} custom-call(s32[2]{0:T(128)S(1)} %pad_add_fusion.1.place, f32[8,4,1792]{2,1,0:T(4,128)S(1)} %all-to-all-done.2.got, f32[4,128]{1,0:T(4,128)S(1)} %get-tuple-element.37.g3, f32[128,12672]{1,0:T(8,128)S(1)} %copy-done), custom_call_target="tpu_custom_call" | custom-call | flops 300000000 | bytes 6500000 | tf_op jit(solution)/shard_map/pallas_call | solution.py:58
  136.7 2.3 %all-to-all-done.3.got0 = f32[8,4,1024]{2,1,0:T(4,128)S(1)} async-done(((f32[8,4,1024]{2,1,0:T(4,128)}), f32[8,4,1024]{2,1,0:T(4,128)S(1)}, u32[]{:S(2)}, u32[]{:S(2)}) %all-to-all-start.3) | async-done | bytes 131104 | tf_op jit(solution)/shard_map/all_to_all | solution.py:373
  138.9 1.5 copy-done.4
  140.4 1.5 shard_map.112
  142.0 19.3 %all-gather.1.x = f32[16,4,1920]{2,1,0:T(4,128)S(1)} all-gather(f32[1,4,1920]{2,1,0:T(4,128)S(1)} %bitcast.16), channel_id=2, replica_groups=mesh['zh'=2,'zq'=4,'y'=8,'core'=2,'rhs'=4] {'y','core'}, dimensions={0}, use_global_device_ids=true | all-gather | bytes 522240 | tf_op jit(solution)/shard_map/all_gather | solution.py:393
  161.3 0.0 copy-done.8
  161.3 2.9 %shard_map.113 = (f32[64,2048]{1,0:T(8,128)}, f32[32,64]{1,0:T(8,128)}) custom-call(s32[16,8]{1,0:T(8,128)S(1)} %copy.27.blocks, s32[4]{0:T(128)S(1)} %pad_add_fusion.at, f32[16,4,1920]{2,1,0:T(4,128)S(1)} %all-gather.1.x, f32[64,2048]{1,0:T(8,128)S(1)} %copy-done.8, f32[16,64,128]{2,1,0:T(8,128)S(1)} %copy-done.10), custom_call_target="tpu_custom_call" | custom-call | flops 20000000 | bytes 2000000 | tf_op jit(solution)/shard_map/pallas_call | solution.py:58
  (30 shorter events, 0.1 us)
Async XLA Ops:
  7.2 13.7 %copy-start.2 = (f32[16,64,128]{2,1,0:T(8,128)S(1)}, f32[16,64,128]{2,1,0:T(8,128)}, u32[]{:S(2)}) copy-start(f32[16,64,128]{2,1,0:T(8,128)} %panel.3) | copy-start | bytes 1572868
  7.2 13.7 %copy-start.1 = (f32[16,128,128]{2,1,0:T(8,128)S(1)}, f32[16,128,128]{2,1,0:T(8,128)}, u32[]{:S(2)}) copy-start(f32[16,128,128]{2,1,0:T(8,128)} %inverse.5) | copy-start | bytes 3145732
  7.2 13.7 %copy-start.5 = (f32[64,2048]{1,0:T(8,128)S(1)}, f32[64,2048]{1,0:T(8,128)}, u32[]{:S(2)}) copy-start(f32[64,2048]{1,0:T(8,128)} %shift.1) | copy-start | bytes 1572868
  7.2 0.9 copy-start.13
  8.1 0.7 copy-start.14
  8.8 11.6 %copy-start.17 = (s32[16,8]{0,1:T(8,128)S(1)}, s32[16,8]{0,1:T(8,128)}, u32[]{:S(2)}) copy-start(s32[16,8]{0,1:T(8,128)} %param.15) | copy-start | bytes 1540
  8.8 11.7 %copy-start.16 = (f32[64,32]{0,1:T(8,128)S(1)}, f32[64,32]{0,1:T(8,128)}, u32[]{:S(2)}) copy-start(f32[64,32]{0,1:T(8,128)} %param.12) | copy-start | bytes 24580
  8.8 12.1 %copy-start.15 = (f32[64,32]{0,1:T(8,128)S(1)}, f32[64,32]{0,1:T(8,128)}, u32[]{:S(2)}) copy-start(f32[64,32]{0,1:T(8,128)} %param.10) | copy-start | bytes 24580
  10.0 29.5 %all-to-all-start = ((f32[16,8,1568]{2,1,0:T(8,128)}), f32[16,8,1568]{2,1,0:T(8,128)S(1)}, u32[]{:S(2)}, u32[]{:S(2)}) async-start(f32[16,8,1568]{2,1,0:T(8,128)} %shard_map.104), calls=%async_computation | async-start | bytes 1703936 | tf_op jit(solution)/shard_map/all_to_all | solution.py:300
  20.3 79.2 %all-gather.4.cloned.1.call-start = ((), (), s32[]{:S(2)}) async-start(), calls=%async_computation.4 | async-start | bytes 6893568 | tf_op jit(solution)/shard_map/all_gather | solution.py:325
  27.9 0.8 copy-start.11
  28.7 12.3 %copy-start.12 = (f32[64,2048]{1,0:T(8,128)S(1)}, f32[64,2048]{1,0:T(8,128)}, u32[]{:S(2)}) copy-start(f32[64,2048]{1,0:T(8,128)} %copy-done.11) | copy-start | bytes 1572868
  41.0 16.6 %copy-start.6 = (f32[64,2048]{1,0:T(8,128)S(1)}, f32[64,2048]{1,0:T(8,128)}, u32[]{:S(2)}) copy-start(f32[64,2048]{1,0:T(8,128)} %noise.1) | copy-start | bytes 1572868
  42.9 6.1 %collective-permute-start = (f32[8,4,2048]{2,1,0:T(4,128)S(1)}, f32[8,4,2048]{2,1,0:T(4,128)S(1)}, u32[]{:S(2)}, u32[]{:S(2)}) collective-permute-start(f32[8,4,2048]{2,1,0:T(4,128)S(1)} %dynamic-slice_bitcast_fusion), channel_id=1, source_target_pairs={{0,4},{4,0},{1,5},{5,1},{2,6},{6,2},{3,7},{7,3},{8,12},{12,8},{9,1... | collective-permute-start | bytes 786440 | tf_op jit(solution)/shard_map/ppermute | solution.py:331
  50.7 20.3 %all-to-all-start.1 = ((f32[8,4,2048]{2,1,0:T(4,128)}), f32[8,4,2048]{2,1,0:T(4,128)S(1)}, u32[]{:S(2)}, u32[]{:S(2)}) async-start(f32[8,4,2048]{2,1,0:T(4,128)} %bitcast_add_fusion), calls=%async_computation.1 | async-start | bytes 524288 | tf_op jit(solution)/shard_map/all_to_all | solution.py:332
  60.5 0.9 copy-start.9
  61.4 43.4 %copy-start.7 = (f32[64,2048]{1,0:T(8,128)}, f32[64,2048]{1,0:T(8,128)S(1)}, u32[]{:S(2)}) copy-start(f32[64,2048]{1,0:T(8,128)S(1)} %get-tuple-element.40.base) | copy-start | bytes 1572868
  104.8 18.6 %all-to-all-start.2 = ((f32[8,4,1792]{2,1,0:T(4,128)}), f32[8,4,1792]{2,1,0:T(4,128)S(1)}, u32[]{:S(2)}, u32[]{:S(2)}) async-start(f32[8,4,1792]{2,1,0:T(4,128)} %get-tuple-element.31), calls=%async_computation.2 | async-start | bytes 458752 | tf_op jit(solution)/shard_map/all_to_all | solution.py:357
  122.0 1.3 copy-start.3
  124.5 14.4 %all-to-all-start.3 = ((f32[8,4,1024]{2,1,0:T(4,128)}), f32[8,4,1024]{2,1,0:T(4,128)S(1)}, u32[]{:S(2)}, u32[]{:S(2)}) async-start(f32[8,4,1024]{2,1,0:T(4,128)} %shard_map.110), calls=%async_computation.3 | async-start | bytes 262144 | tf_op jit(solution)/shard_map/all_to_all | solution.py:373
  131.2 2.8 %copy-start = (f32[128,12672]{1,0:T(8,128)S(1)}, f32[128,12672]{1,0:T(8,128)}, u32[]{:S(2)}) copy-start(f32[128,12672]{1,0:T(8,128)} %all-gather.4.cloned.1.call-done.source) | copy-start | bytes 19464196
  138.9 1.5 copy-start.4
  140.4 20.8 %copy-start.8 = (f32[64,2048]{1,0:T(8,128)S(1)}, f32[64,2048]{1,0:T(8,128)}, u32[]{:S(2)}) copy-start(f32[64,2048]{1,0:T(8,128)} %copy-done.7) | copy-start | bytes 1572868
  140.4 20.8 %copy-start.10 = (f32[16,64,128]{2,1,0:T(8,128)S(1)}, f32[16,64,128]{2,1,0:T(8,128)}, u32[]{:S(2)}) copy-start(f32[16,64,128]{2,1,0:T(8,128)} %copy-done.9) | copy-start | bytes 1572868
Sparse Core Ops, SparseCore 0:
  41.1 58.3 all-gather.3

commit v6 on v5

--- a/solution.py
+++ b/solution.py
@@ -19,7 +19,6 @@
 L3_AT = 9728
 L0_AT = 11648
 PACK = 12672
-RANGES = {"l1": (0, L2_AT), "l2": (L2_AT, L3_AT), "l3": (L3_AT, L0_AT)}
 
 exact = lax.Precision.HIGHEST
 MIB = 1024 * 1024
@@ -101,6 +100,14 @@
     out[:, L0_AT:] = inv[:, :1024]
 
 
+def vm(*shape):
+    return pltpu.VMEM(shape, jnp.float32)
+
+
+def bf16(*shape):
+    return jax.ShapeDtypeStruct(shape, jnp.bfloat16)
+
+
 def leaf_forward_kernel(blocks, at, shift, sep_t, sep_noise, inverse, panel, lf_out, pay_out, acc):
     acc[...] = jnp.zeros_like(acc)
 
@@ -133,47 +140,47 @@
     lax.fori_loop(0, NODES, step, 0)
 
 
-def fetch(source, path, sems, order):
-    copies = {}
-    for name in order:
-        lo, hi = RANGES[name]
-        copies[name] = pltpu.make_async_copy(source.at[:, lo:hi], path.at[:, lo:hi], sems.at[order.index(name)])
-        copies[name].start()
+def fetch(source, sems, target, blocks, at, width, first, used=None):
+    used = used or width
+    copies = []
+    for q in range(blocks):
+        copies.append(
+            pltpu.make_async_copy(
+                source.at[:, at + q * width : at + q * width + used],
+                target.at[q * 128 : (q + 1) * 128, :],
+                sems.at[first + q],
+            )
+        )
+        copies[q].start()
     return copies
 
 
-def forward_kernel(place, v, noise, source, send_out, g3_out, path, sems):
-    copies = fetch(source, path, sems, ("l3", "l2", "l1"))
+def forward_kernel(place, v, noise, source, send_out, g3_out, l1, l2, l3, sems):
+    copies3 = fetch(source, sems, l3, 1, L3_AT, 1920, 0)
+    copies2 = fetch(source, sems, l2, 2, L2_AT, 1792, 1)
+    copies1 = fetch(source, sems, l1, 4, 0, 1536, 3)
     w = v[...]
-    copies["l3"].wait()
-    g3 = nt(w[:, 1792:], path[:, L3_AT : L3_AT + 128])
-    w = w[:, :1792] - nn(g3, path[:, L3_AT + 128 : L0_AT])
+    copies3[0].wait()
+    g3 = nt(w[:, 1792:], l3[:, :128])
+    w = w[:, :1792] - nn(g3, l3[:, 128:])
     g3_out[...] = g3 + noise[3]
     zq = place[0]
-    copies["l2"].wait()
-    two = []
-    r2 = w[:, 1536:]
-    w = w[:, :1536]
-    for p in range(2):
-        at = L2_AT + p * 1792
-        g = nt(r2, path[:, at : at + 256])
-        w = w - nn(g, path[:, at + 256 : at + 1792])
-        two.append(g + jnp.where(zq % 2 == p, noise[2], 0.0))
-    r1 = w[:, 1024:]
-    w = w[:, :1024]
-    copies["l1"].wait()
-    one = []
-    for q in range(4):
-        at = q * 1536
-        g = nt(r1, path[:, at : at + 512])
-        w = w - nn(g, path[:, at + 512 : at + 1536])
-        one.append(g + jnp.where(zq == q, noise[1], 0.0))
+    for copy in copies2:
+        copy.wait()
+    g2 = nt(w[:, 1536:], l2[:, :256])
+    w = w[:, :1536] - nn(g2, l2[:, 256:])
+    for copy in copies1:
+        copy.wait()
+    g1 = nt(w[:, 1024:], l1[:, :512])
+    w = w[:, :1024] - nn(g1, l1[:, 512:])
     for d in range(8):
         send_out[d, :, :1024] = w
         for q in range(4):
-            send_out[d, :, 1024 + q * 128 : 1152 + q * 128] = one[q]
+            lanes = slice(q * 128, (q + 1) * 128)
+            send_out[d, :, 1024 + q * 128 : 1152 + q * 128] = g1[:, lanes] + jnp.where(zq == q, noise[1], 0.0)
         for p in range(2):
-            send_out[d, :, 1536 + p * 128 : 1664 + p * 128] = two[p]
+            lanes = slice(p * 128, (p + 1) * 128)
+            send_out[d, :, 1536 + p * 128 : 1664 + p * 128] = g2[:, lanes] + jnp.where(zq % 2 == p, noise[2], 0.0)
 
 
 def top_kernel(got, noise, path, send_out):
@@ -186,70 +193,43 @@
         send_out[d] = x0
 
 
-def operator_kernel(source, high_out, low_out, path, found, sems):
-    copies = fetch(source, path, sems, ("l1", "l2", "l3"))
-
-    def keep(lo, hi):
-        high, low = halves(found[lo:hi, :])
-        high_out[lo:hi, :] = high
-        low_out[lo:hi, :] = low
-
-    copies["l1"].wait()
-    total = None
-    for q in range(4):
-        at = q * 1536
-        term = tn(path[:, at : at + 512], path[:, at + 512 : at + 1536])
-        total = term if total is None else total + term
-    found[:512, :] = -total
-    keep(0, 512)
-    copies["l2"].wait()
-    total = None
-    for p in range(2):
-        at = L2_AT + p * 1792
-        y = path[:, at + 256 : at + 1280] + nn(path[:, at + 1280 : at + 1792], found[:512, :])
-        term = tn(path[:, at : at + 256], y)
-        total = term if total is None else total + term
-    found[512:768, :] = -total
-    keep(512, 768)
-    copies["l3"].wait()
-    y = path[:, L3_AT + 128 : L3_AT + 1152] + nn(path[:, L3_AT + 1152 : L0_AT], found[:768, :])
-    found[768:, :] = -tn(path[:, L3_AT : L3_AT + 128], y)
-    keep(768, 896)
-
-
-def rest_kernel(place, got, g3, source, x_out, path, sems):
-    copies = fetch(source, path, sems, ("l1", "l2", "l3"))
+def operator_kernel(source, map_out, l1, sems):
+    for copy in fetch(source, sems, l1, 4, 0, 1536, 0):
+        copy.wait()
+    found = -tn(l1[:, :512], l1[:, 512:])
+    map_out[...] = found
+
+
+def lower_kernel(place, got, g3, upper, source, x_out, found, inv1, l2, l3, sems):
+    copies = fetch(source, sems, inv1, 4, 0, 1536, 3, 512)
+    copies += fetch(source, sems, l2, 2, L2_AT, 1792, 1)
+    copies += fetch(source, sems, l3, 1, L3_AT, 1920, 0)
     z = place[0] + 4 * place[1]
     g1 = jnp.zeros((GROUP, 512), jnp.float32)
     g2 = jnp.zeros((GROUP, 256), jnp.float32)
     for d in range(8):
         g1 = g1 + jnp.where(z // 4 == d // 4, got[d, :, 1024:1536], 0.0)
         g2 = g2 + jnp.where(z // 2 == d // 2, got[d, :, 1536:], 0.0)
-    copies["l1"].wait()
-    x1 = jnp.zeros((GROUP, 512), jnp.float32)
-    for q in range(4):
-        x1 = x1 + nn(g1[:, q * 128 : (q + 1) * 128], path[:, q * 1536 : q * 1536 + 512])
+    for copy in copies:
+        copy.wait()
+    x1 = nn(g1, inv1[...])
     x_out[:, :512] = x1
-    copies["l2"].wait()
-    x2 = jnp.zeros((GROUP, 256), jnp.float32)
-    for p in range(2):
-        at = L2_AT + p * 1792
-        y = g2[:, p * 128 : (p + 1) * 128] - nt(x_out[:, :512], path[:, at + 1280 : at + 1792])
-        x2 = x2 + nn(y, path[:, at : at + 256])
+    x2 = nn(g2 - nt(x1, l2[:, 1280:]), l2[:, :256])
     x_out[:, 512:768] = x2
-    copies["l3"].wait()
-    y = g3[...] - nt(x_out[:, :768], path[:, L3_AT + 1152 : L0_AT])
-    x_out[:, 768:] = nn(y, path[:, L3_AT : L3_AT + 128])
-
-
-def backward_kernel(got0, rest, high, low, x_out):
+    x_out[:, 768:] = nn(g3[...] - nt(x_out[:, :768], l3[:, 1152:]), l3[:, :128])
+    y = l2[:, 256:1280] + nn(l2[:, 1280:], upper[...])
+    found[:256, :] = -tn(l2[:, :256], y)
+    y = l3[:, 128:1152] + nn(l3[:, 1152:1664], upper[...]) + nn(l3[:, 1664:], found[:256, :])
+    found[256:, :] = -tn(l3[:, :128], y)
+
+
+def backward_kernel(got0, rest, upper, lower, x_out):
     x0 = got0[0]
     for d in range(1, 8):
         x0 = x0 + got0[d]
     x_out[:, :1024] = x0
-    xh, xl = halves(x0)
-    dot = lambda p, q: lax.dot_general(p, q[...], (((1,), (1,)), ((), ())), preferred_element_type=jnp.float32)
-    x_out[:, 1024:] = rest[...] + (dot(xh, high) + (dot(xh, low) + dot(xl, high)))
+    x_out[:, 1024:1536] = rest[:, :512] + nt(x0, upper[...])
+    x_out[:, 1536:] = rest[:, 512:] + nt(x0, lower[...])
 
 
 def leaf_backward_kernel(blocks, at, x, base, w, leaf_out, sep_out, rows_s, cols_s):
@@ -271,10 +251,6 @@
         return carry
 
     lax.fori_loop(0, NODES, step, 0, unroll=4)
-
-
-def path_scratch(*more):
-    return [pltpu.VMEM((128, L0_AT), jnp.float32), *more, pltpu.SemaphoreType.DMA((3,))]
 
 
 def body(
@@ -348,44 +324,44 @@
         [place, v, noise, path],
         smem=1,
         hbm=1,
-        scratch=path_scratch(),
+        scratch=[vm(512, 1536), vm(256, 1792), vm(128, 1920), pltpu.SemaphoreType.DMA((7,))],
         vmem=48,
         flops=12_000_000,
         nbytes=6_500_000,
     )
     path, send = lax.optimization_barrier((path, send))
     got = lax.all_to_all(send, zz, 0, 0)
-    high, low = call(
+    upper = call(
         operator_kernel,
-        [jax.ShapeDtypeStruct((896, 1024), jnp.bfloat16)] * 2,
+        f32(512, 1024),
         [path],
         hbm=1,
-        scratch=path_scratch(pltpu.VMEM((896, 1024), jnp.float32)),
+        scratch=[vm(512, 1536), pltpu.SemaphoreType.DMA((4,))],
         vmem=48,
-        flops=3_500_000_000,
+        flops=1_600_000_000,
         nbytes=10_000_000,
     )
     top_rows = path[:, L0_AT:]
-    got, high, low, top_rows = lax.optimization_barrier((got, high, low, top_rows))
+    got, upper, top_rows = lax.optimization_barrier((got, upper, top_rows))
     top_send = call(
         top_kernel, f32(8, GROUP, 1024), [got, noise, top_rows], flops=2_000_000, nbytes=600_000, vmem=8
     )
     got0 = lax.all_to_all(top_send, zz, 0, 0)
-    rest = call(
-        rest_kernel,
-        f32(GROUP, 896),
-        [place, got, g3, path],
+    rest, lower = call(
+        lower_kernel,
+        [f32(GROUP, 896), f32(384, 1024)],
+        [place, got, g3, upper, path],
         smem=1,
         hbm=1,
-        scratch=path_scratch(),
-        vmem=20,
-        flops=300_000_000,
-        nbytes=6_500_000,
+        scratch=[vm(512, 512), vm(256, 1792), vm(128, 1920), pltpu.SemaphoreType.DMA((7,))],
+        vmem=48,
+        flops=2_200_000_000,
+        nbytes=10_000_000,
     )
     x = call(
         backward_kernel,
         f32(GROUP, ANC),
-        [got0, rest, high, low],
+        [got0, rest, upper, lower],
         flops=20_000_000,
         nbytes=4_000_000,
         vmem=16,

time: 172 us -> 169 us (0.983)
  local copies, waits for them, and re-layouts: 12.6 us -> 8.81 us
  waiting for transfers between devices: 51.7 us -> 55.4 us
  starting transfers between devices: 36.4 us -> 33.7 us
    all_to_all x1, waiting for transfers between devices: 0.01 us -> 5.69 us  [body(): got = lax.all_to_all(send, zz, 0, 0)]
    all_to_all x1, starting transfers between devices: 6.64 us -> 3.37 us  [body(): got0 = lax.all_to_all(top_send, zz, 0, 0)]
    unnamed x38 -> x34, local copies, waits for them, and re-layouts: 9.15 us -> 6.02 us
    all_to_all x1, waiting for transfers between devices: 2.25 us -> 0.07 us  [body(): got0 = lax.all_to_all(top_send, zz, 0, 0)]
  transfers between devices with their start and end apart: 6 -> 6, of which waited for: 5 -> 6; matrix products, arithmetic and copies ran while one was open for 3% -> 3% of each run, Pallas kernels for 12% -> 12%
where the time goes in v6:
time: 169 us; the launch traced here: 168 us
  waiting for transfers between devices  55.4 us (33%)
  Pallas kernels  34.2 us (20%)
  starting transfers between devices  33.7 us (20%)
  blocking collectives  19.4 us (11%)
  between operations  14.3 us (8%)
  local copies, waits for them, and re-layouts  8.81 us (5%)
  other arithmetic  2 us (1%)
    pallas_call x10, Pallas kernels, call(): pl.pallas_call(kernel, out_shape=outs, in_specs=[pl.BlockSpec(memory_spac...  34.2 us
    all_gather x1, waiting for transfers between devices, body(): path = lax.all_gather(packed, yc, axis=0, tiled=True)  28.6 us
    all_gather x1, blocking collectives, body(): gathered = lax.all_gather(x, yc, axis=0, tiled=False)  19.4 us
    all_to_all x1, waiting for transfers between devices, body(): quad = lax.all_to_all(copies, ('zq', 'rhs'), 0, 0)  10.7 us
    all_to_all x1, starting transfers between devices, body(): quad = lax.all_to_all(copies, ('zq', 'rhs'), 0, 0)  10.4 us
    all_to_all x1, waiting for transfers between devices, body(): pay = lax.all_to_all(pay, 'y', 0, 0)  9.1 us
    all_to_all x1, starting transfers between devices, body(): got = lax.all_to_all(send, zz, 0, 0)  8.18 us
    all_to_all x1, starting transfers between devices, body(): pay = lax.all_to_all(pay, 'y', 0, 0)  6.82 us
  transfers between devices with their start and end apart: 6, of which 6 were waited for; matrix products, arithmetic and copies ran while one was open for 3% of the time, Pallas kernels for 12%

profile of v6, /device:TPU:1, one launch (start us, length us, event | category | flops | bytes accessed | tf_op | source)
XLA Modules:
  0.0 167.9 jit_solution(7427085471172961932)
XLA Ops:
  7.2 0.0 copy-start.4
  7.2 0.9 copy-done.11
  8.1 0.7 copy-done.12
  8.8 1.1 shard_map.104
  10.0 10.4 %all-to-all-start = ((f32[16,8,1568]{2,1,0:T(8,128)}), f32[16,8,1568]{2,1,0:T(8,128)S(1)}, u32[]{:S(2)}, u32[]{:S(2)}) async-start(f32[16,8,1568]{2,1,0:T(8,128)} %shard_map.104), calls=%async_computation | async-start | bytes 1703936 | tf_op jit(solution)/shard_map/all_to_all | solution.py:276
  20.4 0.0 all-gather.4.cloned.1.call-start
  20.5 0.1 copy.27.blocks
  20.5 0.1 copy.22
  20.6 0.1 pad.2.clone
  20.7 0.1 pad_add_fusion.at
  20.8 0.1 maximum_maximum_fusion.sep_noise
  20.9 0.0 copy-done.4
  20.9 0.0 copy-done.1
  20.9 0.0 copy-done.13
  20.9 7.0 %shard_map.105 = (f32[64,2048]{1,0:T(8,128)S(1)}, f32[64,2048]{1,0:T(8,128)S(1)}) custom-call(s32[16,8]{1,0:T(8,128)S(1)} %copy.27.blocks, s32[4]{0:T(128)S(1)} %pad_add_fusion.at, f32[64,2048]{1,0:T(8,128)S(1)} %copy-done.4, f32[32,64]{1,0:T(8,128)S(1)} %bitcast.17, f32[64,128]{1,0:T(8,128)S(1)} %maximum_maximum_fusion.sep_noise, ...), custom_call_target="tpu_custom_call" | custom-call | flops 50000000 | bytes 3000000 | tf_op jit(solution)/shard_map/pallas_call | solution.py:57
  27.9 0.8 copy-done.10
  28.7 0.1 pad_add_fusion.1.place
  28.8 10.7 %all-to-all-done.quad = f32[16,8,1568]{2,1,0:T(8,128)S(1)} async-done(((f32[16,8,1568]{2,1,0:T(8,128)}), f32[16,8,1568]{2,1,0:T(8,128)S(1)}, u32[]{:S(2)}, u32[]{:S(2)}) %all-to-all-start) | async-done | bytes 802848 | tf_op jit(solution)/shard_map/all_to_all | solution.py:276
  39.5 1.5 shard_map.106
  41.0 0.0 all-gather.4.cloned.1.call-update
  41.0 1.2 reshape.13
  42.2 4.9 %collective-permute-start = (f32[8,4,2048]{2,1,0:T(4,128)S(1)}, f32[8,4,2048]{2,1,0:T(4,128)}, u32[]{:S(2)}, u32[]{:S(2)}) collective-permute-start(f32[8,4,2048]{2,1,0:T(4,128)S(1)} %dynamic-slice_bitcast_fusion), channel_id=1, source_target_pairs={{0,4},{4,0},{1,5},{5,1},{2,6},{6,2},{3,7},{7,3},{8,12},{12,8},{9,1... | collective-permute-start | bytes 786440 | tf_op jit(solution)/shard_map/ppermute | solution.py:307
  47.2 1.3 collective-permute-done
  48.4 1.7 %bitcast_add_fusion = f32[8,4,2048]{2,1,0:T(4,128)} fusion(f32[8,4,2048]{2,1,0:T(4,128)} %collective-permute-done, f32[8,2,4,2048]{3,2,1,0:T(4,128)S(1)} %reshape.13, s32[]{:T(128)S(6)} %select_n.47), kind=kLoop, calls=%fused_computation | loop fusion | flops 65536 | bytes 786436 | tf_op jit(solution)/shard_map/add | solution.py:307
  50.2 6.8 %all-to-all-start.1 = ((f32[8,4,2048]{2,1,0:T(4,128)}), f32[8,4,2048]{2,1,0:T(4,128)S(1)}, u32[]{:S(2)}, u32[]{:S(2)}) async-start(f32[8,4,2048]{2,1,0:T(4,128)} %bitcast_add_fusion), calls=%async_computation.1 | async-start | bytes 524288 | tf_op jit(solution)/shard_map/all_to_all | solution.py:308
  57.0 3.0 %shard_map.107 = (f32[64,2048]{1,0:T(8,128)S(1)}, f32[16,64,128]{2,1,0:T(8,128)S(1)}) custom-call(f32[64,2048]{1,0:T(8,128)S(1)} %get-tuple-element.25.lf, f32[64,2048]{1,0:T(8,128)S(1)} %copy-done.5, f32[16,128,128]{2,1,0:T(8,128)S(1)} %copy-done, f32[16,64,128]{2,1,0:T(8,128)S(1)} %copy-done.1), custom_call_target="tpu_custom_call" | custom-call | flops 70000000 | bytes 4000000 | tf_op jit(solution)/shard_map/pallas_call | solution.py:57
  60.0 0.8 copy-done.8
  60.8 9.1 %all-to-all-done.1 = f32[8,4,2048]{2,1,0:T(4,128)S(1)} async-done(((f32[8,4,2048]{2,1,0:T(4,128)}), f32[8,4,2048]{2,1,0:T(4,128)S(1)}, u32[]{:S(2)}, u32[]{:S(2)}) %all-to-all-start.1) | async-done | bytes 262176 | tf_op jit(solution)/shard_map/all_to_all | solution.py:308
  69.9 0.1 reshape.14
  70.1 0.1 copy.26
  70.2 0.2 reshape.15.noise
  70.4 28.6 %all-gather.4.cloned.1.call-done.source = f32[128,12672]{1,0:T(8,128)} async-done(((f32[8,12672]{1,0:T(8,128)}), f32[128,12672]{1,0:T(8,128)}) %all-gather.4.cloned.1.call-update) | async-done | bytes 6488080 | tf_op jit(solution)/shard_map/all_gather | solution.py:301
  99.0 5.8 %shard_map.108 = (f32[8,4,1792]{2,1,0:T(4,128)}, f32[4,128]{1,0:T(4,128)S(1)}) custom-call(s32[2]{0:T(128)S(1)} %pad_add_fusion.1.place, f32[4,1920]{1,0:T(4,128)S(1)} %slice_reduce_fusion.v, f32[4,4,128]{2,1,0:T(4,128)S(1)} %reshape.15.noise, f32[128,12672]{1,0:T(8,128)} %all-gather.4.cloned.1.call-done.source), custom_call_target="tpu_custom_call" | custom-call | flops 12000000 | bytes 6500000 | tf_op jit(solution)/shard_map/pallas_call | solution.py:57
  104.7 0.0 copy-done.6
  104.7 8.2 %all-to-all-start.2 = ((f32[8,4,1792]{2,1,0:T(4,128)}), f32[8,4,1792]{2,1,0:T(4,128)S(1)}, u32[]{:S(2)}, u32[]{:S(2)}) async-start(f32[8,4,1792]{2,1,0:T(4,128)} %get-tuple-element.30), calls=%async_computation.2 | async-start | bytes 458752 | tf_op jit(solution)/shard_map/all_to_all | solution.py:333
  112.9 1.1 slice.11.path
  114.0 3.7 %shard_map.109.upper = f32[512,1024]{1,0:T(8,128)S(1)} custom-call(f32[128,12672]{1,0:T(8,128)} %all-gather.4.cloned.1.call-done.source), custom_call_target="tpu_custom_call" | custom-call | flops 1600000000 | bytes 10000000 | tf_op jit(solution)/shard_map/pallas_call | solution.py:57
  117.7 5.7 %all-to-all-done.2.got = f32[8,4,1792]{2,1,0:T(4,128)S(1)} async-done(((f32[8,4,1792]{2,1,0:T(4,128)}), f32[8,4,1792]{2,1,0:T(4,128)S(1)}, u32[]{:S(2)}, u32[]{:S(2)}) %all-to-all-start.2) | async-done | bytes 229408 | tf_op jit(solution)/shard_map/all_to_all | solution.py:333
  123.4 1.2 shard_map.110
  124.6 3.4 %all-to-all-start.3 = ((f32[8,4,1024]{2,1,0:T(4,128)}), f32[8,4,1024]{2,1,0:T(4,128)S(1)}, u32[]{:S(2)}, u32[]{:S(2)}) async-start(f32[8,4,1024]{2,1,0:T(4,128)} %shard_map.110), calls=%async_computation.3 | async-start | bytes 262144 | tf_op jit(solution)/shard_map/all_to_all | solution.py:349
  128.0 6.6 %shard_map.111 = (f32[4,896]{1,0:T(4,128)S(1)}, f32[384,1024]{1,0:T(8,128)S(1)}) custom-call(s32[2]{0:T(128)S(1)} %pad_add_fusion.1.place, f32[8,4,1792]{2,1,0:T(4,128)S(1)} %all-to-all-done.2.got, f32[4,128]{1,0:T(4,128)S(1)} %get-tuple-element.34.g3, f32[512,1024]{1,0:T(8,128)S(1)} %shard_map.109.upper, f32[128,12672]{1,0:T(8,128)} %all-gather.4.cloned.1.call-done.source), custom_call_target="tpu_custom_call" | custom-call | flops 2200000000 | bytes 10000000 | tf_op jit(solution)/shard_map/pallas_call | solution.py:57
  134.6 0.0 copy-start.2
  134.6 1.2 copy-done.2
  135.8 0.1 all-to-all-done.3.got0
  135.8 1.4 copy-done.3
  137.3 1.5 shard_map.112
  138.8 19.4 %all-gather.1.x = f32[16,4,1920]{2,1,0:T(4,128)S(1)} all-gather(f32[1,4,1920]{2,1,0:T(4,128)S(1)} %bitcast.16), channel_id=2, replica_groups=mesh['zh'=2,'zq'=4,'y'=8,'core'=2,'rhs'=4] {'y','core'}, dimensions={0}, use_global_device_ids=true | all-gather | bytes 522240 | tf_op jit(solution)/shard_map/all_gather | solution.py:369
  158.2 2.9 %shard_map.113 = (f32[64,2048]{1,0:T(8,128)}, f32[32,64]{1,0:T(8,128)}) custom-call(s32[16,8]{1,0:T(8,128)S(1)} %copy.27.blocks, s32[4]{0:T(128)S(1)} %pad_add_fusion.at, f32[16,4,1920]{2,1,0:T(4,128)S(1)} %all-gather.1.x, f32[64,2048]{1,0:T(8,128)S(1)} %copy-done.7, f32[16,64,128]{2,1,0:T(8,128)S(1)} %copy-done.9), custom_call_target="tpu_custom_call" | custom-call | flops 20000000 | bytes 2000000 | tf_op jit(solution)/shard_map/pallas_call | solution.py:57
  (26 shorter events, 0.1 us)
Async XLA Ops:
  7.2 13.7 %copy-start.4 = (f32[64,2048]{1,0:T(8,128)S(1)}, f32[64,2048]{1,0:T(8,128)}, u32[]{:S(2)}) copy-start(f32[64,2048]{1,0:T(8,128)} %shift.1) | copy-start | bytes 1572868
  7.2 13.7 %copy-start = (f32[16,128,128]{2,1,0:T(8,128)S(1)}, f32[16,128,128]{2,1,0:T(8,128)}, u32[]{:S(2)}) copy-start(f32[16,128,128]{2,1,0:T(8,128)} %inverse.5) | copy-start | bytes 3145732
  7.2 13.7 %copy-start.1 = (f32[16,64,128]{2,1,0:T(8,128)S(1)}, f32[16,64,128]{2,1,0:T(8,128)}, u32[]{:S(2)}) copy-start(f32[16,64,128]{2,1,0:T(8,128)} %panel.3) | copy-start | bytes 1572868
  7.2 0.9 copy-start.11
  8.1 0.7 copy-start.12
  8.8 11.6 %copy-start.15 = (s32[16,8]{0,1:T(8,128)S(1)}, s32[16,8]{0,1:T(8,128)}, u32[]{:S(2)}) copy-start(s32[16,8]{0,1:T(8,128)} %param.15) | copy-start | bytes 1540
  8.8 11.7 %copy-start.14 = (f32[64,32]{0,1:T(8,128)S(1)}, f32[64,32]{0,1:T(8,128)}, u32[]{:S(2)}) copy-start(f32[64,32]{0,1:T(8,128)} %param.12) | copy-start | bytes 24580
  8.8 12.1 %copy-start.13 = (f32[64,32]{0,1:T(8,128)S(1)}, f32[64,32]{0,1:T(8,128)}, u32[]{:S(2)}) copy-start(f32[64,32]{0,1:T(8,128)} %param.10) | copy-start | bytes 24580
  10.0 29.5 %all-to-all-start = ((f32[16,8,1568]{2,1,0:T(8,128)}), f32[16,8,1568]{2,1,0:T(8,128)S(1)}, u32[]{:S(2)}, u32[]{:S(2)}) async-start(f32[16,8,1568]{2,1,0:T(8,128)} %shard_map.104), calls=%async_computation | async-start | bytes 1703936 | tf_op jit(solution)/shard_map/all_to_all | solution.py:276
  20.4 78.6 %all-gather.4.cloned.1.call-start = ((), (), s32[]{:S(2)}) async-start(), calls=%async_computation.4 | async-start | bytes 6893568 | tf_op jit(solution)/shard_map/all_gather | solution.py:301
  27.9 0.8 copy-start.10
  39.5 17.5 %copy-start.5 = (f32[64,2048]{1,0:T(8,128)S(1)}, f32[64,2048]{1,0:T(8,128)}, u32[]{:S(2)}) copy-start(f32[64,2048]{1,0:T(8,128)} %noise.1) | copy-start | bytes 1572868
  42.2 6.2 %collective-permute-start = (f32[8,4,2048]{2,1,0:T(4,128)S(1)}, f32[8,4,2048]{2,1,0:T(4,128)}, u32[]{:S(2)}, u32[]{:S(2)}) collective-permute-start(f32[8,4,2048]{2,1,0:T(4,128)S(1)} %dynamic-slice_bitcast_fusion), channel_id=1, source_target_pairs={{0,4},{4,0},{1,5},{5,1},{2,6},{6,2},{3,7},{7,3},{8,12},{12,8},{9,1... | collective-permute-start | bytes 786440 | tf_op jit(solution)/shard_map/ppermute | solution.py:307
  50.2 19.7 %all-to-all-start.1 = ((f32[8,4,2048]{2,1,0:T(4,128)}), f32[8,4,2048]{2,1,0:T(4,128)S(1)}, u32[]{:S(2)}, u32[]{:S(2)}) async-start(f32[8,4,2048]{2,1,0:T(4,128)} %bitcast_add_fusion), calls=%async_computation.1 | async-start | bytes 524288 | tf_op jit(solution)/shard_map/all_to_all | solution.py:308
  60.0 0.8 copy-start.8
  60.8 43.9 %copy-start.6 = (f32[64,2048]{1,0:T(8,128)}, f32[64,2048]{1,0:T(8,128)S(1)}, u32[]{:S(2)}) copy-start(f32[64,2048]{1,0:T(8,128)S(1)} %get-tuple-element.38.base) | copy-start | bytes 1572868
  104.7 18.7 %all-to-all-start.2 = ((f32[8,4,1792]{2,1,0:T(4,128)}), f32[8,4,1792]{2,1,0:T(4,128)S(1)}, u32[]{:S(2)}, u32[]{:S(2)}) async-start(f32[8,4,1792]{2,1,0:T(4,128)} %get-tuple-element.30), calls=%async_computation.2 | async-start | bytes 458752 | tf_op jit(solution)/shard_map/all_to_all | solution.py:333
  124.6 11.2 %all-to-all-start.3 = ((f32[8,4,1024]{2,1,0:T(4,128)}), f32[8,4,1024]{2,1,0:T(4,128)S(1)}, u32[]{:S(2)}, u32[]{:S(2)}) async-start(f32[8,4,1024]{2,1,0:T(4,128)} %shard_map.110), calls=%async_computation.3 | async-start | bytes 262144 | tf_op jit(solution)/shard_map/all_to_all | solution.py:349
  134.6 1.2 copy-start.2
  135.8 1.4 copy-start.3
  137.2 20.9 %copy-start.7 = (f32[64,2048]{1,0:T(8,128)S(1)}, f32[64,2048]{1,0:T(8,128)}, u32[]{:S(2)}) copy-start(f32[64,2048]{1,0:T(8,128)} %copy-done.6) | copy-start | bytes 1572868
  137.3 21.0 %copy-start.9 = (f32[16,64,128]{2,1,0:T(8,128)S(1)}, f32[16,64,128]{2,1,0:T(8,128)}, u32[]{:S(2)}) copy-start(f32[16,64,128]{2,1,0:T(8,128)} %copy-done.8) | copy-start | bytes 1572868
Sparse Core Ops, SparseCore 0:
  41.1 57.7 all-gather.3

commit v7 on v6

--- a/solution.py
+++ b/solution.py
@@ -71,7 +71,13 @@
     return jax.ShapeDtypeStruct(shape, jnp.float32)
 
 
-def copies_kernel(inverse, coupling, out):
+def copies_kernel(inverse_in, coupling_in, out, inverse, coupling, sems):
+    one = pltpu.make_async_copy(inverse_in, inverse, sems.at[0])
+    two = pltpu.make_async_copy(coupling_in, coupling, sems.at[1])
+    one.start()
+    two.start()
+    one.wait()
+    two.wait()
     for d in range(16):
         out[d, :, :480] = inverse[...]
         out[d, :, 480:] = coupling[...]
@@ -193,14 +199,23 @@
         send_out[d] = x0
 
 
-def operator_kernel(source, map_out, l1, sems):
-    for copy in fetch(source, sems, l1, 4, 0, 1536, 0):
+def operator_kernel(source, upper, lower, l1, l2, l3, sems):
+    copies1 = fetch(source, sems, l1, 4, 0, 1536, 3)
+    copies2 = fetch(source, sems, l2, 2, L2_AT, 1792, 1)
+    copies3 = fetch(source, sems, l3, 1, L3_AT, 1920, 0)
+    for copy in copies1:
         copy.wait()
-    found = -tn(l1[:, :512], l1[:, 512:])
-    map_out[...] = found
-
-
-def lower_kernel(place, got, g3, upper, source, x_out, found, inv1, l2, l3, sems):
+    upper[...] = -tn(l1[:, :512], l1[:, 512:])
+    for copy in copies2:
+        copy.wait()
+    y = l2[:, 256:1280] + nn(l2[:, 1280:], upper[...])
+    lower[:256, :] = -tn(l2[:, :256], y)
+    copies3[0].wait()
+    y = l3[:, 128:1152] + nn(l3[:, 1152:1664], upper[...]) + nn(l3[:, 1664:], lower[:256, :])
+    lower[256:, :] = -tn(l3[:, :128], y)
+
+
+def rest_kernel(place, got, g3, upper, lower, source, x_out, inv1, l2, l3, sems):
     copies = fetch(source, sems, inv1, 4, 0, 1536, 3, 512)
     copies += fetch(source, sems, l2, 2, L2_AT, 1792, 1)
     copies += fetch(source, sems, l3, 1, L3_AT, 1920, 0)
@@ -217,10 +232,6 @@
     x2 = nn(g2 - nt(x1, l2[:, 1280:]), l2[:, :256])
     x_out[:, 512:768] = x2
     x_out[:, 768:] = nn(g3[...] - nt(x_out[:, :768], l3[:, 1152:]), l3[:, :128])
-    y = l2[:, 256:1280] + nn(l2[:, 1280:], upper[...])
-    found[:256, :] = -tn(l2[:, :256], y)
-    y = l3[:, 128:1152] + nn(l3[:, 1152:1664], upper[...]) + nn(l3[:, 1664:], found[:256, :])
-    found[256:, :] = -tn(l3[:, :128], y)
 
 
 def backward_kernel(got0, rest, upper, lower, x_out):
@@ -272,7 +283,14 @@
     place = jnp.stack([zq, zh]).astype(jnp.int32)
     at = jnp.stack([STARTS[k] + dev % (128 >> k) * SEP_DEV for k in range(LEVELS)]).astype(jnp.int32)
 
-    copies = call(copies_kernel, f32(16, 8, 1568), [sep_inverse, sep_coupling], nbytes=900_000)
+    copies = call(
+        copies_kernel,
+        f32(16, 8, 1568),
+        [sep_inverse, sep_coupling],
+        hbm=2,
+        scratch=[vm(8, 480), vm(8, 1088), pltpu.SemaphoreType.DMA((2,))],
+        nbytes=900_000,
+    )
     quad = lax.all_to_all(copies, ("zq", "rhs"), 0, 0)
     first = lax.axis_index("core") == 0
     noise_slot = jnp.concatenate(
@@ -331,32 +349,32 @@
     )
     path, send = lax.optimization_barrier((path, send))
     got = lax.all_to_all(send, zz, 0, 0)
-    upper = call(
+    upper, lower = call(
         operator_kernel,
-        f32(512, 1024),
+        [f32(512, 1024), f32(384, 1024)],
         [path],
         hbm=1,
-        scratch=[vm(512, 1536), pltpu.SemaphoreType.DMA((4,))],
+        scratch=[vm(512, 1536), vm(256, 1792), vm(128, 1920), pltpu.SemaphoreType.DMA((7,))],
         vmem=48,
-        flops=1_600_000_000,
+        flops=3_500_000_000,
         nbytes=10_000_000,
     )
     top_rows = path[:, L0_AT:]
-    got, upper, top_rows = lax.optimization_barrier((got, upper, top_rows))
+    got, upper, lower, top_rows = lax.optimization_barrier((got, upper, lower, top_rows))
     top_send = call(
         top_kernel, f32(8, GROUP, 1024), [got, noise, top_rows], flops=2_000_000, nbytes=600_000, vmem=8
     )
     got0 = lax.all_to_all(top_send, zz, 0, 0)
-    rest, lower = call(
-        lower_kernel,
-        [f32(GROUP, 896), f32(384, 1024)],
-        [place, got, g3, upper, path],
+    rest = call(
+        rest_kernel,
+        f32(GROUP, 896),
+        [place, got, g3, upper, lower, path],
         smem=1,
         hbm=1,
         scratch=[vm(512, 512), vm(256, 1792), vm(128, 1920), pltpu.SemaphoreType.DMA((7,))],
         vmem=48,
-        flops=2_200_000_000,
-        nbytes=10_000_000,
+        flops=300_000_000,
+        nbytes=8_000_000,
     )
     x = call(
         backward_kernel,

time: 169 us -> 170 us (level)
    all_to_all x1, waiting for transfers between devices: 5.69 us -> 1.75 us  [body(): got = lax.all_to_all(send, zz, 0, 0)]
    all_to_all x1, waiting for transfers between devices: 0.07 us -> 2.24 us  [body(): got0 = lax.all_to_all(top_send, zz, 0, 0)]
    unnamed x34 -> x36, local copies, waits for them, and re-layouts: 6.02 us -> 7.43 us
where the time goes in v7:
time: 170 us; the launch traced here: 169 us
  waiting for transfers between devices  53.7 us (32%)
  starting transfers between devices  35.3 us (21%)
  Pallas kernels  34.6 us (20%)
  blocking collectives  19.2 us (11%)
  between operations  14.3 us (8%)
  local copies, waits for them, and re-layouts  10.2 us (6%)
  other arithmetic  1.99 us (1%)
    pallas_call x10, Pallas kernels, call(): pl.pallas_call(kernel, out_shape=outs, in_specs=[pl.BlockSpec(memory_spac...  34.6 us
    all_gather x1, waiting for transfers between devices, body(): path = lax.all_gather(packed, yc, axis=0, tiled=True)  28.6 us
    all_gather x1, blocking collectives, body(): gathered = lax.all_gather(x, yc, axis=0, tiled=False)  19.2 us
    all_to_all x1, waiting for transfers between devices, body(): quad = lax.all_to_all(copies, ('zq', 'rhs'), 0, 0)  10.7 us
    all_to_all x1, starting transfers between devices, body(): quad = lax.all_to_all(copies, ('zq', 'rhs'), 0, 0)  10.4 us
    all_to_all x1, waiting for transfers between devices, body(): pay = lax.all_to_all(pay, 'y', 0, 0)  9.08 us
    all_to_all x1, starting transfers between devices, body(): got = lax.all_to_all(send, zz, 0, 0)  8.19 us
    unnamed x36, local copies, waits for them, and re-layouts  7.43 us
  transfers between devices with their start and end apart: 6, of which 6 were waited for; matrix products, arithmetic and copies ran while one was open for 3% of the time, Pallas kernels for 12%

profile of v7, /device:TPU:1, one launch (start us, length us, event | category | flops | bytes accessed | tf_op | source)
XLA Modules:
  0.0 169.2 jit_solution(1269855625704261062)
XLA Ops:
  7.2 0.0 copy-start.4
  7.2 0.0 copy-start.3
  7.2 0.0 copy-start.5
  7.2 0.9 copy-done.12
  8.1 0.7 copy-done.13
  8.8 1.2 shard_map.104
  10.1 10.4 %all-to-all-start = ((f32[16,8,1568]{2,1,0:T(8,128)}), f32[16,8,1568]{2,1,0:T(8,128)S(1)}, u32[]{:S(2)}, u32[]{:S(2)}) async-start(f32[16,8,1568]{2,1,0:T(8,128)} %shard_map.104), calls=%async_computation | async-start | bytes 1703936 | tf_op jit(solution)/shard_map/all_to_all | solution.py:294
  20.5 0.0 all-gather.4.cloned.1.call-start
  20.6 0.1 copy.27.blocks
  20.7 0.1 copy.22
  20.7 0.1 pad.2.clone
  20.8 0.1 pad_add_fusion.at
  20.9 0.1 maximum_maximum_fusion.sep_noise
  21.0 7.0 %shard_map.105 = (f32[64,2048]{1,0:T(8,128)S(1)}, f32[64,2048]{1,0:T(8,128)S(1)}) custom-call(s32[16,8]{1,0:T(8,128)S(1)} %copy.27.blocks, s32[4]{0:T(128)S(1)} %pad_add_fusion.at, f32[64,2048]{1,0:T(8,128)S(1)} %copy-done.5, f32[32,64]{1,0:T(8,128)S(1)} %bitcast.17, f32[64,128]{1,0:T(8,128)S(1)} %maximum_maximum_fusion.sep_noise, ...), custom_call_target="tpu_custom_call" | custom-call | flops 50000000 | bytes 3000000 | tf_op jit(solution)/shard_map/pallas_call | solution.py:57
  28.0 0.8 copy-done.11
  28.8 0.1 pad_add_fusion.1.place
  28.9 10.7 %all-to-all-done.quad = f32[16,8,1568]{2,1,0:T(8,128)S(1)} async-done(((f32[16,8,1568]{2,1,0:T(8,128)}), f32[16,8,1568]{2,1,0:T(8,128)S(1)}, u32[]{:S(2)}, u32[]{:S(2)}) %all-to-all-start) | async-done | bytes 802848 | tf_op jit(solution)/shard_map/all_to_all | solution.py:294
  39.6 1.5 shard_map.106
  41.1 0.0 all-gather.4.cloned.1.call-update
  41.1 1.2 reshape.13
  42.4 4.9 %collective-permute-start = (f32[8,4,2048]{2,1,0:T(4,128)S(1)}, f32[8,4,2048]{2,1,0:T(4,128)}, u32[]{:S(2)}, u32[]{:S(2)}) collective-permute-start(f32[8,4,2048]{2,1,0:T(4,128)S(1)} %dynamic-slice_bitcast_fusion), channel_id=1, source_target_pairs={{0,4},{4,0},{1,5},{5,1},{2,6},{6,2},{3,7},{7,3},{8,12},{12,8},{9,1... | collective-permute-start | bytes 786440 | tf_op jit(solution)/shard_map/ppermute | solution.py:325
  47.3 1.3 collective-permute-done
  48.6 1.7 %bitcast_add_fusion = f32[8,4,2048]{2,1,0:T(4,128)} fusion(f32[8,4,2048]{2,1,0:T(4,128)} %collective-permute-done, f32[8,2,4,2048]{3,2,1,0:T(4,128)S(1)} %reshape.13, s32[]{:T(128)S(6)} %select_n.47), kind=kLoop, calls=%fused_computation | loop fusion | flops 65536 | bytes 786436 | tf_op jit(solution)/shard_map/add | solution.py:325
  50.3 6.8 %all-to-all-start.1 = ((f32[8,4,2048]{2,1,0:T(4,128)}), f32[8,4,2048]{2,1,0:T(4,128)S(1)}, u32[]{:S(2)}, u32[]{:S(2)}) async-start(f32[8,4,2048]{2,1,0:T(4,128)} %bitcast_add_fusion), calls=%async_computation.1 | async-start | bytes 524288 | tf_op jit(solution)/shard_map/all_to_all | solution.py:326
  57.1 3.0 %shard_map.107 = (f32[64,2048]{1,0:T(8,128)S(1)}, f32[16,64,128]{2,1,0:T(8,128)S(1)}) custom-call(f32[64,2048]{1,0:T(8,128)S(1)} %get-tuple-element.26.lf, f32[64,2048]{1,0:T(8,128)S(1)} %copy-done.6, f32[16,128,128]{2,1,0:T(8,128)S(1)} %copy-done.3, f32[16,64,128]{2,1,0:T(8,128)S(1)} %copy-done.4), custom_call_target="tpu_custom_call" | custom-call | flops 70000000 | bytes 4000000 | tf_op jit(solution)/shard_map/pallas_call | solution.py:57
  60.1 0.8 copy-done.9
  60.9 9.1 %all-to-all-done.1 = f32[8,4,2048]{2,1,0:T(4,128)S(1)} async-done(((f32[8,4,2048]{2,1,0:T(4,128)}), f32[8,4,2048]{2,1,0:T(4,128)S(1)}, u32[]{:S(2)}, u32[]{:S(2)}) %all-to-all-start.1) | async-done | bytes 262176 | tf_op jit(solution)/shard_map/all_to_all | solution.py:326
  70.0 0.1 reshape.14
  70.2 0.1 copy.26
  70.2 0.2 reshape.15.noise
  70.5 28.6 %all-gather.4.cloned.1.call-done.source = f32[128,12672]{1,0:T(8,128)} async-done(((f32[8,12672]{1,0:T(8,128)}), f32[128,12672]{1,0:T(8,128)}) %all-gather.4.cloned.1.call-update) | async-done | bytes 6488080 | tf_op jit(solution)/shard_map/all_gather | solution.py:319
  99.1 5.8 %shard_map.108 = (f32[8,4,1792]{2,1,0:T(4,128)}, f32[4,128]{1,0:T(4,128)S(1)}) custom-call(s32[2]{0:T(128)S(1)} %pad_add_fusion.1.place, f32[4,1920]{1,0:T(4,128)S(1)} %slice_reduce_fusion.v, f32[4,4,128]{2,1,0:T(4,128)S(1)} %reshape.15.noise, f32[128,12672]{1,0:T(8,128)} %all-gather.4.cloned.1.call-done.source), custom_call_target="tpu_custom_call" | custom-call | flops 12000000 | bytes 6500000 | tf_op jit(solution)/shard_map/pallas_call | solution.py:57
  104.9 0.0 copy-done.7
  104.9 8.2 %all-to-all-start.2 = ((f32[8,4,1792]{2,1,0:T(4,128)}), f32[8,4,1792]{2,1,0:T(4,128)S(1)}, u32[]{:S(2)}, u32[]{:S(2)}) async-start(f32[8,4,1792]{2,1,0:T(4,128)} %get-tuple-element.31), calls=%async_computation.2 | async-start | bytes 458752 | tf_op jit(solution)/shard_map/all_to_all | solution.py:351
  113.1 1.1 slice.11.path
  114.1 6.5 %shard_map.109 = (f32[512,1024]{1,0:T(8,128)S(1)}, f32[384,1024]{1,0:T(8,128)S(1)}) custom-call(f32[128,12672]{1,0:T(8,128)} %all-gather.4.cloned.1.call-done.source), custom_call_target="tpu_custom_call" | custom-call | flops 3500000000 | bytes 10000000 | tf_op jit(solution)/shard_map/pallas_call | solution.py:57
  120.6 0.0 copy-start
  120.7 1.2 copy-done
  121.8 1.7 %all-to-all-done.2.got = f32[8,4,1792]{2,1,0:T(4,128)S(1)} async-done(((f32[8,4,1792]{2,1,0:T(4,128)}), f32[8,4,1792]{2,1,0:T(4,128)S(1)}, u32[]{:S(2)}, u32[]{:S(2)}) %all-to-all-start.2) | async-done | bytes 229408 | tf_op jit(solution)/shard_map/all_to_all | solution.py:351
  123.6 1.2 shard_map.110
  124.8 4.9 %all-to-all-start.3 = ((f32[8,4,1024]{2,1,0:T(4,128)}), f32[8,4,1024]{2,1,0:T(4,128)S(1)}, u32[]{:S(2)}, u32[]{:S(2)}) async-start(f32[8,4,1024]{2,1,0:T(4,128)} %shard_map.110), calls=%async_computation.3 | async-start | bytes 262144 | tf_op jit(solution)/shard_map/all_to_all | solution.py:367
  129.7 1.4 copy-done.1
  131.1 4.1 %shard_map.111.rest = f32[4,896]{1,0:T(4,128)S(1)} custom-call(s32[2]{0:T(128)S(1)} %pad_add_fusion.1.place, f32[8,4,1792]{2,1,0:T(4,128)S(1)} %all-to-all-done.2.got, f32[4,128]{1,0:T(4,128)S(1)} %get-tuple-element.37.g3, f32[512,1024]{1,0:T(8,128)S(1)} %get-tuple-element.38.upper, f32[384,1024]{1,0:T(8,128)S(1)} %copy-done.1, ...), custom_call_target="tpu_custom_call" | custom-call | flops 300000000 | bytes 8000000 | tf_op jit(solution)/shard_map/pallas_call | solution.py:57
  135.2 2.2 %all-to-all-done.3.got0 = f32[8,4,1024]{2,1,0:T(4,128)S(1)} async-done(((f32[8,4,1024]{2,1,0:T(4,128)}), f32[8,4,1024]{2,1,0:T(4,128)S(1)}, u32[]{:S(2)}, u32[]{:S(2)}) %all-to-all-start.3) | async-done | bytes 131104 | tf_op jit(solution)/shard_map/all_to_all | solution.py:367
  137.4 1.4 copy-done.2
  138.8 1.5 shard_map.112
  140.4 19.2 %all-gather.1.x = f32[16,4,1920]{2,1,0:T(4,128)S(1)} all-gather(f32[1,4,1920]{2,1,0:T(4,128)S(1)} %bitcast.16), channel_id=2, replica_groups=mesh['zh'=2,'zq'=4,'y'=8,'core'=2,'rhs'=4] {'y','core'}, dimensions={0}, use_global_device_ids=true | all-gather | bytes 522240 | tf_op jit(solution)/shard_map/all_gather | solution.py:387
  159.5 2.9 %shard_map.113 = (f32[64,2048]{1,0:T(8,128)}, f32[32,64]{1,0:T(8,128)}) custom-call(s32[16,8]{1,0:T(8,128)S(1)} %copy.27.blocks, s32[4]{0:T(128)S(1)} %pad_add_fusion.at, f32[16,4,1920]{2,1,0:T(4,128)S(1)} %all-gather.1.x, f32[64,2048]{1,0:T(8,128)S(1)} %copy-done.8, f32[16,64,128]{2,1,0:T(8,128)S(1)} %copy-done.10), custom_call_target="tpu_custom_call" | custom-call | flops 20000000 | bytes 2000000 | tf_op jit(solution)/shard_map/pallas_call | solution.py:57
  (28 shorter events, 0.1 us)
Async XLA Ops:
  7.2 13.8 %copy-start.4 = (f32[16,64,128]{2,1,0:T(8,128)S(1)}, f32[16,64,128]{2,1,0:T(8,128)}, u32[]{:S(2)}) copy-start(f32[16,64,128]{2,1,0:T(8,128)} %panel.3) | copy-start | bytes 1572868
  7.2 13.8 %copy-start.3 = (f32[16,128,128]{2,1,0:T(8,128)S(1)}, f32[16,128,128]{2,1,0:T(8,128)}, u32[]{:S(2)}) copy-start(f32[16,128,128]{2,1,0:T(8,128)} %inverse.3) | copy-start | bytes 3145732
  7.2 13.8 %copy-start.5 = (f32[64,2048]{1,0:T(8,128)S(1)}, f32[64,2048]{1,0:T(8,128)}, u32[]{:S(2)}) copy-start(f32[64,2048]{1,0:T(8,128)} %shift.1) | copy-start | bytes 1572868
  7.2 0.9 copy-start.12
  8.1 0.7 copy-start.13
  8.8 11.7 %copy-start.16 = (s32[16,8]{0,1:T(8,128)S(1)}, s32[16,8]{0,1:T(8,128)}, u32[]{:S(2)}) copy-start(s32[16,8]{0,1:T(8,128)} %param.15) | copy-start | bytes 1540
  8.8 11.8 %copy-start.15 = (f32[64,32]{0,1:T(8,128)S(1)}, f32[64,32]{0,1:T(8,128)}, u32[]{:S(2)}) copy-start(f32[64,32]{0,1:T(8,128)} %param.12) | copy-start | bytes 24580
  8.8 12.2 %copy-start.14 = (f32[64,32]{0,1:T(8,128)S(1)}, f32[64,32]{0,1:T(8,128)}, u32[]{:S(2)}) copy-start(f32[64,32]{0,1:T(8,128)} %param.10) | copy-start | bytes 24580
  10.1 29.5 %all-to-all-start = ((f32[16,8,1568]{2,1,0:T(8,128)}), f32[16,8,1568]{2,1,0:T(8,128)S(1)}, u32[]{:S(2)}, u32[]{:S(2)}) async-start(f32[16,8,1568]{2,1,0:T(8,128)} %shard_map.104), calls=%async_computation | async-start | bytes 1703936 | tf_op jit(solution)/shard_map/all_to_all | solution.py:294
  20.5 78.6 %all-gather.4.cloned.1.call-start = ((), (), s32[]{:S(2)}) async-start(), calls=%async_computation.4 | async-start | bytes 6893568 | tf_op jit(solution)/shard_map/all_gather | solution.py:319
  28.0 0.8 copy-start.11
  39.6 17.5 %copy-start.6 = (f32[64,2048]{1,0:T(8,128)S(1)}, f32[64,2048]{1,0:T(8,128)}, u32[]{:S(2)}) copy-start(f32[64,2048]{1,0:T(8,128)} %noise.1) | copy-start | bytes 1572868
  42.4 6.2 %collective-permute-start = (f32[8,4,2048]{2,1,0:T(4,128)S(1)}, f32[8,4,2048]{2,1,0:T(4,128)}, u32[]{:S(2)}, u32[]{:S(2)}) collective-permute-start(f32[8,4,2048]{2,1,0:T(4,128)S(1)} %dynamic-slice_bitcast_fusion), channel_id=1, source_target_pairs={{0,4},{4,0},{1,5},{5,1},{2,6},{6,2},{3,7},{7,3},{8,12},{12,8},{9,1... | collective-permute-start | bytes 786440 | tf_op jit(solution)/shard_map/ppermute | solution.py:325
  50.3 19.7 %all-to-all-start.1 = ((f32[8,4,2048]{2,1,0:T(4,128)}), f32[8,4,2048]{2,1,0:T(4,128)S(1)}, u32[]{:S(2)}, u32[]{:S(2)}) async-start(f32[8,4,2048]{2,1,0:T(4,128)} %bitcast_add_fusion), calls=%async_computation.1 | async-start | bytes 524288 | tf_op jit(solution)/shard_map/all_to_all | solution.py:326
  60.1 0.8 copy-start.9
  60.9 43.9 %copy-start.7 = (f32[64,2048]{1,0:T(8,128)}, f32[64,2048]{1,0:T(8,128)S(1)}, u32[]{:S(2)}) copy-start(f32[64,2048]{1,0:T(8,128)S(1)} %get-tuple-element.40.base) | copy-start | bytes 1572868
  104.9 18.7 %all-to-all-start.2 = ((f32[8,4,1792]{2,1,0:T(4,128)}), f32[8,4,1792]{2,1,0:T(4,128)S(1)}, u32[]{:S(2)}, u32[]{:S(2)}) async-start(f32[8,4,1792]{2,1,0:T(4,128)} %get-tuple-element.31), calls=%async_computation.2 | async-start | bytes 458752 | tf_op jit(solution)/shard_map/all_to_all | solution.py:351
  120.6 1.2 copy-start
  124.8 12.7 %all-to-all-start.3 = ((f32[8,4,1024]{2,1,0:T(4,128)}), f32[8,4,1024]{2,1,0:T(4,128)S(1)}, u32[]{:S(2)}, u32[]{:S(2)}) async-start(f32[8,4,1024]{2,1,0:T(4,128)} %shard_map.110), calls=%async_computation.3 | async-start | bytes 262144 | tf_op jit(solution)/shard_map/all_to_all | solution.py:367
  129.7 1.4 copy-start.1
  137.4 1.4 copy-start.2
  138.8 20.7 %copy-start.8 = (f32[64,2048]{1,0:T(8,128)S(1)}, f32[64,2048]{1,0:T(8,128)}, u32[]{:S(2)}) copy-start(f32[64,2048]{1,0:T(8,128)} %copy-done.7) | copy-start | bytes 1572868
  138.8 20.7 %copy-start.10 = (f32[16,64,128]{2,1,0:T(8,128)S(1)}, f32[16,64,128]{2,1,0:T(8,128)}, u32[]{:S(2)}) copy-start(f32[16,64,128]{2,1,0:T(8,128)} %copy-done.9) | copy-start | bytes 1572868
Sparse Core Ops, SparseCore 0:
  41.2 57.7 all-gather.3

commit v8 on v6

--- a/solution.py
+++ b/solution.py
@@ -169,15 +169,17 @@
         copy.wait()
     g2 = nt(w[:, 1536:], l2[:, :256])
     w = w[:, :1536] - nn(g2, l2[:, 256:])
-    for copy in copies1:
-        copy.wait()
-    g1 = nt(w[:, 1024:], l1[:, :512])
-    w = w[:, :1024] - nn(g1, l1[:, 512:])
+    r1 = w[:, 1024:]
+    w = w[:, :1024]
+    g1 = []
+    for q in range(4):
+        copies1[q].wait()
+        g1.append(nt(r1, l1[q * 128 : (q + 1) * 128, :512]))
+        w = w - nn(g1[q], l1[q * 128 : (q + 1) * 128, 512:])
     for d in range(8):
         send_out[d, :, :1024] = w
         for q in range(4):
-            lanes = slice(q * 128, (q + 1) * 128)
-            send_out[d, :, 1024 + q * 128 : 1152 + q * 128] = g1[:, lanes] + jnp.where(zq == q, noise[1], 0.0)
+            send_out[d, :, 1024 + q * 128 : 1152 + q * 128] = g1[q] + jnp.where(zq == q, noise[1], 0.0)
         for p in range(2):
             lanes = slice(p * 128, (p + 1) * 128)
             send_out[d, :, 1536 + p * 128 : 1664 + p * 128] = g2[:, lanes] + jnp.where(zq % 2 == p, noise[2], 0.0)
@@ -227,14 +229,17 @@
     x0 = got0[0]
     for d in range(1, 8):
         x0 = x0 + got0[d]
-    x_out[:, :1024] = x0
-    x_out[:, 1024:1536] = rest[:, :512] + nt(x0, upper[...])
-    x_out[:, 1536:] = rest[:, 512:] + nt(x0, lower[...])
+    x1 = rest[:, :512] + nt(x0, upper[...])
+    x2 = rest[:, 512:] + nt(x0, lower[...])
+    for d in range(8):
+        x_out[d, :, :1024] = x0
+        x_out[d, :, 1024:1536] = x1
+        x_out[d, :, 1536:] = x2
 
 
 def leaf_backward_kernel(blocks, at, x, base, w, leaf_out, sep_out, rows_s, cols_s):
     for g in range(PLANE):
-        rows_s[g * GROUP : (g + 1) * GROUP, :] = x[g]
+        rows_s[g * GROUP : (g + 1) * GROUP, :] = x[g % 2, g // 2]
     for c in range(ANC // TILE):
         cols_s[c * TILE : (c + 1) * TILE, :] = rows_s[:, c * TILE : (c + 1) * TILE].T
     for k in range(LEVELS):
@@ -360,13 +365,14 @@
     )
     x = call(
         backward_kernel,
-        f32(GROUP, ANC),
+        f32(8, GROUP, ANC),
         [got0, rest, upper, lower],
         flops=20_000_000,
         nbytes=4_000_000,
         vmem=16,
     )
-    gathered = lax.all_gather(x, yc, axis=0, tiled=False)
+    x = lax.all_to_all(x, "y", 0, 0)
+    gathered = lax.all_gather(x, "core", axis=0, tiled=False)
 
     leaf_out, sep_t = call(
         leaf_backward_kernel,

time: 169 us -> 169 us (level)
    all_gather x1, blocking collectives: 19.4 us -> 5.88 us  [body(): gathered = lax.all_gather(x, 'core', axis=0, tiled=False)]
    all_to_all x0 -> x1, blocking collectives: none -> 13.1 us  [body(): x = lax.all_to_all(x, 'y', 0, 0)]
where the time goes in v8:
time: 169 us; the launch traced here: 168 us
  waiting for transfers between devices  55.4 us (33%)
  Pallas kernels  34.8 us (21%)
  starting transfers between devices  33.7 us (20%)
  blocking collectives  19 us (11%)
  between operations  14.3 us (8%)
  local copies, waits for them, and re-layouts  8.81 us (5%)
  other arithmetic  2 us (1%)
    pallas_call x10, Pallas kernels, call(): pl.pallas_call(kernel, out_shape=outs, in_specs=[pl.BlockSpec(memory_spac...  34.8 us
    all_gather x1, waiting for transfers between devices, body(): path = lax.all_gather(packed, yc, axis=0, tiled=True)  28.6 us
    all_to_all x1, blocking collectives, body(): x = lax.all_to_all(x, 'y', 0, 0)  13.1 us
    all_to_all x1, waiting for transfers between devices, body(): quad = lax.all_to_all(copies, ('zq', 'rhs'), 0, 0)  10.7 us
    all_to_all x1, starting transfers between devices, body(): quad = lax.all_to_all(copies, ('zq', 'rhs'), 0, 0)  10.4 us
    all_to_all x1, waiting for transfers between devices, body(): pay = lax.all_to_all(pay, 'y', 0, 0)  9.1 us
    all_to_all x1, starting transfers between devices, body(): got = lax.all_to_all(send, zz, 0, 0)  8.18 us
    all_to_all x1, starting transfers between devices, body(): pay = lax.all_to_all(pay, 'y', 0, 0)  6.82 us
  transfers between devices with their start and end apart: 6, of which 6 were waited for; matrix products, arithmetic and copies ran while one was open for 3% of the time, Pallas kernels for 12%

profile of v8, /device:TPU:1, one launch (start us, length us, event | category | flops | bytes accessed | tf_op | source)
XLA Modules:
  0.0 168.1 jit_solution(734296584852431205)
XLA Ops:
  7.2 0.9 copy-done.11
  8.1 0.7 copy-done.12
  8.8 1.1 shard_map.104
  10.0 10.4 %all-to-all-start = ((f32[16,8,1568]{2,1,0:T(8,128)}), f32[16,8,1568]{2,1,0:T(8,128)S(1)}, u32[]{:S(2)}, u32[]{:S(2)}) async-start(f32[16,8,1568]{2,1,0:T(8,128)} %shard_map.104), calls=%async_computation | async-start | bytes 1703936 | tf_op jit(solution)/shard_map/all_to_all | solution.py:281
  20.4 0.0 all-gather.3.cloned.1.call-start
  20.5 0.1 copy.27.blocks
  20.5 0.1 copy.22
  20.6 0.1 pad.2.clone
  20.7 0.1 pad_add_fusion.at
  20.8 0.1 maximum_maximum_fusion.sep_noise
  20.9 0.0 copy-done.4
  20.9 0.0 copy-done.1
  20.9 0.0 copy-done.13
  20.9 7.0 %shard_map.105 = (f32[64,2048]{1,0:T(8,128)S(1)}, f32[64,2048]{1,0:T(8,128)S(1)}) custom-call(s32[16,8]{1,0:T(8,128)S(1)} %copy.27.blocks, s32[4]{0:T(128)S(1)} %pad_add_fusion.at, f32[64,2048]{1,0:T(8,128)S(1)} %copy-done.4, f32[32,64]{1,0:T(8,128)S(1)} %bitcast.17, f32[64,128]{1,0:T(8,128)S(1)} %maximum_maximum_fusion.sep_noise, ...), custom_call_target="tpu_custom_call" | custom-call | flops 50000000 | bytes 3000000 | tf_op jit(solution)/shard_map/pallas_call | solution.py:57
  27.9 0.8 copy-done.10
  28.7 0.1 pad_add_fusion.1.place
  28.8 10.7 %all-to-all-done.quad = f32[16,8,1568]{2,1,0:T(8,128)S(1)} async-done(((f32[16,8,1568]{2,1,0:T(8,128)}), f32[16,8,1568]{2,1,0:T(8,128)S(1)}, u32[]{:S(2)}, u32[]{:S(2)}) %all-to-all-start) | async-done | bytes 802848 | tf_op jit(solution)/shard_map/all_to_all | solution.py:281
  39.5 1.5 shard_map.106
  41.0 0.0 all-gather.3.cloned.1.call-update
  41.0 1.2 reshape.13
  42.2 4.9 %collective-permute-start = (f32[8,4,2048]{2,1,0:T(4,128)S(1)}, f32[8,4,2048]{2,1,0:T(4,128)}, u32[]{:S(2)}, u32[]{:S(2)}) collective-permute-start(f32[8,4,2048]{2,1,0:T(4,128)S(1)} %dynamic-slice_bitcast_fusion), channel_id=1, source_target_pairs={{0,4},{4,0},{1,5},{5,1},{2,6},{6,2},{3,7},{7,3},{8,12},{12,8},{9,1... | collective-permute-start | bytes 786440 | tf_op jit(solution)/shard_map/ppermute | solution.py:312
  47.2 1.3 collective-permute-done
  48.4 1.7 %bitcast_add_fusion = f32[8,4,2048]{2,1,0:T(4,128)} fusion(f32[8,4,2048]{2,1,0:T(4,128)} %collective-permute-done, f32[8,2,4,2048]{3,2,1,0:T(4,128)S(1)} %reshape.13, s32[]{:T(128)S(6)} %select_n.47), kind=kLoop, calls=%fused_computation | loop fusion | flops 65536 | bytes 786436 | tf_op jit(solution)/shard_map/add | solution.py:312
  50.2 6.8 %all-to-all-start.1 = ((f32[8,4,2048]{2,1,0:T(4,128)}), f32[8,4,2048]{2,1,0:T(4,128)S(1)}, u32[]{:S(2)}, u32[]{:S(2)}) async-start(f32[8,4,2048]{2,1,0:T(4,128)} %bitcast_add_fusion), calls=%async_computation.1 | async-start | bytes 524288 | tf_op jit(solution)/shard_map/all_to_all | solution.py:313
  57.0 3.0 %shard_map.107 = (f32[64,2048]{1,0:T(8,128)S(1)}, f32[16,64,128]{2,1,0:T(8,128)S(1)}) custom-call(f32[64,2048]{1,0:T(8,128)S(1)} %get-tuple-element.25.lf, f32[64,2048]{1,0:T(8,128)S(1)} %copy-done.5, f32[16,128,128]{2,1,0:T(8,128)S(1)} %copy-done, f32[16,64,128]{2,1,0:T(8,128)S(1)} %copy-done.1), custom_call_target="tpu_custom_call" | custom-call | flops 70000000 | bytes 4000000 | tf_op jit(solution)/shard_map/pallas_call | solution.py:57
  60.0 0.8 copy-done.8
  60.8 9.1 %all-to-all-done.1 = f32[8,4,2048]{2,1,0:T(4,128)S(1)} async-done(((f32[8,4,2048]{2,1,0:T(4,128)}), f32[8,4,2048]{2,1,0:T(4,128)S(1)}, u32[]{:S(2)}, u32[]{:S(2)}) %all-to-all-start.1) | async-done | bytes 262176 | tf_op jit(solution)/shard_map/all_to_all | solution.py:313
  69.9 0.1 reshape.14
  70.1 0.1 copy.26
  70.2 0.2 reshape.15.noise
  70.4 28.6 %all-gather.3.cloned.1.call-done.source = f32[128,12672]{1,0:T(8,128)} async-done(((f32[8,12672]{1,0:T(8,128)}), f32[128,12672]{1,0:T(8,128)}) %all-gather.3.cloned.1.call-update) | async-done | bytes 6488080 | tf_op jit(solution)/shard_map/all_gather | solution.py:306
  99.0 6.4 %shard_map.108 = (f32[8,4,1792]{2,1,0:T(4,128)}, f32[4,128]{1,0:T(4,128)S(1)}) custom-call(s32[2]{0:T(128)S(1)} %pad_add_fusion.1.place, f32[4,1920]{1,0:T(4,128)S(1)} %slice_reduce_fusion.v, f32[4,4,128]{2,1,0:T(4,128)S(1)} %reshape.15.noise, f32[128,12672]{1,0:T(8,128)} %all-gather.3.cloned.1.call-done.source), custom_call_target="tpu_custom_call" | custom-call | flops 12000000 | bytes 6500000 | tf_op jit(solution)/shard_map/pallas_call | solution.py:57
  105.3 0.0 copy-done.6
  105.3 8.2 %all-to-all-start.2 = ((f32[8,4,1792]{2,1,0:T(4,128)}), f32[8,4,1792]{2,1,0:T(4,128)S(1)}, u32[]{:S(2)}, u32[]{:S(2)}) async-start(f32[8,4,1792]{2,1,0:T(4,128)} %get-tuple-element.30), calls=%async_computation.2 | async-start | bytes 458752 | tf_op jit(solution)/shard_map/all_to_all | solution.py:338
  113.5 1.1 slice.11.path
  114.6 3.7 %shard_map.109.upper = f32[512,1024]{1,0:T(8,128)S(1)} custom-call(f32[128,12672]{1,0:T(8,128)} %all-gather.3.cloned.1.call-done.source), custom_call_target="tpu_custom_call" | custom-call | flops 1600000000 | bytes 10000000 | tf_op jit(solution)/shard_map/pallas_call | solution.py:57
  118.3 5.7 %all-to-all-done.2.got = f32[8,4,1792]{2,1,0:T(4,128)S(1)} async-done(((f32[8,4,1792]{2,1,0:T(4,128)}), f32[8,4,1792]{2,1,0:T(4,128)S(1)}, u32[]{:S(2)}, u32[]{:S(2)}) %all-to-all-start.2) | async-done | bytes 229408 | tf_op jit(solution)/shard_map/all_to_all | solution.py:338
  124.0 1.2 shard_map.110
  125.2 3.4 %all-to-all-start.3 = ((f32[8,4,1024]{2,1,0:T(4,128)}), f32[8,4,1024]{2,1,0:T(4,128)S(1)}, u32[]{:S(2)}, u32[]{:S(2)}) async-start(f32[8,4,1024]{2,1,0:T(4,128)} %shard_map.110), calls=%async_computation.3 | async-start | bytes 262144 | tf_op jit(solution)/shard_map/all_to_all | solution.py:354
  128.6 6.6 %shard_map.111 = (f32[4,896]{1,0:T(4,128)S(1)}, f32[384,1024]{1,0:T(8,128)S(1)}) custom-call(s32[2]{0:T(128)S(1)} %pad_add_fusion.1.place, f32[8,4,1792]{2,1,0:T(4,128)S(1)} %all-to-all-done.2.got, f32[4,128]{1,0:T(4,128)S(1)} %get-tuple-element.34.g3, f32[512,1024]{1,0:T(8,128)S(1)} %shard_map.109.upper, f32[128,12672]{1,0:T(8,128)} %all-gather.3.cloned.1.call-done.source), custom_call_target="tpu_custom_call" | custom-call | flops 2200000000 | bytes 10000000 | tf_op jit(solution)/shard_map/pallas_call | solution.py:57
  135.2 0.0 copy-start.2
  135.2 1.2 copy-done.2
  136.4 0.1 all-to-all-done.3.got0
  136.4 1.4 copy-done.3
  137.8 1.5 shard_map.112
  139.4 13.1 %all_to_all.25 = f32[8,4,1920]{2,1,0:T(4,128)S(1)} all-to-all(f32[8,4,1920]{2,1,0:T(4,128)S(1)} %shard_map.112), channel_id=1, replica_groups=mesh['zh'=2,'zq'=4,'y'=8,'core'=2,'rhs'=4] {'y'}, dimensions={0} | all-to-all | bytes 491520 | tf_op jit(solution)/shard_map/all_to_all | solution.py:374
  152.5 5.9 %all-gather = f32[16,4,1920]{2,1,0:T(4,128)S(1)} all-gather(f32[8,4,1920]{2,1,0:T(4,128)S(1)} %all_to_all.25), channel_id=2, replica_groups=mesh['zh'=2,'zq'=4,'y'=8,'core'=2,'rhs'=4] {'core'}, dimensions={0}, use_global_device_ids=true | all-gather | bytes 737280 | tf_op jit(solution)/shard_map/all_gather | solution.py:375
  158.4 2.9 %shard_map.113 = (f32[64,2048]{1,0:T(8,128)}, f32[32,64]{1,0:T(8,128)}) custom-call(s32[16,8]{1,0:T(8,128)S(1)} %copy.27.blocks, s32[4]{0:T(128)S(1)} %pad_add_fusion.at, f32[2,8,4,1920]{3,2,1,0:T(4,128)S(1)} %bitcast.16, f32[64,2048]{1,0:T(8,128)S(1)} %copy-done.7, f32[16,64,128]{2,1,0:T(8,128)S(1)} %copy-done.9), custom_call_target="tpu_custom_call" | custom-call | flops 20000000 | bytes 2000000 | tf_op jit(solution)/shard_map/pallas_call | solution.py:57
  (27 shorter events, 0.1 us)
Async XLA Ops:
  7.2 13.7 %copy-start.4 = (f32[64,2048]{1,0:T(8,128)S(1)}, f32[64,2048]{1,0:T(8,128)}, u32[]{:S(2)}) copy-start(f32[64,2048]{1,0:T(8,128)} %shift.1) | copy-start | bytes 1572868
  7.2 13.7 %copy-start = (f32[16,128,128]{2,1,0:T(8,128)S(1)}, f32[16,128,128]{2,1,0:T(8,128)}, u32[]{:S(2)}) copy-start(f32[16,128,128]{2,1,0:T(8,128)} %inverse.5) | copy-start | bytes 3145732
  7.2 13.7 %copy-start.1 = (f32[16,64,128]{2,1,0:T(8,128)S(1)}, f32[16,64,128]{2,1,0:T(8,128)}, u32[]{:S(2)}) copy-start(f32[16,64,128]{2,1,0:T(8,128)} %panel.3) | copy-start | bytes 1572868
  7.2 0.9 copy-start.11
  8.1 0.7 copy-start.12
  8.8 11.6 %copy-start.15 = (s32[16,8]{0,1:T(8,128)S(1)}, s32[16,8]{0,1:T(8,128)}, u32[]{:S(2)}) copy-start(s32[16,8]{0,1:T(8,128)} %param.15) | copy-start | bytes 1540
  8.8 11.7 %copy-start.14 = (f32[64,32]{0,1:T(8,128)S(1)}, f32[64,32]{0,1:T(8,128)}, u32[]{:S(2)}) copy-start(f32[64,32]{0,1:T(8,128)} %param.12) | copy-start | bytes 24580
  8.8 12.1 %copy-start.13 = (f32[64,32]{0,1:T(8,128)S(1)}, f32[64,32]{0,1:T(8,128)}, u32[]{:S(2)}) copy-start(f32[64,32]{0,1:T(8,128)} %param.10) | copy-start | bytes 24580
  10.0 29.5 %all-to-all-start = ((f32[16,8,1568]{2,1,0:T(8,128)}), f32[16,8,1568]{2,1,0:T(8,128)S(1)}, u32[]{:S(2)}, u32[]{:S(2)}) async-start(f32[16,8,1568]{2,1,0:T(8,128)} %shard_map.104), calls=%async_computation | async-start | bytes 1703936 | tf_op jit(solution)/shard_map/all_to_all | solution.py:281
  20.4 78.6 %all-gather.3.cloned.1.call-start = ((), (), s32[]{:S(2)}) async-start(), calls=%async_computation.5 | async-start | bytes 6893568 | tf_op jit(solution)/shard_map/all_gather | solution.py:306
  27.9 0.8 copy-start.10
  39.5 17.5 %copy-start.5 = (f32[64,2048]{1,0:T(8,128)S(1)}, f32[64,2048]{1,0:T(8,128)}, u32[]{:S(2)}) copy-start(f32[64,2048]{1,0:T(8,128)} %noise.1) | copy-start | bytes 1572868
  42.2 6.2 %collective-permute-start = (f32[8,4,2048]{2,1,0:T(4,128)S(1)}, f32[8,4,2048]{2,1,0:T(4,128)}, u32[]{:S(2)}, u32[]{:S(2)}) collective-permute-start(f32[8,4,2048]{2,1,0:T(4,128)S(1)} %dynamic-slice_bitcast_fusion), channel_id=1, source_target_pairs={{0,4},{4,0},{1,5},{5,1},{2,6},{6,2},{3,7},{7,3},{8,12},{12,8},{9,1... | collective-permute-start | bytes 786440 | tf_op jit(solution)/shard_map/ppermute | solution.py:312
  50.2 19.7 %all-to-all-start.1 = ((f32[8,4,2048]{2,1,0:T(4,128)}), f32[8,4,2048]{2,1,0:T(4,128)S(1)}, u32[]{:S(2)}, u32[]{:S(2)}) async-start(f32[8,4,2048]{2,1,0:T(4,128)} %bitcast_add_fusion), calls=%async_computation.1 | async-start | bytes 524288 | tf_op jit(solution)/shard_map/all_to_all | solution.py:313
  60.0 0.8 copy-start.8
  60.8 44.5 %copy-start.6 = (f32[64,2048]{1,0:T(8,128)}, f32[64,2048]{1,0:T(8,128)S(1)}, u32[]{:S(2)}) copy-start(f32[64,2048]{1,0:T(8,128)S(1)} %get-tuple-element.38.base) | copy-start | bytes 1572868
  105.3 18.7 %all-to-all-start.2 = ((f32[8,4,1792]{2,1,0:T(4,128)}), f32[8,4,1792]{2,1,0:T(4,128)S(1)}, u32[]{:S(2)}, u32[]{:S(2)}) async-start(f32[8,4,1792]{2,1,0:T(4,128)} %get-tuple-element.30), calls=%async_computation.2 | async-start | bytes 458752 | tf_op jit(solution)/shard_map/all_to_all | solution.py:338
  125.2 11.2 %all-to-all-start.3 = ((f32[8,4,1024]{2,1,0:T(4,128)}), f32[8,4,1024]{2,1,0:T(4,128)S(1)}, u32[]{:S(2)}, u32[]{:S(2)}) async-start(f32[8,4,1024]{2,1,0:T(4,128)} %shard_map.110), calls=%async_computation.3 | async-start | bytes 262144 | tf_op jit(solution)/shard_map/all_to_all | solution.py:354
  135.2 1.2 copy-start.2
  136.4 1.4 copy-start.3
  137.8 20.5 %copy-start.7 = (f32[64,2048]{1,0:T(8,128)S(1)}, f32[64,2048]{1,0:T(8,128)}, u32[]{:S(2)}) copy-start(f32[64,2048]{1,0:T(8,128)} %copy-done.6) | copy-start | bytes 1572868
  137.8 20.5 %copy-start.9 = (f32[16,64,128]{2,1,0:T(8,128)S(1)}, f32[16,64,128]{2,1,0:T(8,128)}, u32[]{:S(2)}) copy-start(f32[16,64,128]{2,1,0:T(8,128)} %copy-done.8) | copy-start | bytes 1572868
Sparse Core Ops, SparseCore 0:
  41.1 57.7 all-gather.2

commit v9 on v6

--- a/solution.py
+++ b/solution.py
@@ -72,32 +72,32 @@
 
 
 def copies_kernel(inverse, coupling, out):
-    for d in range(16):
+    for d in range(4):
         out[d, :, :480] = inverse[...]
         out[d, :, 480:] = coupling[...]
 
 
-def pack_kernel(place, quad, out):
-    def rows_of(plane):
-        parts = [quad[plane * 4 + x] for x in range(4)]
-        inv = jnp.concatenate([p[:, :480] for p in parts], axis=1)
-        cou = jnp.concatenate([p[:, 480:] for p in parts], axis=1)
-        return inv, cou
-
+def rows_kernel(parts, send_out, own_out):
+    inv = jnp.concatenate([parts[x, :, :480] for x in range(4)], axis=1)
+    cou = jnp.concatenate([parts[x, :, 480:] for x in range(4)], axis=1)
+    for d in range(4):
+        send_out[d, :, :512] = inv[:, 1024:1536]
+        send_out[d, :, 512:1536] = cou[:, :1024]
+        send_out[d, :, 1536:1792] = inv[:, 1536:1792]
+        send_out[d, :, 1792:] = cou[:, 1024:2560]
+    own_out[:, :128] = inv[:, 1792:]
+    own_out[:, 128:1920] = cou[:, 2560:]
+    own_out[:, 1920:] = inv[:, :1024]
+
+
+def pack_kernel(place, quad, own, out):
     for q in range(4):
-        inv, cou = rows_of(q)
-        out[:, q * 1536 : q * 1536 + 512] = inv[:, 1024:1536]
-        out[:, q * 1536 + 512 : (q + 1) * 1536] = cou[:, :1024]
+        out[:, q * 1536 : (q + 1) * 1536] = quad[q, :, :1536]
     pair = place[0] // 2 * 2
     for p in range(2):
-        inv, cou = rows_of(pair + p)
         at = L2_AT + p * 1792
-        out[:, at : at + 256] = inv[:, 1536:1792]
-        out[:, at + 256 : at + 1792] = cou[:, 1024:2560]
-    inv, cou = rows_of(place[0])
-    out[:, L3_AT : L3_AT + 128] = inv[:, 1792:]
-    out[:, L3_AT + 128 : L0_AT] = cou[:, 2560:]
-    out[:, L0_AT:] = inv[:, :1024]
+        out[:, at : at + 1792] = quad[pair + p, :, 1536:]
+    out[:, L3_AT:] = own[...]
 
 
 def vm(*shape):
@@ -272,8 +272,10 @@
     place = jnp.stack([zq, zh]).astype(jnp.int32)
     at = jnp.stack([STARTS[k] + dev % (128 >> k) * SEP_DEV for k in range(LEVELS)]).astype(jnp.int32)
 
-    copies = call(copies_kernel, f32(16, 8, 1568), [sep_inverse, sep_coupling], nbytes=900_000)
-    quad = lax.all_to_all(copies, ("zq", "rhs"), 0, 0)
+    copies = call(copies_kernel, f32(4, 8, 1568), [sep_inverse, sep_coupling], nbytes=300_000)
+    parts = lax.all_to_all(copies, "rhs", 0, 0)
+    pieces, own = call(rows_kernel, [f32(4, 8, 3328), f32(8, 2944)], [parts], nbytes=900_000)
+    quad = lax.all_to_all(pieces, "zq", 0, 0)
     first = lax.axis_index("core") == 0
     noise_slot = jnp.concatenate(
         [jnp.where(first, sep_noise, 0.0), jnp.where(first, 0.0, sep_noise), jnp.zeros((SAMPLES, 64), jnp.float32)],
@@ -297,7 +299,7 @@
         nbytes=3_000_000,
     )
     quad, pay = lax.optimization_barrier((quad, pay))
-    packed = call(pack_kernel, f32(8, PACK), [place, quad], smem=1, nbytes=1_500_000)
+    packed = call(pack_kernel, f32(8, PACK), [place, quad, own], smem=1, nbytes=1_500_000)
     path = lax.all_gather(packed, yc, axis=0, tiled=True)
 
     core = lax.axis_index("core")

time: 169 us -> 166 us (0.982)
  waiting for transfers between devices: 55.4 us -> 47.1 us
  local copies, waits for them, and re-layouts: 8.81 us -> 12.7 us
    all_to_all x1 -> x2, waiting for transfers between devices: 10.7 us -> 4.94 us  [the longest x1 3.63 us: body(): parts = lax.all_to_all(copies, 'rhs', 0, 0)]
    all_gather x1, waiting for transfers between devices: 28.6 us -> 25.2 us  [body(): path = lax.all_gather(packed, yc, axis=0, tiled=True)]
    unnamed x34 -> x30, local copies, waits for them, and re-layouts: 6.02 us -> 8.19 us
    all_to_all x1 -> x2, starting transfers between devices: 10.4 us -> 11.8 us  [the longest x1 6.98 us: body(): quad = lax.all_to_all(pieces, 'zq', 0, 0)]
    pallas_call x10 -> x11, Pallas kernels: 34.2 us -> 34.6 us  [call(): pl.pallas_call(kernel, out_shape=outs, in_specs=[pl.BlockSpec(memory_spac...]
  transfers between devices with their start and end apart: 6 -> 7, of which waited for: 6 -> 7; matrix products, arithmetic and copies ran while one was open for 3% -> 5% of each run, Pallas kernels for 12% -> 12%
where the time goes in v9:
time: 166 us; the launch traced here: 165 us
  waiting for transfers between devices  47.1 us (28%)
  starting transfers between devices  35 us (21%)
  Pallas kernels  34.6 us (21%)
  blocking collectives  19.7 us (12%)
  between operations  14.2 us (9%)
  local copies, waits for them, and re-layouts  12.7 us (8%)
  other arithmetic  2 us (1%)
    pallas_call x11, Pallas kernels, call(): pl.pallas_call(kernel, out_shape=outs, in_specs=[pl.BlockSpec(memory_spac...  34.6 us
    all_gather x1, waiting for transfers between devices, body(): path = lax.all_gather(packed, yc, axis=0, tiled=True)  25.2 us
    all_gather x1, blocking collectives, body(): gathered = lax.all_gather(x, yc, axis=0, tiled=False)  19.7 us
    all_to_all x1, waiting for transfers between devices, body(): pay = lax.all_to_all(pay, 'y', 0, 0)  10 us
    unnamed x30, local copies, waits for them, and re-layouts  8.19 us
    all_to_all x1, starting transfers between devices, body(): got = lax.all_to_all(send, zz, 0, 0)  7.11 us
    all_to_all x1, starting transfers between devices, body(): quad = lax.all_to_all(pieces, 'zq', 0, 0)  6.98 us
    all_to_all x1, starting transfers between devices, body(): pay = lax.all_to_all(pay, 'y', 0, 0)  6.82 us
  transfers between devices with their start and end apart: 7, of which 7 were waited for; matrix products, arithmetic and copies ran while one was open for 5% of the time, Pallas kernels for 12%

profile of v9, /device:TPU:1, one launch (start us, length us, event | category | flops | bytes accessed | tf_op | source)
XLA Modules:
  0.0 165.3 jit_solution(6174417768909294543)
XLA Ops:
  7.2 0.0 copy-start.4
  7.2 0.0 copy-start
  7.2 0.9 copy-done.11
  8.1 0.7 copy-done.13
  8.8 0.8 shard_map.104
  9.6 4.8 %all-to-all-start = ((f32[4,8,1568]{2,1,0:T(8,128)}), f32[4,8,1568]{2,1,0:T(8,128)S(1)}, u32[]{:S(2)}, u32[]{:S(2)}) async-start(f32[4,8,1568]{2,1,0:T(8,128)} %shard_map.104), calls=%async_computation | async-start | bytes 425984 | tf_op jit(solution)/shard_map/all_to_all | solution.py:276
  14.5 0.8 copy.27.blocks
  15.2 0.8 copy.22
  16.0 0.1 pad.2.clone
  16.1 3.6 %all-to-all-done.parts = f32[4,8,1568]{2,1,0:T(8,128)S(1)} async-done(((f32[4,8,1568]{2,1,0:T(8,128)}), f32[4,8,1568]{2,1,0:T(8,128)S(1)}, u32[]{:S(2)}, u32[]{:S(2)}) %all-to-all-start) | async-done | bytes 200736 | tf_op jit(solution)/shard_map/all_to_all | solution.py:276
  19.7 0.9 shard_map.105
  20.6 7.0 %all-to-all-start.1 = ((f32[4,8,3328]{2,1,0:T(8,128)}), f32[4,8,3328]{2,1,0:T(8,128)S(1)}, u32[]{:S(2)}, u32[]{:S(2)}) async-start(f32[4,8,3328]{2,1,0:T(8,128)} %get-tuple-element.24), calls=%async_computation.1 | async-start | bytes 851968 | tf_op jit(solution)/shard_map/all_to_all | solution.py:278
  27.6 0.1 pad_add_fusion.at
  27.7 0.1 maximum_maximum_fusion.sep_noise
  27.8 7.0 %shard_map.106 = (f32[64,2048]{1,0:T(8,128)S(1)}, f32[64,2048]{1,0:T(8,128)S(1)}) custom-call(s32[16,8]{1,0:T(8,128)S(1)} %copy.27.blocks, s32[4]{0:T(128)S(1)} %pad_add_fusion.at, f32[64,2048]{1,0:T(8,128)S(1)} %copy-done.4, f32[32,64]{1,0:T(8,128)S(1)} %bitcast.17, f32[64,128]{1,0:T(8,128)S(1)} %maximum_maximum_fusion.sep_noise, ...), custom_call_target="tpu_custom_call" | custom-call | flops 50000000 | bytes 3000000 | tf_op jit(solution)/shard_map/pallas_call | solution.py:57
  34.8 0.8 copy-done.10
  35.6 0.1 pad_add_fusion.1.place
  35.6 1.3 all-to-all-done.1.quad
  36.9 1.3 shard_map.107
  38.2 0.0 all-gather.4.cloned.1.call-update
  38.3 2.0 %reshape.13 = f32[8,2,4,2048]{3,2,1,0:T(4,128)} reshape(f32[64,2048]{1,0:T(8,128)} %copy-done.10) | data formatting | bytes 1048576 | tf_op jit(solution)/shard_map/reshape | solution.py:306
  40.2 1.0 dynamic-slice_bitcast_fusion
  41.2 5.9 %collective-permute-start = (f32[8,4,2048]{2,1,0:T(4,128)S(1)}, f32[8,4,2048]{2,1,0:T(4,128)S(1)}, u32[]{:S(2)}, u32[]{:S(2)}) collective-permute-start(f32[8,4,2048]{2,1,0:T(4,128)S(1)} %dynamic-slice_bitcast_fusion), channel_id=1, source_target_pairs={{0,4},{4,0},{1,5},{5,1},{2,6},{6,2},{3,7},{7,3},{8,12},{12,8},{9,1... | collective-permute-start | bytes 786440 | tf_op jit(solution)/shard_map/ppermute | solution.py:309
  47.1 1.1 collective-permute-done
  48.2 1.7 %bitcast_add_fusion = f32[8,4,2048]{2,1,0:T(4,128)} fusion(f32[8,4,2048]{2,1,0:T(4,128)S(1)} %collective-permute-done, f32[8,2,4,2048]{3,2,1,0:T(4,128)} %reshape.13, s32[]{:T(128)S(6)} %select_n.47), kind=kLoop, calls=%fused_computation | loop fusion | flops 65536 | bytes 786436 | tf_op jit(solution)/shard_map/add | solution.py:309
  50.0 6.8 %all-to-all-start.2 = ((f32[8,4,2048]{2,1,0:T(4,128)}), f32[8,4,2048]{2,1,0:T(4,128)S(1)}, u32[]{:S(2)}, u32[]{:S(2)}) async-start(f32[8,4,2048]{2,1,0:T(4,128)} %bitcast_add_fusion), calls=%async_computation.2 | async-start | bytes 524288 | tf_op jit(solution)/shard_map/all_to_all | solution.py:310
  56.8 3.0 %shard_map.108 = (f32[64,2048]{1,0:T(8,128)S(1)}, f32[16,64,128]{2,1,0:T(8,128)S(1)}) custom-call(f32[64,2048]{1,0:T(8,128)S(1)} %get-tuple-element.29.lf, f32[64,2048]{1,0:T(8,128)S(1)} %copy-done.5, f32[16,128,128]{2,1,0:T(8,128)S(1)} %copy-done, f32[16,64,128]{2,1,0:T(8,128)S(1)} %copy-done.1), custom_call_target="tpu_custom_call" | custom-call | flops 70000000 | bytes 4000000 | tf_op jit(solution)/shard_map/pallas_call | solution.py:57
  59.8 0.8 copy-done.6
  60.6 0.8 copy-done.8
  61.4 10.0 %all-to-all-done.2 = f32[8,4,2048]{2,1,0:T(4,128)S(1)} async-done(((f32[8,4,2048]{2,1,0:T(4,128)}), f32[8,4,2048]{2,1,0:T(4,128)S(1)}, u32[]{:S(2)}, u32[]{:S(2)}) %all-to-all-start.2) | async-done | bytes 262176 | tf_op jit(solution)/shard_map/all_to_all | solution.py:310
  71.4 0.1 reshape.14
  71.6 0.1 copy.26
  71.6 0.2 reshape.15.noise
  71.9 25.2 %all-gather.4.cloned.1.call-done.source = f32[128,12672]{1,0:T(8,128)} async-done(((f32[8,12672]{1,0:T(8,128)}), f32[128,12672]{1,0:T(8,128)}) %all-gather.4.cloned.1.call-update) | async-done | bytes 6488080 | tf_op jit(solution)/shard_map/all_gather | solution.py:303
  97.1 5.8 %shard_map.109 = (f32[8,4,1792]{2,1,0:T(4,128)}, f32[4,128]{1,0:T(4,128)S(1)}) custom-call(s32[2]{0:T(128)S(1)} %pad_add_fusion.1.place, f32[4,1920]{1,0:T(4,128)S(1)} %slice_reduce_fusion.v, f32[4,4,128]{2,1,0:T(4,128)S(1)} %reshape.15.noise, f32[128,12672]{1,0:T(8,128)} %all-gather.4.cloned.1.call-done.source), custom_call_target="tpu_custom_call" | custom-call | flops 12000000 | bytes 6500000 | tf_op jit(solution)/shard_map/pallas_call | solution.py:57
  102.9 7.1 %all-to-all-start.3 = ((f32[8,4,1792]{2,1,0:T(4,128)}), f32[8,4,1792]{2,1,0:T(4,128)S(1)}, u32[]{:S(2)}, u32[]{:S(2)}) async-start(f32[8,4,1792]{2,1,0:T(4,128)} %get-tuple-element.34), calls=%async_computation.3 | async-start | bytes 458752 | tf_op jit(solution)/shard_map/all_to_all | solution.py:335
  110.0 1.1 slice.11.path
  111.1 3.7 %shard_map.110.upper = f32[512,1024]{1,0:T(8,128)S(1)} custom-call(f32[128,12672]{1,0:T(8,128)} %all-gather.4.cloned.1.call-done.source), custom_call_target="tpu_custom_call" | custom-call | flops 1600000000 | bytes 10000000 | tf_op jit(solution)/shard_map/pallas_call | solution.py:57
  114.8 5.7 %all-to-all-done.3.got = f32[8,4,1792]{2,1,0:T(4,128)S(1)} async-done(((f32[8,4,1792]{2,1,0:T(4,128)}), f32[8,4,1792]{2,1,0:T(4,128)S(1)}, u32[]{:S(2)}, u32[]{:S(2)}) %all-to-all-start.3) | async-done | bytes 229408 | tf_op jit(solution)/shard_map/all_to_all | solution.py:335
  120.5 1.2 shard_map.111
  121.7 3.4 %all-to-all-start.4 = ((f32[8,4,1024]{2,1,0:T(4,128)}), f32[8,4,1024]{2,1,0:T(4,128)S(1)}, u32[]{:S(2)}, u32[]{:S(2)}) async-start(f32[8,4,1024]{2,1,0:T(4,128)} %shard_map.111), calls=%async_computation.4 | async-start | bytes 262144 | tf_op jit(solution)/shard_map/all_to_all | solution.py:351
  125.1 6.6 %shard_map.112 = (f32[4,896]{1,0:T(4,128)S(1)}, f32[384,1024]{1,0:T(8,128)S(1)}) custom-call(s32[2]{0:T(128)S(1)} %pad_add_fusion.1.place, f32[8,4,1792]{2,1,0:T(4,128)S(1)} %all-to-all-done.3.got, f32[4,128]{1,0:T(4,128)S(1)} %get-tuple-element.38.g3, f32[512,1024]{1,0:T(8,128)S(1)} %shard_map.110.upper, f32[128,12672]{1,0:T(8,128)} %all-gather.4.cloned.1.call-done.source), custom_call_target="tpu_custom_call" | custom-call | flops 2200000000 | bytes 10000000 | tf_op jit(solution)/shard_map/pallas_call | solution.py:57
  131.7 1.2 copy-done.2
  132.8 0.1 all-to-all-done.4.got0
  132.9 1.4 copy-done.3
  134.3 1.5 shard_map.113
  135.8 19.7 %all-gather.1.x = f32[16,4,1920]{2,1,0:T(4,128)S(1)} all-gather(f32[1,4,1920]{2,1,0:T(4,128)S(1)} %bitcast.16), channel_id=2, replica_groups=mesh['zh'=2,'zq'=4,'y'=8,'core'=2,'rhs'=4] {'y','core'}, dimensions={0}, use_global_device_ids=true | all-gather | bytes 522240 | tf_op jit(solution)/shard_map/all_gather | solution.py:371
  155.6 2.9 %shard_map.114 = (f32[64,2048]{1,0:T(8,128)}, f32[32,64]{1,0:T(8,128)}) custom-call(s32[16,8]{1,0:T(8,128)S(1)} %copy.27.blocks, s32[4]{0:T(128)S(1)} %pad_add_fusion.at, f32[16,4,1920]{2,1,0:T(4,128)S(1)} %all-gather.1.x, f32[64,2048]{1,0:T(8,128)S(1)} %copy-done.7, f32[16,64,128]{2,1,0:T(8,128)S(1)} %copy-done.9), custom_call_target="tpu_custom_call" | custom-call | flops 20000000 | bytes 2000000 | tf_op jit(solution)/shard_map/pallas_call | solution.py:57
  (25 shorter events, 0.1 us)
Async XLA Ops:
  7.2 20.6 %copy-start.4 = (f32[64,2048]{1,0:T(8,128)S(1)}, f32[64,2048]{1,0:T(8,128)}, u32[]{:S(2)}) copy-start(f32[64,2048]{1,0:T(8,128)} %shift.1) | copy-start | bytes 1572868
  7.2 20.6 %copy-start = (f32[16,128,128]{2,1,0:T(8,128)S(1)}, f32[16,128,128]{2,1,0:T(8,128)}, u32[]{:S(2)}) copy-start(f32[16,128,128]{2,1,0:T(8,128)} %inverse.5) | copy-start | bytes 3145732
  7.2 20.6 %copy-start.1 = (f32[16,64,128]{2,1,0:T(8,128)S(1)}, f32[16,64,128]{2,1,0:T(8,128)}, u32[]{:S(2)}) copy-start(f32[16,64,128]{2,1,0:T(8,128)} %panel.3) | copy-start | bytes 1572868
  7.2 0.9 copy-start.11
  8.1 0.7 copy-start.13
  8.8 18.9 %copy-start.12 = (f32[64,32]{0,1:T(8,128)S(1)}, f32[64,32]{0,1:T(8,128)}, u32[]{:S(2)}) copy-start(f32[64,32]{0,1:T(8,128)} %param.10) | copy-start | bytes 24580
  9.6 10.1 %all-to-all-start = ((f32[4,8,1568]{2,1,0:T(8,128)}), f32[4,8,1568]{2,1,0:T(8,128)S(1)}, u32[]{:S(2)}, u32[]{:S(2)}) async-start(f32[4,8,1568]{2,1,0:T(8,128)} %shard_map.104), calls=%async_computation | async-start | bytes 425984 | tf_op jit(solution)/shard_map/all_to_all | solution.py:276
  20.6 16.3 %all-to-all-start.1 = ((f32[4,8,3328]{2,1,0:T(8,128)}), f32[4,8,3328]{2,1,0:T(8,128)S(1)}, u32[]{:S(2)}, u32[]{:S(2)}) async-start(f32[4,8,3328]{2,1,0:T(8,128)} %get-tuple-element.24), calls=%async_computation.1 | async-start | bytes 851968 | tf_op jit(solution)/shard_map/all_to_all | solution.py:278
  27.6 69.5 %all-gather.4.cloned.1.call-start = ((), (), s32[]{:S(2)}) async-start(), calls=%async_computation.5 | async-start | bytes 6893568 | tf_op jit(solution)/shard_map/all_gather | solution.py:303
  34.8 0.8 copy-start.10
  36.9 19.9 %copy-start.5 = (f32[64,2048]{1,0:T(8,128)S(1)}, f32[64,2048]{1,0:T(8,128)}, u32[]{:S(2)}) copy-start(f32[64,2048]{1,0:T(8,128)} %noise.1) | copy-start | bytes 1572868
  41.2 7.0 %collective-permute-start = (f32[8,4,2048]{2,1,0:T(4,128)S(1)}, f32[8,4,2048]{2,1,0:T(4,128)S(1)}, u32[]{:S(2)}, u32[]{:S(2)}) collective-permute-start(f32[8,4,2048]{2,1,0:T(4,128)S(1)} %dynamic-slice_bitcast_fusion), channel_id=1, source_target_pairs={{0,4},{4,0},{1,5},{5,1},{2,6},{6,2},{3,7},{7,3},{8,12},{12,8},{9,1... | collective-permute-start | bytes 786440 | tf_op jit(solution)/shard_map/ppermute | solution.py:309
  50.0 21.4 %all-to-all-start.2 = ((f32[8,4,2048]{2,1,0:T(4,128)}), f32[8,4,2048]{2,1,0:T(4,128)S(1)}, u32[]{:S(2)}, u32[]{:S(2)}) async-start(f32[8,4,2048]{2,1,0:T(4,128)} %bitcast_add_fusion), calls=%async_computation.2 | async-start | bytes 524288 | tf_op jit(solution)/shard_map/all_to_all | solution.py:310
  59.8 0.8 copy-start.6
  60.6 0.8 copy-start.8
  102.9 17.6 %all-to-all-start.3 = ((f32[8,4,1792]{2,1,0:T(4,128)}), f32[8,4,1792]{2,1,0:T(4,128)S(1)}, u32[]{:S(2)}, u32[]{:S(2)}) async-start(f32[8,4,1792]{2,1,0:T(4,128)} %get-tuple-element.34), calls=%async_computation.3 | async-start | bytes 458752 | tf_op jit(solution)/shard_map/all_to_all | solution.py:335
  121.7 11.2 %all-to-all-start.4 = ((f32[8,4,1024]{2,1,0:T(4,128)}), f32[8,4,1024]{2,1,0:T(4,128)S(1)}, u32[]{:S(2)}, u32[]{:S(2)}) async-start(f32[8,4,1024]{2,1,0:T(4,128)} %shard_map.111), calls=%async_computation.4 | async-start | bytes 262144 | tf_op jit(solution)/shard_map/all_to_all | solution.py:351
  131.6 1.2 copy-start.2
  132.9 1.4 copy-start.3
  134.3 21.2 %copy-start.7 = (f32[64,2048]{1,0:T(8,128)S(1)}, f32[64,2048]{1,0:T(8,128)}, u32[]{:S(2)}) copy-start(f32[64,2048]{1,0:T(8,128)} %copy-done.6) | copy-start | bytes 1572868
  134.3 21.2 %copy-start.9 = (f32[16,64,128]{2,1,0:T(8,128)S(1)}, f32[16,64,128]{2,1,0:T(8,128)}, u32[]{:S(2)}) copy-start(f32[16,64,128]{2,1,0:T(8,128)} %copy-done.8) | copy-start | bytes 1572868
Sparse Core Ops, SparseCore 0:
  38.4 58.6 all-gather.3

commit v10 on v9

--- a/solution.py
+++ b/solution.py
@@ -52,14 +52,16 @@
     return [pl.BlockSpec(memory_space=pltpu.VMEM)] * n
 
 
-def call(kernel, outs, ins, smem=0, hbm=0, scratch=(), flops=0, nbytes=0, vmem=12):
+def call(kernel, outs, ins, smem=0, hbm=0, scratch=(), flops=0, nbytes=0, vmem=12, pin=False):
     many = isinstance(outs, (list, tuple))
+    held = len(ins) - hbm if pin else len(ins)
+    ins = list(ins[:held]) + [pltpu.with_memory_space_constraint(x, pltpu.HBM) for x in ins[held:]]
     return pl.pallas_call(
         kernel,
         out_shape=outs,
         in_specs=[pl.BlockSpec(memory_space=pltpu.SMEM)] * smem
         + vspec(len(ins) - smem - hbm)
-        + [pl.BlockSpec(memory_space=pl.ANY)] * hbm,
+        + [pl.BlockSpec(memory_space=pltpu.HBM if pin else pl.ANY)] * hbm,
         out_specs=tuple(vspec(len(outs))) if many else vspec(1)[0],
         scratch_shapes=list(scratch),
         compiler_params=pltpu.CompilerParams(vmem_limit_bytes=vmem * MIB),
@@ -71,7 +73,13 @@
     return jax.ShapeDtypeStruct(shape, jnp.float32)
 
 
-def copies_kernel(inverse, coupling, out):
+def copies_kernel(inverse_in, coupling_in, out, inverse, coupling, sems):
+    one = pltpu.make_async_copy(inverse_in, inverse, sems.at[0])
+    two = pltpu.make_async_copy(coupling_in, coupling, sems.at[1])
+    one.start()
+    two.start()
+    one.wait()
+    two.wait()
     for d in range(4):
         out[d, :, :480] = inverse[...]
         out[d, :, 480:] = coupling[...]
@@ -272,7 +280,15 @@
     place = jnp.stack([zq, zh]).astype(jnp.int32)
     at = jnp.stack([STARTS[k] + dev % (128 >> k) * SEP_DEV for k in range(LEVELS)]).astype(jnp.int32)
 
-    copies = call(copies_kernel, f32(4, 8, 1568), [sep_inverse, sep_coupling], nbytes=300_000)
+    copies = call(
+        copies_kernel,
+        f32(4, 8, 1568),
+        [sep_inverse, sep_coupling],
+        hbm=2,
+        pin=True,
+        scratch=[vm(8, 480), vm(8, 1088), pltpu.SemaphoreType.DMA((2,))],
+        nbytes=300_000,
+    )
     parts = lax.all_to_all(copies, "rhs", 0, 0)
     pieces, own = call(rows_kernel, [f32(4, 8, 3328), f32(8, 2944)], [parts], nbytes=900_000)
     quad = lax.all_to_all(pieces, "zq", 0, 0)

time: 166 us -> 166 us (level)
    unnamed x30 -> x26, local copies, waits for them, and re-layouts: 8.19 us -> 6.58 us
where the time goes in v10:
time: 166 us; the launch traced here: 165 us
  waiting for transfers between devices  47.1 us (28%)
  Pallas kernels  35.5 us (21%)
  starting transfers between devices  35 us (21%)
  blocking collectives  19.7 us (12%)
  between operations  14.2 us (9%)
  local copies, waits for them, and re-layouts  11.1 us (7%)
  other arithmetic  2 us (1%)
    pallas_call x11, Pallas kernels, call(): pl.pallas_call(kernel, out_shape=outs, in_specs=[pl.BlockSpec(memory_spac...  35.5 us
    all_gather x1, waiting for transfers between devices, body(): path = lax.all_gather(packed, yc, axis=0, tiled=True)  25.2 us
    all_gather x1, blocking collectives, body(): gathered = lax.all_gather(x, yc, axis=0, tiled=False)  19.7 us
    all_to_all x1, waiting for transfers between devices, body(): pay = lax.all_to_all(pay, 'y', 0, 0)  10 us
    all_to_all x1, starting transfers between devices, body(): got = lax.all_to_all(send, zz, 0, 0)  7.11 us
    all_to_all x1, starting transfers between devices, body(): quad = lax.all_to_all(pieces, 'zq', 0, 0)  6.98 us
    all_to_all x1, starting transfers between devices, body(): pay = lax.all_to_all(pay, 'y', 0, 0)  6.82 us
    unnamed x26, local copies, waits for them, and re-layouts  6.58 us
  transfers between devices with their start and end apart: 7, of which 7 were waited for; matrix products, arithmetic and copies ran while one was open for 5% of the time, Pallas kernels for 12%

profile of v10, /device:TPU:1, one launch (start us, length us, event | category | flops | bytes accessed | tf_op | source)
XLA Modules:
  0.0 164.6 jit_solution(11009498126493399894)
XLA Ops:
  7.2 0.0 copy-start.4
  7.2 0.0 copy-start.11
  7.2 1.7 %shard_map.104 = f32[4,8,1568]{2,1,0:T(8,128)} custom-call(f32[8,480]{1,0:T(8,128)} %inverse_in.1, f32[8,1088]{1,0:T(8,128)} %coupling_in.1), custom_call_target="tpu_custom_call" | custom-call | bytes 300000 | tf_op jit(solution)/shard_map/pallas_call | solution.py:59
  8.9 4.9 %all-to-all-start = ((f32[4,8,1568]{2,1,0:T(8,128)}), f32[4,8,1568]{2,1,0:T(8,128)S(1)}, u32[]{:S(2)}, u32[]{:S(2)}) async-start(f32[4,8,1568]{2,1,0:T(8,128)} %shard_map.104), calls=%async_computation | async-start | bytes 425984 | tf_op jit(solution)/shard_map/all_to_all | solution.py:292
  13.8 0.8 copy.27.blocks
  14.6 0.8 copy.22
  15.4 0.1 pad.2.clone
  15.4 3.6 %all-to-all-done.parts = f32[4,8,1568]{2,1,0:T(8,128)S(1)} async-done(((f32[4,8,1568]{2,1,0:T(8,128)}), f32[4,8,1568]{2,1,0:T(8,128)S(1)}, u32[]{:S(2)}, u32[]{:S(2)}) %all-to-all-start) | async-done | bytes 200736 | tf_op jit(solution)/shard_map/all_to_all | solution.py:292
  19.1 0.9 shard_map.105
  19.9 7.0 %all-to-all-start.1 = ((f32[4,8,3328]{2,1,0:T(8,128)}), f32[4,8,3328]{2,1,0:T(8,128)S(1)}, u32[]{:S(2)}, u32[]{:S(2)}) async-start(f32[4,8,3328]{2,1,0:T(8,128)} %get-tuple-element.24), calls=%async_computation.1 | async-start | bytes 851968 | tf_op jit(solution)/shard_map/all_to_all | solution.py:294
  26.9 0.1 pad_add_fusion.at
  27.0 0.1 maximum_maximum_fusion.sep_noise
  27.1 0.0 copy-done.11
  27.1 7.0 %shard_map.106 = (f32[64,2048]{1,0:T(8,128)S(1)}, f32[64,2048]{1,0:T(8,128)S(1)}) custom-call(s32[16,8]{1,0:T(8,128)S(1)} %copy.27.blocks, s32[4]{0:T(128)S(1)} %pad_add_fusion.at, f32[64,2048]{1,0:T(8,128)S(1)} %copy-done.4, f32[32,64]{1,0:T(8,128)S(1)} %bitcast.17, f32[64,128]{1,0:T(8,128)S(1)} %maximum_maximum_fusion.sep_noise, ...), custom_call_target="tpu_custom_call" | custom-call | flops 50000000 | bytes 3000000 | tf_op jit(solution)/shard_map/pallas_call | solution.py:59
  34.1 0.8 copy-done.10
  34.9 0.1 pad_add_fusion.1.place
  35.0 1.3 all-to-all-done.1.quad
  36.3 1.3 shard_map.107
  37.6 0.0 all-gather.4.cloned.1.call-update
  37.6 2.0 %reshape.13 = f32[8,2,4,2048]{3,2,1,0:T(4,128)} reshape(f32[64,2048]{1,0:T(8,128)} %copy-done.10) | data formatting | bytes 1048576 | tf_op jit(solution)/shard_map/reshape | solution.py:322
  39.6 1.0 dynamic-slice_bitcast_fusion
  40.6 5.9 %collective-permute-start = (f32[8,4,2048]{2,1,0:T(4,128)S(1)}, f32[8,4,2048]{2,1,0:T(4,128)S(1)}, u32[]{:S(2)}, u32[]{:S(2)}) collective-permute-start(f32[8,4,2048]{2,1,0:T(4,128)S(1)} %dynamic-slice_bitcast_fusion), channel_id=1, source_target_pairs={{0,4},{4,0},{1,5},{5,1},{2,6},{6,2},{3,7},{7,3},{8,12},{12,8},{9,1... | collective-permute-start | bytes 786440 | tf_op jit(solution)/shard_map/ppermute | solution.py:325
  46.5 1.1 collective-permute-done
  47.6 1.7 %bitcast_add_fusion = f32[8,4,2048]{2,1,0:T(4,128)} fusion(f32[8,4,2048]{2,1,0:T(4,128)S(1)} %collective-permute-done, f32[8,2,4,2048]{3,2,1,0:T(4,128)} %reshape.13, s32[]{:T(128)S(6)} %select_n.47), kind=kLoop, calls=%fused_computation | loop fusion | flops 65536 | bytes 786436 | tf_op jit(solution)/shard_map/add | solution.py:325
  49.3 6.8 %all-to-all-start.2 = ((f32[8,4,2048]{2,1,0:T(4,128)}), f32[8,4,2048]{2,1,0:T(4,128)S(1)}, u32[]{:S(2)}, u32[]{:S(2)}) async-start(f32[8,4,2048]{2,1,0:T(4,128)} %bitcast_add_fusion), calls=%async_computation.2 | async-start | bytes 524288 | tf_op jit(solution)/shard_map/all_to_all | solution.py:326
  56.2 0.0 copy-done.5
  56.2 3.0 %shard_map.108 = (f32[64,2048]{1,0:T(8,128)S(1)}, f32[16,64,128]{2,1,0:T(8,128)S(1)}) custom-call(f32[64,2048]{1,0:T(8,128)S(1)} %get-tuple-element.29.lf, f32[64,2048]{1,0:T(8,128)S(1)} %copy-done.5, f32[16,128,128]{2,1,0:T(8,128)S(1)} %copy-done, f32[16,64,128]{2,1,0:T(8,128)S(1)} %copy-done.1), custom_call_target="tpu_custom_call" | custom-call | flops 70000000 | bytes 4000000 | tf_op jit(solution)/shard_map/pallas_call | solution.py:59
  59.2 0.8 copy-done.6
  60.0 0.8 copy-done.8
  60.8 10.0 %all-to-all-done.2 = f32[8,4,2048]{2,1,0:T(4,128)S(1)} async-done(((f32[8,4,2048]{2,1,0:T(4,128)}), f32[8,4,2048]{2,1,0:T(4,128)S(1)}, u32[]{:S(2)}, u32[]{:S(2)}) %all-to-all-start.2) | async-done | bytes 262176 | tf_op jit(solution)/shard_map/all_to_all | solution.py:326
  70.8 0.1 reshape.14
  71.0 0.1 copy.26
  71.0 0.2 reshape.15.noise
  71.3 25.2 %all-gather.4.cloned.1.call-done.source = f32[128,12672]{1,0:T(8,128)} async-done(((f32[8,12672]{1,0:T(8,128)}), f32[128,12672]{1,0:T(8,128)}) %all-gather.4.cloned.1.call-update) | async-done | bytes 6488080 | tf_op jit(solution)/shard_map/all_gather | solution.py:319
  96.5 5.8 %shard_map.109 = (f32[8,4,1792]{2,1,0:T(4,128)}, f32[4,128]{1,0:T(4,128)S(1)}) custom-call(s32[2]{0:T(128)S(1)} %pad_add_fusion.1.place, f32[4,1920]{1,0:T(4,128)S(1)} %slice_reduce_fusion.v, f32[4,4,128]{2,1,0:T(4,128)S(1)} %reshape.15.noise, f32[128,12672]{1,0:T(8,128)} %all-gather.4.cloned.1.call-done.source), custom_call_target="tpu_custom_call" | custom-call | flops 12000000 | bytes 6500000 | tf_op jit(solution)/shard_map/pallas_call | solution.py:59
  102.2 7.1 %all-to-all-start.3 = ((f32[8,4,1792]{2,1,0:T(4,128)}), f32[8,4,1792]{2,1,0:T(4,128)S(1)}, u32[]{:S(2)}, u32[]{:S(2)}) async-start(f32[8,4,1792]{2,1,0:T(4,128)} %get-tuple-element.34), calls=%async_computation.3 | async-start | bytes 458752 | tf_op jit(solution)/shard_map/all_to_all | solution.py:351
  109.3 1.1 slice.11.path
  110.4 3.7 %shard_map.110.upper = f32[512,1024]{1,0:T(8,128)S(1)} custom-call(f32[128,12672]{1,0:T(8,128)} %all-gather.4.cloned.1.call-done.source), custom_call_target="tpu_custom_call" | custom-call | flops 1600000000 | bytes 10000000 | tf_op jit(solution)/shard_map/pallas_call | solution.py:59
  114.2 5.7 %all-to-all-done.3.got = f32[8,4,1792]{2,1,0:T(4,128)S(1)} async-done(((f32[8,4,1792]{2,1,0:T(4,128)}), f32[8,4,1792]{2,1,0:T(4,128)S(1)}, u32[]{:S(2)}, u32[]{:S(2)}) %all-to-all-start.3) | async-done | bytes 229408 | tf_op jit(solution)/shard_map/all_to_all | solution.py:351
  119.9 1.2 shard_map.111
  121.1 3.4 %all-to-all-start.4 = ((f32[8,4,1024]{2,1,0:T(4,128)}), f32[8,4,1024]{2,1,0:T(4,128)S(1)}, u32[]{:S(2)}, u32[]{:S(2)}) async-start(f32[8,4,1024]{2,1,0:T(4,128)} %shard_map.111), calls=%async_computation.4 | async-start | bytes 262144 | tf_op jit(solution)/shard_map/all_to_all | solution.py:367
  124.4 6.6 %shard_map.112 = (f32[4,896]{1,0:T(4,128)S(1)}, f32[384,1024]{1,0:T(8,128)S(1)}) custom-call(s32[2]{0:T(128)S(1)} %pad_add_fusion.1.place, f32[8,4,1792]{2,1,0:T(4,128)S(1)} %all-to-all-done.3.got, f32[4,128]{1,0:T(4,128)S(1)} %get-tuple-element.38.g3, f32[512,1024]{1,0:T(8,128)S(1)} %shard_map.110.upper, f32[128,12672]{1,0:T(8,128)} %all-gather.4.cloned.1.call-done.source), custom_call_target="tpu_custom_call" | custom-call | flops 2200000000 | bytes 10000000 | tf_op jit(solution)/shard_map/pallas_call | solution.py:59
  131.0 1.2 copy-done.2
  132.2 0.1 all-to-all-done.4.got0
  132.3 1.4 copy-done.3
  133.7 1.5 shard_map.113
  135.2 19.7 %all-gather.1.x = f32[16,4,1920]{2,1,0:T(4,128)S(1)} all-gather(f32[1,4,1920]{2,1,0:T(4,128)S(1)} %bitcast.16), channel_id=2, replica_groups=mesh['zh'=2,'zq'=4,'y'=8,'core'=2,'rhs'=4] {'y','core'}, dimensions={0}, use_global_device_ids=true | all-gather | bytes 522240 | tf_op jit(solution)/shard_map/all_gather | solution.py:387
  154.9 2.9 %shard_map.114 = (f32[64,2048]{1,0:T(8,128)}, f32[32,64]{1,0:T(8,128)}) custom-call(s32[16,8]{1,0:T(8,128)S(1)} %copy.27.blocks, s32[4]{0:T(128)S(1)} %pad_add_fusion.at, f32[16,4,1920]{2,1,0:T(4,128)S(1)} %all-gather.1.x, f32[64,2048]{1,0:T(8,128)S(1)} %copy-done.7, f32[16,64,128]{2,1,0:T(8,128)S(1)} %copy-done.9), custom_call_target="tpu_custom_call" | custom-call | flops 20000000 | bytes 2000000 | tf_op jit(solution)/shard_map/pallas_call | solution.py:59
  (21 shorter events, 0.1 us)
Async XLA Ops:
  7.2 19.9 %copy-start.4 = (f32[64,2048]{1,0:T(8,128)S(1)}, f32[64,2048]{1,0:T(8,128)}, u32[]{:S(2)}) copy-start(f32[64,2048]{1,0:T(8,128)} %shift.1) | copy-start | bytes 1572868
  7.2 19.9 %copy-start.11 = (f32[64,32]{0,1:T(8,128)S(1)}, f32[64,32]{0,1:T(8,128)}, u32[]{:S(2)}) copy-start(f32[64,32]{0,1:T(8,128)} %param.10) | copy-start | bytes 24580
  7.2 19.9 %copy-start = (f32[16,128,128]{2,1,0:T(8,128)S(1)}, f32[16,128,128]{2,1,0:T(8,128)}, u32[]{:S(2)}) copy-start(f32[16,128,128]{2,1,0:T(8,128)} %inverse.3) | copy-start | bytes 3145732
  7.2 19.9 %copy-start.1 = (f32[16,64,128]{2,1,0:T(8,128)S(1)}, f32[16,64,128]{2,1,0:T(8,128)}, u32[]{:S(2)}) copy-start(f32[16,64,128]{2,1,0:T(8,128)} %panel.3) | copy-start | bytes 1572868
  8.9 10.1 %all-to-all-start = ((f32[4,8,1568]{2,1,0:T(8,128)}), f32[4,8,1568]{2,1,0:T(8,128)S(1)}, u32[]{:S(2)}, u32[]{:S(2)}) async-start(f32[4,8,1568]{2,1,0:T(8,128)} %shard_map.104), calls=%async_computation | async-start | bytes 425984 | tf_op jit(solution)/shard_map/all_to_all | solution.py:292
  19.9 16.3 %all-to-all-start.1 = ((f32[4,8,3328]{2,1,0:T(8,128)}), f32[4,8,3328]{2,1,0:T(8,128)S(1)}, u32[]{:S(2)}, u32[]{:S(2)}) async-start(f32[4,8,3328]{2,1,0:T(8,128)} %get-tuple-element.24), calls=%async_computation.1 | async-start | bytes 851968 | tf_op jit(solution)/shard_map/all_to_all | solution.py:294
  26.9 69.5 %all-gather.4.cloned.1.call-start = ((), (), s32[]{:S(2)}) async-start(), calls=%async_computation.5 | async-start | bytes 6893568 | tf_op jit(solution)/shard_map/all_gather | solution.py:319
  34.1 0.8 copy-start.10
  36.3 19.9 %copy-start.5 = (f32[64,2048]{1,0:T(8,128)S(1)}, f32[64,2048]{1,0:T(8,128)}, u32[]{:S(2)}) copy-start(f32[64,2048]{1,0:T(8,128)} %noise.1) | copy-start | bytes 1572868
  40.6 7.0 %collective-permute-start = (f32[8,4,2048]{2,1,0:T(4,128)S(1)}, f32[8,4,2048]{2,1,0:T(4,128)S(1)}, u32[]{:S(2)}, u32[]{:S(2)}) collective-permute-start(f32[8,4,2048]{2,1,0:T(4,128)S(1)} %dynamic-slice_bitcast_fusion), channel_id=1, source_target_pairs={{0,4},{4,0},{1,5},{5,1},{2,6},{6,2},{3,7},{7,3},{8,12},{12,8},{9,1... | collective-permute-start | bytes 786440 | tf_op jit(solution)/shard_map/ppermute | solution.py:325
  49.3 21.4 %all-to-all-start.2 = ((f32[8,4,2048]{2,1,0:T(4,128)}), f32[8,4,2048]{2,1,0:T(4,128)S(1)}, u32[]{:S(2)}, u32[]{:S(2)}) async-start(f32[8,4,2048]{2,1,0:T(4,128)} %bitcast_add_fusion), calls=%async_computation.2 | async-start | bytes 524288 | tf_op jit(solution)/shard_map/all_to_all | solution.py:326
  59.2 0.8 copy-start.6
  60.0 0.8 copy-start.8
  102.2 17.6 %all-to-all-start.3 = ((f32[8,4,1792]{2,1,0:T(4,128)}), f32[8,4,1792]{2,1,0:T(4,128)S(1)}, u32[]{:S(2)}, u32[]{:S(2)}) async-start(f32[8,4,1792]{2,1,0:T(4,128)} %get-tuple-element.34), calls=%async_computation.3 | async-start | bytes 458752 | tf_op jit(solution)/shard_map/all_to_all | solution.py:351
  121.1 11.2 %all-to-all-start.4 = ((f32[8,4,1024]{2,1,0:T(4,128)}), f32[8,4,1024]{2,1,0:T(4,128)S(1)}, u32[]{:S(2)}, u32[]{:S(2)}) async-start(f32[8,4,1024]{2,1,0:T(4,128)} %shard_map.111), calls=%async_computation.4 | async-start | bytes 262144 | tf_op jit(solution)/shard_map/all_to_all | solution.py:367
  131.0 1.2 copy-start.2
  132.3 1.4 copy-start.3
  133.7 21.2 %copy-start.7 = (f32[64,2048]{1,0:T(8,128)S(1)}, f32[64,2048]{1,0:T(8,128)}, u32[]{:S(2)}) copy-start(f32[64,2048]{1,0:T(8,128)} %copy-done.6) | copy-start | bytes 1572868
  133.7 21.2 %copy-start.9 = (f32[16,64,128]{2,1,0:T(8,128)S(1)}, f32[16,64,128]{2,1,0:T(8,128)}, u32[]{:S(2)}) copy-start(f32[16,64,128]{2,1,0:T(8,128)} %copy-done.8) | copy-start | bytes 1572868
Sparse Core Ops, SparseCore 0:
  37.7 58.6 all-gather.3
